TPU v7x, 512 devices: a whole 4x4x16 slice. The times are simulated.
512 devices in a mesh: row: 8 (over x, z_hi), col: 8 (over y, core), depth: 8 (over z_lo).
Axes of the slice: x: 4, y: 4, z: 16 (z_hi: 2, z_lo: 8; z = z_hi * 8 + z_lo), core: 2. Of those that a mesh axis runs over, the one named last changes fastest.
Arguments:
- inputs: bfloat16 [4096, 3072], P(('depth', 'row'), 'col'), may hold values from -6 to 6
- up_weight: bfloat16 [3072, 12288], P('col', 'row'), may hold values from -0.109375 to 0.109375
- down_weight: bfloat16 [12288, 3072], P('row', 'col'), may hold values from -0.0546875 to 0.0546875
- out_grad: bfloat16 [4096, 3072], P(('depth', 'row'), 'col'), may hold values from -6 to 6
Outputs:
- outputs: bfloat16 [4096, 3072], P(('depth', 'row'), 'col')
- in_grad: bfloat16 [4096, 3072], P(('depth', 'row'), 'col')
- up_grad: bfloat16 [3072, 12288], P('col', 'row')
- down_grad: bfloat16 [12288, 3072], P('row', 'col')
All inputs are finite; a program needn't handle non-finite values.
Results may differ from a plain program's by a relative error of at most 0.028.
Values may be sent and summed in bfloat16 or wider, within the bound.
No kernel may reach another device: no remote copies, remote signals or barrier semaphores. Data moves between devices by JAX's collectives and lax.ppermute only.
A program may use at most 64 MiB of HBM per device.

v0:
```python
import jax
import jax.numpy as jnp
from jax import lax
from jax.sharding import PartitionSpec as P


def gelu_value(preact):
    wide = preact.astype(jnp.float32)
    return 0.5 * wide * (1.0 + jax.scipy.special.erf(wide * 0.7071067811865476))


def gelu_slope(preact):
    wide = preact.astype(jnp.float32)
    return (
        0.5 * (1.0 + jax.scipy.special.erf(wide * 0.7071067811865476))
        + wide * jnp.exp(-0.5 * wide * wide) * 0.3989422804014327
    )


def product(left, right, flipped):
    if flipped:
        return lax.dot_general(
            left, right, (((1,), (1,)), ((), ())), preferred_element_type=jnp.float32
        )
    return jnp.dot(left, right, preferred_element_type=jnp.float32)


def over_tokens(left, right):
    return lax.dot_general(
        left, right, (((0,), (0,)), ((), ())), preferred_element_type=jnp.float32
    )


def column_sums(left, right, flipped):
    return lax.psum_scatter(
        product(left, right, flipped).astype(jnp.bfloat16), "col", scatter_dimension=0, tiled=True
    ).astype(jnp.float32)


def row_sums(left, right, flipped):
    return lax.psum_scatter(
        product(left, right, flipped).astype(jnp.bfloat16), "row", scatter_dimension=0, tiled=True
    ).astype(jnp.float32)


def gather_columns(values):
    return lax.all_gather(values, "col", axis=0, tiled=True)


def on_device(inputs, up_weight, down_weight, out_grad):
    every_input, every_grad = (
        lax.all_gather(inputs, "row", axis=0, tiled=True),
        lax.all_gather(out_grad, "row", axis=0, tiled=True),
    )
    loss_scale = float(every_grad.shape[0] * lax.axis_size("depth")) ** (-0.5)
    preact = column_sums(every_input, up_weight, False).astype(jnp.bfloat16)
    every_act = gather_columns(gelu_value(preact).astype(jnp.bfloat16))
    outputs = row_sums(every_act, down_weight, False).astype(jnp.bfloat16)
    down_term = loss_scale * over_tokens(every_act, every_grad)
    act_grad = column_sums(every_grad, down_weight, True)
    hidden_grad = (act_grad * gelu_slope(preact)).astype(jnp.bfloat16)
    every_hidden = gather_columns(hidden_grad)
    in_grad = row_sums(every_hidden, up_weight, True).astype(jnp.bfloat16)
    up_term = loss_scale * over_tokens(every_input, every_hidden)
    up_total, down_total = (
        lax.psum(up_term.astype(jnp.bfloat16), "depth").astype(jnp.float32),
        lax.psum(down_term.astype(jnp.bfloat16), "depth").astype(jnp.float32),
    )
    up_grad = up_total.astype(jnp.bfloat16)
    down_grad = down_total.astype(jnp.bfloat16)
    return (outputs, in_grad, up_grad, down_grad)


def solution(mesh):
    in_specs = (
        P(("depth", "row"), "col"),
        P("col", "row"),
        P("row", "col"),
        P(("depth", "row"), "col"),
    )
    out_specs = (
        P(("depth", "row"), "col"),
        P(("depth", "row"), "col"),
        P("col", "row"),
        P("row", "col"),
    )
    return jax.shard_map(
        on_device, mesh=mesh, in_specs=in_specs, out_specs=out_specs, check_vma=False
    )
```

profile of v0, /device:TPU:6, one launch (start us, length us, event | category | flops | bytes accessed | tf_op | source)
XLA Modules:
  0.0 658.7 jit_solution(8589776357170328186)
XLA Ops:
  7.2 0.0 copy-start
  7.2 0.0 reduce-scatter.5.cloned.1.call-start
  7.2 78.0 %all_gather.12 = bf16[512,384]{1,0:T(8,128)(2,1)S(1)} all-gather(bf16[64,384]{1,0:T(8,128)(2,1)} %param.4), channel_id=1, replica_groups=mesh['row'=8,'col'=8,'depth'=8] {'row'}, dimensions={0}, use_global_device_ids=true | all-gather | bytes 442368 | tf_op jit(solution)/shard_map/all_gather | solution.py:52
  85.2 3.4 convolution_convert_fusion.1
  88.6 0.0 copy-start.3
  88.6 0.0 reduce-scatter.5.cloned.1.call-update
  88.6 0.0 reduce-scatter.9.cloned.1.call-start
  88.7 0.7 copy-done.3
  89.4 77.8 %all_gather.14 = bf16[512,384]{1,0:T(8,128)(2,1)S(1)} all-gather(bf16[64,384]{1,0:T(8,128)(2,1)S(1)} %copy-done.3), channel_id=1, replica_groups=mesh['row'=8,'col'=8,'depth'=8] {'row'}, dimensions={0}, use_global_device_ids=true | all-gather | bytes 442368 | tf_op jit(solution)/shard_map/all_gather | solution.py:53
  167.3 0.0 copy-done
  167.3 2.2 convolution_convert_fusion
  169.4 0.0 reduce-scatter.9.cloned.1.call-update
  169.4 0.0 all-gather.5.cloned.1.call-start
  169.5 0.0 reduce-scatter.5.cloned.1.call-done
  169.5 46.4 %reduce-scatter.9.cloned.1.call-done = bf16[64,1536]{1,0:T(8,128)(2,1)} async-done(((bf16[512,1536]{1,0:T(8,128)(2,1)}), bf16[64,1536]{1,0:T(8,128)(2,1)}) %reduce-scatter.9.cloned.1.call-update) | async-done | bytes 196624 | tf_op jit(solution)/shard_map/reduce_scatter | solution.py:35
  215.9 2.0 fusion.11
  217.9 0.0 all-gather.5.cloned.1.call-update
  217.9 0.0 all-gather.3.cloned.1.call-start
  218.0 0.5 all-gather.3.cloned.1.call-update
  218.5 0.0 all-reduce.3.cloned.1.call-start
  218.6 31.0 %all-gather.5.cloned.1.call-done = bf16[512,1536]{1,0:T(8,128)(2,1)} async-done(((bf16[64,1536]{1,0:T(8,128)(2,1)}), bf16[512,1536]{1,0:T(8,128)(2,1)}) %all-gather.5.cloned.1.call-update) | async-done | bytes 1572880 | tf_op jit(solution)/shard_map/all_gather | solution.py:47
  249.6 3.4 fusion.2
  253.0 31.4 %all-gather.3.cloned.1.call-done = bf16[512,1536]{1,0:T(8,128)(2,1)} async-done(((bf16[64,1536]{1,0:T(8,128)(2,1)}), bf16[512,1536]{1,0:T(8,128)(2,1)}) %all-gather.3.cloned.1.call-update) | async-done | bytes 1572880 | tf_op jit(solution)/shard_map/all_gather | solution.py:47
  284.5 3.4 fusion.1
  287.9 0.0 all-reduce.3.cloned.1.call-update
  287.9 0.0 copy-start.1
  287.9 0.0 reduce-scatter.7.cloned.1.call-start
  288.0 3.2 convolution_convert_fusion.3
  291.2 0.0 reduce-scatter.7.cloned.1.call-update
  291.2 0.0 reduce-scatter.11.cloned.1.call-start
  291.3 0.0 copy-done.1
  291.3 3.1 convolution_convert_fusion.2
  294.4 0.0 reduce-scatter.11.cloned.1.call-update
  294.4 137.2 %all-reduce.3.cloned.1.call-done = (bf16[384,1536]{0,1:T(8,128)(2,1)}, bf16[1536,384]{1,0:T(8,128)(2,1)}) async-done(((bf16[384,1536]{0,1:T(8,128)(2,1)}, bf16[1536,384]{1,0:T(8,128)(2,1)}), (bf16[384,1536]{0,1:T(8,128)(2,1)}, bf16[1536,384]{1,0:T(8,128)(2,1)})) %all-reduce.3.cloned.1.call-update) | async-done | bytes 2359312 | tf_op jit(solution)/shard_map/psum | solution.py:66
  431.6 0.0 copy-start.2
  431.6 2.5 copy.8
  434.1 110.0 %reduce-scatter.7.cloned.1.call-done = bf16[64,384]{1,0:T(8,128)(2,1)} async-done(((bf16[512,384]{1,0:T(8,128)(2,1)}), bf16[64,384]{1,0:T(8,128)(2,1)}) %reduce-scatter.7.cloned.1.call-update) | async-done | bytes 49168 | tf_op jit(solution)/shard_map/reduce_scatter | solution.py:41
  544.1 106.7 %reduce-scatter.11.cloned.1.call-done = bf16[64,384]{1,0:T(8,128)(2,1)} async-done(((bf16[512,384]{1,0:T(8,128)(2,1)}), bf16[64,384]{1,0:T(8,128)(2,1)}) %reduce-scatter.11.cloned.1.call-update) | async-done | bytes 49168 | tf_op jit(solution)/shard_map/reduce_scatter | solution.py:41
  650.8 0.0 copy-done.2
  650.8 1.0 copy.11
Async XLA Ops:
  7.2 160.1 %copy-start = (bf16[1536,384]{1,0:T(8,128)(2,1)S(1)}, bf16[1536,384]{1,0:T(8,128)(2,1)}, u32[]{:S(2)}) copy-start(bf16[1536,384]{1,0:T(8,128)(2,1)} %param.6) | copy-start | bytes 3538948
  7.2 162.3 %reduce-scatter.5.cloned.1.call-start = ((), (), s32[]{:S(2)}) async-start(), calls=%async_computation.4 | async-start | bytes 1769472 | tf_op jit(solution)/shard_map/reduce_scatter | solution.py:35
  88.6 0.8 copy-start.3
  88.6 127.3 %reduce-scatter.9.cloned.1.call-start = ((), (), s32[]{:S(2)}) async-start(), calls=%async_computation.7 | async-start | bytes 1769472 | tf_op jit(solution)/shard_map/reduce_scatter | solution.py:35
  169.4 80.1 %all-gather.5.cloned.1.call-start = ((), (), s32[]{:S(2)}) async-start(), calls=%async_computation.8 | async-start | bytes 1769472 | tf_op jit(solution)/shard_map/all_gather | solution.py:47
  217.9 66.5 %all-gather.3.cloned.1.call-start = ((), (), s32[]{:S(2)}) async-start(), calls=%async_computation.5 | async-start | bytes 1769472 | tf_op jit(solution)/shard_map/all_gather | solution.py:47
  218.5 213.1 %all-reduce.3.cloned.1.call-start = ((), (), s32[]{:S(2)}) async-start(), calls=%async_computation.10 | async-start | bytes 4718592 | tf_op jit(solution)/shard_map/psum | solution.py:66
  287.9 3.4 copy-start.1
  287.9 256.2 %reduce-scatter.7.cloned.1.call-start = ((), (), s32[]{:S(2)}) async-start(), calls=%async_computation.6 | async-start | bytes 442368 | tf_op jit(solution)/shard_map/reduce_scatter | solution.py:41
  291.2 359.6 %reduce-scatter.11.cloned.1.call-start = ((), (), s32[]{:S(2)}) async-start(), calls=%async_computation.9 | async-start | bytes 442368 | tf_op jit(solution)/shard_map/reduce_scatter | solution.py:41
  431.6 219.2 %copy-start.2 = (bf16[1536,384]{1,0:T(8,128)(2,1)S(1)}, bf16[1536,384]{1,0:T(8,128)(2,1)}, u32[]{:S(2)}) copy-start(bf16[1536,384]{1,0:T(8,128)(2,1)} %get-tuple-element.15) | copy-start | bytes 3538948
Sparse Core Ops, SparseCore 0:
  88.8 47.5 reduce-scatter.4
  169.6 46.3 reduce-scatter.8
  218.6 30.9 all-gather.4
  252.1 32.2 all-gather.2
  288.0 143.5 all-reduce.2
  436.5 107.5 reduce-scatter.6
  549.1 101.6 reduce-scatter.10
where the time goes:
time: 659 us
  waiting for transfers between devices  463 us (70%)
  blocking collectives  156 us (24%)
  matrix products  18.8 us (3%)
  between operations  14.2 us (2%)
    reduce_scatter x2, waiting for transfers between devices, row_sums(): lax.psum_scatter(product(left, right, flipped).astype(jnp.bfloat16), 'row...  217 us
    psum x1, waiting for transfers between devices, on_device(): lax.psum(up_term.astype(jnp.bfloat16), 'depth').astype(jnp.float32)  137 us
    all_gather x1, blocking collectives, on_device(): lax.all_gather(inputs, 'row', axis=0, tiled=True)  78 us
    all_gather x1, blocking collectives, on_device(): lax.all_gather(out_grad, 'row', axis=0, tiled=True)  77.8 us
    all_gather x2, waiting for transfers between devices, gather_columns(): return lax.all_gather(values, 'col', axis=0, tiled=True)  62.5 us
    reduce_scatter x2, waiting for transfers between devices, column_sums(): lax.psum_scatter(product(left, right, flipped).astype(jnp.bfloat16), 'col...  46.4 us
  transfers between devices with their start and end apart: 7, of which 6 were waited for; matrix products, arithmetic and copies ran while one was open for 2% of the time, Pallas kernels for 0%

commit v1 on v0

v1 whole, which is shorter than its diff:
```python
import jax
import jax.numpy as jnp
from jax import lax
from jax.sharding import Mesh
from jax.sharding import PartitionSpec as P

F32 = jnp.float32
BF16 = jnp.bfloat16


def gelu_value(wide):
    return 0.5 * wide * (1.0 + jax.scipy.special.erf(wide * 0.7071067811865476))


def gelu_slope(wide):
    return (
        0.5 * (1.0 + jax.scipy.special.erf(wide * 0.7071067811865476))
        + wide * jnp.exp(-0.5 * wide * wide) * 0.3989422804014327
    )


def contract(left, right, dims):
    return lax.dot_general(left, right, (dims, ((), ())), preferred_element_type=F32)


def scatter_sum(values, axis):
    count = lax.axis_size(axis)
    parts = lax.all_to_all(values, axis, 0, 0, tiled=True)
    parts = parts.reshape((count, parts.shape[0] // count) + parts.shape[1:])
    return jnp.sum(parts.astype(F32), axis=0)


def spread(values, axis):
    count = lax.axis_size(axis)
    copies = jnp.broadcast_to(values[None], (count,) + values.shape)
    return lax.all_to_all(copies.reshape((-1,) + values.shape[1:]), axis, 0, 0, tiled=True)


def other_half(values):
    depth = lax.axis_size("d")
    pairs = [
        (h * depth + d, (1 - h) * depth + (d + depth // 2) % depth)
        for h in range(2)
        for d in range(depth)
    ]
    return lax.ppermute(values, ("h", "d"), pairs)


def on_device(inputs, up_weight, down_weight, out_grad):
    hidden = up_weight.shape[1]
    features = inputs.shape[1]
    own = inputs.shape[0]
    tokens = own * 64
    loss_scale = float(tokens) ** (-0.5)

    rows = jnp.concatenate([inputs, out_grad], axis=1)
    rows = jnp.concatenate([rows, other_half(rows)], axis=0)
    rows = lax.all_gather(rows, "x", axis=0, tiled=True)
    every_input, every_grad = rows[:, :features], rows[:, features:]

    partial = jnp.concatenate(
        [
            contract(every_input, up_weight, ((1,), (0,))).astype(BF16),
            contract(every_grad, down_weight, ((1,), (1,))).astype(BF16),
        ],
        axis=1,
    )
    partial = scatter_sum(partial, "k").astype(BF16)
    sums = scatter_sum(partial, "y")
    preact = sums[:, :hidden].astype(BF16).astype(F32)
    act = gelu_value(preact).astype(BF16)
    hidden_grad = (sums[:, hidden:] * gelu_slope(preact)).astype(BF16)
    both = jnp.concatenate([act, hidden_grad], axis=1)
    both = spread(spread(both, "y"), "k")
    every_act, every_hidden = both[:, :hidden], both[:, hidden:]

    down_term = (loss_scale * contract(every_act, every_grad, ((0,), (0,)))).astype(BF16)
    up_term = (loss_scale * contract(every_input, every_hidden, ((0,), (0,)))).astype(BF16)
    up_grad, down_grad = lax.psum((up_term, down_term), "d")

    features_part = jnp.concatenate(
        [
            contract(every_act, down_weight, ((1,), (0,))).astype(BF16),
            contract(every_hidden, up_weight, ((1,), (1,))).astype(BF16),
        ],
        axis=1,
    )
    mine = scatter_sum(features_part, "x")
    total = mine[:own] + other_half(mine[own:].astype(BF16)).astype(F32)
    total = total.astype(BF16)
    return total[:, :features], total[:, features:], up_grad, down_grad


def solution(mesh):
    split = Mesh(mesh.devices.reshape(4, 2, 4, 2, 8), ("x", "h", "y", "k", "d"))
    rows = P(("d", "x", "h"), ("y", "k"))
    up = P(("y", "k"), ("x", "h"))
    down = P(("x", "h"), ("y", "k"))
    return jax.shard_map(
        on_device,
        mesh=split,
        in_specs=(rows, up, down, rows),
        out_specs=(rows, rows, up, down),
        check_vma=False,
    )
```

time: 659 us -> 279 us (0.42)
  waiting for transfers between devices: 463 us -> 132 us
  blocking collectives: 156 us -> 90.1 us
  starting transfers between devices: 0.28 us -> 21.2 us
  matrix products: 18.8 us -> 9.04 us
    reduce_scatter x4 -> x0, waiting for transfers between devices: 263 us -> none  [the longest x2 217 us: row_sums(): lax.psum_scatter(product(left, right, flipped).astype(jnp.bfloat16), 'row...]
    all_gather x2 -> x1, blocking collectives: 156 us -> 14.2 us  [on_device(): rows = lax.all_gather(rows, 'x', axis=0, tiled=True)]
    all_to_all x0 -> x5, blocking collectives: none -> 75.9 us  [the longest x3 47.3 us: scatter_sum(): parts = lax.all_to_all(values, axis, 0, 0, tiled=True)]
    all_gather x2 -> x0, waiting for transfers between devices: 62.5 us -> none  [gather_columns(): return lax.all_gather(values, 'col', axis=0, tiled=True)]
    psum x1, waiting for transfers between devices: 137 us -> 111 us  [on_device(): up_grad, down_grad = lax.psum((up_term, down_term), 'd')]
    ppermute x0 -> x2, waiting for transfers between devices: none -> 21.5 us  [other_half(): return lax.ppermute(values, ('h', 'd'), pairs)]
    ppermute x0 -> x2, starting transfers between devices: none -> 21.1 us  [other_half(): return lax.ppermute(values, ('h', 'd'), pairs)]
    dot_general x6, matrix products: 18.8 us -> 9.04 us  [contract(): lax.dot_general(left, right, (dims, ((), ())), preferred_element_type=F32)]
  transfers between devices with their start and end apart: 7 -> 3, of which waited for: 6 -> 3; matrix products, arithmetic and copies ran while one was open for 2% -> 2% of each run, Pallas kernels for 0% -> 0%
where the time goes in v1:
time: 279 us
  waiting for transfers between devices  132 us (47%)
  blocking collectives  90.1 us (32%)
  starting transfers between devices  21.2 us (8%)
  between operations  14.2 us (5%)
  matrix products  9.04 us (3%)
  local copies, waits for them, and re-layouts  7.67 us (3%)
  other arithmetic  3.91 us (1%)
    psum x1, waiting for transfers between devices, on_device(): up_grad, down_grad = lax.psum((up_term, down_term), 'd')  111 us
    all_to_all x3, blocking collectives, scatter_sum(): parts = lax.all_to_all(values, axis, 0, 0, tiled=True)  47.3 us
    all_to_all x2, blocking collectives, spread(): lax.all_to_all(copies.reshape((-1,) + values.shape[1:]), axis, 0, 0, tile...  28.6 us
    ppermute x2, waiting for transfers between devices, other_half(): return lax.ppermute(values, ('h', 'd'), pairs)  21.5 us
    ppermute x2, starting transfers between devices, other_half(): return lax.ppermute(values, ('h', 'd'), pairs)  21.1 us
    all_gather x1, blocking collectives, on_device(): rows = lax.all_gather(rows, 'x', axis=0, tiled=True)  14.2 us
    dot_general x6, matrix products, contract(): lax.dot_general(left, right, (dims, ((), ())), preferred_element_type=F32)  9.04 us
    unnamed x17, local copies, waits for them, and re-layouts  6.17 us
  transfers between devices with their start and end apart: 3, of which 3 were waited for; matrix products, arithmetic and copies ran while one was open for 2% of the time, Pallas kernels for 0%

profile of v1, /device:TPU:6, one launch (start us, length us, event | category | flops | bytes accessed | tf_op | source)
XLA Modules:
  0.0 278.6 jit_solution(11034269952820863080)
XLA Ops:
  7.2 0.0 copy-start
  7.2 0.0 copy-start.3
  7.2 0.0 all-reduce.3.cloned.1.call-start
  7.2 1.0 constant_dynamic-update-slice_fusion.1
  8.2 0.8 constant_dynamic-update-slice_fusion
  9.0 12.7 %collective-permute-start = (bf16[64,768]{1,0:T(8,128)(2,1)S(1)}, bf16[64,768]{1,0:T(8,128)(2,1)S(1)}, u32[]{:S(2)}, u32[]{:S(2)}) collective-permute-start(bf16[64,768]{1,0:T(8,128)(2,1)S(1)} %constant_dynamic-update-slice_fusion), channel_id=1, source_target_pairs={{0,68},{1,69},{2,70},{3,71},{4,64},{5,65},{6,66},{7,67},{64,4},{65... | collective-permute-start | bytes 294920 | tf_op jit(solution)/shard_map/ppermute | solution.py:46
  21.7 8.4 %collective-permute-done = bf16[64,768]{1,0:T(8,128)(2,1)S(1)} collective-permute-done((bf16[64,768]{1,0:T(8,128)(2,1)S(1)}, bf16[64,768]{1,0:T(8,128)(2,1)S(1)}, u32[]{:S(2)}, u32[]{:S(2)}) %collective-permute-start) | collective-permute-done | bytes 98336 | tf_op jit(solution)/shard_map/ppermute | solution.py:46
  30.1 14.2 %all_gather.3 = bf16[512,768]{1,0:T(8,128)(2,1)S(1)} all-gather(bf16[128,768]{1,0:T(8,128)(2,1)S(1)} %pad_maximum_fusion.2), channel_id=1, replica_groups=mesh['x'=4,'h'=2,'y'=4,'k'=2,'d'=8] {'x'}, dimensions={0}, use_global_device_ids=true | all-gather | bytes 983040 | tf_op jit(solution)/shard_map/all_gather | solution.py:58
  44.4 0.0 copy-done.3
  44.4 1.0 convolution_convert_fusion
  45.4 0.0 copy-done
  45.4 1.0 convolution_convert_fusion.1
  46.4 0.4 pad_maximum_fusion
  46.8 7.2 %all_to_all.42 = bf16[2,256,3072]{2,1,0:T(8,128)(2,1)} all-to-all(bf16[2,256,3072]{2,1,0:T(8,128)(2,1)S(1)} %bitcast.13), channel_id=1, replica_groups=mesh['x'=4,'h'=2,'y'=4,'k'=2,'d'=8] {'k'}, dimensions={0} | all-to-all | bytes 6291456 | tf_op jit(solution)/shard_map/all_to_all | solution.py:28
  54.1 2.7 reduce_sum.30
  56.7 25.3 %all_to_all.43 = bf16[4,64,3072]{2,1,0:T(8,128)(2,1)S(1)} all-to-all(bf16[4,64,3072]{2,1,0:T(8,128)(2,1)S(1)} %bitcast.14), channel_id=1, replica_groups=mesh['x'=4,'h'=2,'y'=4,'k'=2,'d'=8] {'y'}, dimensions={0} | all-to-all | bytes 3145728 | tf_op jit(solution)/shard_map/all_to_all | solution.py:28
  82.0 0.3 convert_reduce_fusion
  82.3 0.2 fusion.15
  82.5 0.2 broadcast_in_dim.6
  82.7 22.3 %all_to_all.44 = bf16[4,64,3072]{2,1,0:T(8,128)(2,1)S(1)} all-to-all(bf16[4,64,3072]{2,1,0:T(8,128)(2,1)S(1)} %broadcast_in_dim.6), channel_id=1, replica_groups=mesh['x'=4,'h'=2,'y'=4,'k'=2,'d'=8] {'y'}, dimensions={0} | all-to-all | bytes 3145728 | tf_op jit(solution)/shard_map/all_to_all | solution.py:36
  105.0 0.4 broadcast_in_dim.16
  105.4 6.3 %all_to_all.45 = bf16[2,256,3072]{2,1,0:T(8,128)(2,1)S(1)} all-to-all(bf16[2,256,3072]{2,1,0:T(8,128)(2,1)S(1)} %broadcast_in_dim.16), channel_id=1, replica_groups=mesh['x'=4,'h'=2,'y'=4,'k'=2,'d'=8] {'k'}, dimensions={0} | all-to-all | bytes 6291456 | tf_op jit(solution)/shard_map/all_to_all | solution.py:36
  111.6 0.0 copy-start.1
  111.6 2.0 fusion.1
  113.7 0.0 copy-done.1
  113.7 1.8 fusion
  115.5 0.0 all-reduce.3.cloned.1.call-update
  115.5 0.0 copy-start.2
  115.5 0.0 copy-start.4
  115.6 2.4 fusion.11
  117.9 0.0 copy-done.2
  117.9 0.3 copy-done.4
  118.2 0.8 fusion.8
  119.1 0.1 copy_bitcast_fusion
  119.2 14.8 %all_to_all.46 = bf16[4,128,768]{1,2,0:T(8,128)(2,1)S(1)} all-to-all(bf16[4,128,768]{1,2,0:T(8,128)(2,1)S(1)} %copy_bitcast_fusion), channel_id=1, replica_groups=mesh['x'=4,'h'=2,'y'=4,'k'=2,'d'=8] {'x'}, dimensions={0} | all-to-all | bytes 1572864 | tf_op jit(solution)/shard_map/all_to_all | solution.py:28
  134.0 0.1 convert_reduce_fusion.1
  134.1 0.1 slice.88
  134.3 8.4 %collective-permute-start.1 = (bf16[64,768]{0,1:T(8,128)(2,1)S(1)}, bf16[64,768]{0,1:T(8,128)(2,1)S(1)}, u32[]{:S(2)}, u32[]{:S(2)}) collective-permute-start(bf16[64,768]{0,1:T(8,128)(2,1)S(1)} %slice.88), channel_id=1, source_target_pairs={{0,68},{1,69},{2,70},{3,71},{4,64},{5,65},{6,66},{7,67},{64,4},{65... | collective-permute-start | bytes 294920 | tf_op jit(solution)/shard_map/ppermute | solution.py:46
  142.7 13.1 %collective-permute-done.1 = bf16[64,768]{0,1:T(8,128)(2,1)S(1)} collective-permute-done((bf16[64,768]{0,1:T(8,128)(2,1)S(1)}, bf16[64,768]{0,1:T(8,128)(2,1)S(1)}, u32[]{:S(2)}, u32[]{:S(2)}) %collective-permute-start.1) | collective-permute-done | bytes 98336 | tf_op jit(solution)/shard_map/ppermute | solution.py:46
  155.9 0.7 copy.15
  156.6 0.7 copy.14
  157.3 111.0 %all-reduce.3.cloned.1.call-done = (bf16[384,1536]{1,0:T(8,128)(2,1)}, bf16[1536,384]{1,0:T(8,128)(2,1)}) async-done(((bf16[384,1536]{1,0:T(8,128)(2,1)}, bf16[1536,384]{1,0:T(8,128)(2,1)}), (bf16[384,1536]{1,0:T(8,128)(2,1)}, bf16[1536,384]{1,0:T(8,128)(2,1)})) %all-reduce.3.cloned.1.call-update) | async-done | bytes 2359312 | tf_op jit(solution)/shard_map/psum | solution.py:79
  268.3 0.0 copy-start.5
  268.3 2.5 copy.22
  270.8 0.0 copy-done.5
  270.8 1.0 copy.23
  (4 shorter events, 0.1 us)
Async XLA Ops:
  7.2 38.2 %copy-start = (bf16[384,1536]{1,0:T(8,128)(2,1)S(1)}, bf16[384,1536]{1,0:T(8,128)(2,1)}, u32[]{:S(2)}) copy-start(bf16[384,1536]{1,0:T(8,128)(2,1)} %param.5) | copy-start | bytes 3538948
  7.2 37.2 %copy-start.3 = (bf16[1536,384]{1,0:T(8,128)(2,1)S(1)}, bf16[1536,384]{1,0:T(8,128)(2,1)}, u32[]{:S(2)}) copy-start(bf16[1536,384]{1,0:T(8,128)(2,1)} %param.6) | copy-start | bytes 3538948
  7.2 261.1 %all-reduce.3.cloned.1.call-start = ((), (), s32[]{:S(2)}) async-start(), calls=%async_computation.5 | async-start | bytes 4718592 | tf_op jit(solution)/shard_map/psum | solution.py:79
  9.0 21.1 %collective-permute-start = (bf16[64,768]{1,0:T(8,128)(2,1)S(1)}, bf16[64,768]{1,0:T(8,128)(2,1)S(1)}, u32[]{:S(2)}, u32[]{:S(2)}) collective-permute-start(bf16[64,768]{1,0:T(8,128)(2,1)S(1)} %constant_dynamic-update-slice_fusion), channel_id=1, source_target_pairs={{0,68},{1,69},{2,70},{3,71},{4,64},{5,65},{6,66},{7,67},{64,4},{65... | collective-permute-start | bytes 294920 | tf_op jit(solution)/shard_map/ppermute | solution.py:46
  111.6 2.1 copy-start.1
  115.5 2.4 copy-start.2
  115.5 2.7 copy-start.4
  134.3 21.5 %collective-permute-start.1 = (bf16[64,768]{0,1:T(8,128)(2,1)S(1)}, bf16[64,768]{0,1:T(8,128)(2,1)S(1)}, u32[]{:S(2)}, u32[]{:S(2)}) collective-permute-start(bf16[64,768]{0,1:T(8,128)(2,1)S(1)} %slice.88), channel_id=1, source_target_pairs={{0,68},{1,69},{2,70},{3,71},{4,64},{5,65},{6,66},{7,67},{64,4},{65... | collective-permute-start | bytes 294920 | tf_op jit(solution)/shard_map/ppermute | solution.py:46
  268.3 2.5 copy-start.5
Sparse Core Ops, SparseCore 0:
  115.7 152.5 all-reduce.2

commit v2 on v1

v2 whole, which is shorter than its diff:
```python
import jax
import jax.numpy as jnp
from jax import lax
from jax.sharding import Mesh
from jax.sharding import PartitionSpec as P

F32 = jnp.float32
BF16 = jnp.bfloat16


def gelu_value(wide):
    return 0.5 * wide * (1.0 + jax.scipy.special.erf(wide * 0.7071067811865476))


def gelu_slope(wide):
    return (
        0.5 * (1.0 + jax.scipy.special.erf(wide * 0.7071067811865476))
        + wide * jnp.exp(-0.5 * wide * wide) * 0.3989422804014327
    )


def contract(left, right, dims):
    return lax.dot_general(left, right, (dims, ((), ())), preferred_element_type=F32)


def scatter_sum(values, axis):
    count = lax.axis_size(axis)
    parts = lax.all_to_all(values, axis, 0, 0, tiled=True)
    parts = parts.reshape((count, parts.shape[0] // count) + parts.shape[1:])
    return jnp.sum(parts.astype(F32), axis=0)


def spread(values, axis):
    count = lax.axis_size(axis)
    copies = jnp.broadcast_to(values[None], (count,) + values.shape)
    return lax.all_to_all(copies.reshape((-1,) + values.shape[1:]), axis, 0, 0, tiled=True)


def on_device(inputs, up_weight, down_weight, out_grad):
    own, features = inputs.shape
    half = up_weight.shape[1] // 2
    start = lax.axis_index("e") * half
    up_half = lax.dynamic_slice_in_dim(up_weight, start, half, 1)
    down_half = lax.dynamic_slice_in_dim(down_weight, start, half, 0)
    loss_scale = float(own * 64) ** (-0.5)

    rows = jnp.concatenate([inputs, out_grad], axis=1)
    rows = lax.all_gather(rows, ("h", "e"), axis=0, tiled=True)
    rows = spread(rows, "x")
    every_input, every_grad = rows[:, :features], rows[:, features:]

    partial = jnp.concatenate(
        [
            contract(every_input, up_half, ((1,), (0,))).astype(BF16),
            contract(every_grad, down_half, ((1,), (1,))).astype(BF16),
        ],
        axis=1,
    )
    partial = scatter_sum(partial, "k").astype(BF16)
    sums = scatter_sum(partial, "y")
    preact = sums[:, :half].astype(BF16).astype(F32)
    act = gelu_value(preact).astype(BF16)
    hidden_grad = (sums[:, half:] * gelu_slope(preact)).astype(BF16)
    both = jnp.concatenate([act, hidden_grad], axis=1)
    both = spread(spread(both, "y"), "k")
    every_act, every_hidden = both[:, :half], both[:, half:]

    down_term = (loss_scale * contract(every_act, every_grad, ((0,), (0,)))).astype(BF16)
    up_term = (loss_scale * contract(every_input, every_hidden, ((0,), (0,)))).astype(BF16)
    up_piece = scatter_sum(up_term, "l").astype(BF16)
    down_piece = scatter_sum(down_term, "l").astype(BF16)
    piece = jnp.concatenate([up_piece[:, :features], up_piece[:, features:], down_piece], axis=0)
    pieces = lax.all_gather(piece, ("e", "l"), axis=0, tiled=False)
    quarter = features // 4
    pieces = pieces.reshape(2, 4, 4 * quarter, features)
    up_grad = pieces[:, :, : 2 * quarter].reshape(2, 4, 2, quarter, features)
    up_grad = up_grad.transpose(1, 3, 0, 2, 4).reshape(features, 2 * half)
    down_grad = pieces[:, :, 2 * quarter :].reshape(2 * half, features)

    features_part = jnp.concatenate(
        [
            contract(every_act, down_half, ((1,), (0,))).astype(BF16),
            contract(every_hidden, up_half, ((1,), (1,))).astype(BF16),
        ],
        axis=1,
    )
    total = scatter_sum(features_part, "x").astype(BF16)
    total = scatter_sum(total, ("h", "e")).astype(BF16)
    return total[:, :features], total[:, features:], up_grad, down_grad


def solution(mesh):
    split = Mesh(mesh.devices.reshape(4, 2, 4, 2, 2, 4), ("x", "h", "y", "k", "e", "l"))
    rows = P(("e", "l", "x", "h"), ("y", "k"))
    up = P(("y", "k"), ("x", "h"))
    down = P(("x", "h"), ("y", "k"))
    return jax.shard_map(
        on_device,
        mesh=split,
        in_specs=(rows, up, down, rows),
        out_specs=(rows, rows, up, down),
        check_vma=False,
    )
```

time: 279 us -> 266 us (0.953)
  waiting for transfers between devices: 132 us -> 61.1 us
  blocking collectives: 90.1 us -> 151 us
  starting transfers between devices: 21.2 us -> 11.8 us
  other arithmetic: 3.91 us -> 6.77 us
    psum x1 -> x0, waiting for transfers between devices: 111 us -> none  [on_device(): up_grad, down_grad = lax.psum((up_term, down_term), 'd')]
    all_to_all x3 -> x4, blocking collectives: 47.3 us -> 91.4 us  [scatter_sum(): parts = lax.all_to_all(values, axis, 0, 0, tiled=True)]
    all_to_all x0 -> x3, waiting for transfers between devices: none -> 43.8 us  [the longest x2 28.7 us: scatter_sum(): parts = lax.all_to_all(values, axis, 0, 0, tiled=True)]
    ppermute x2 -> x0, waiting for transfers between devices: 21.5 us -> none  [other_half(): return lax.ppermute(values, ('h', 'd'), pairs)]
    ppermute x2 -> x0, starting transfers between devices: 21.1 us -> none  [other_half(): return lax.ppermute(values, ('h', 'd'), pairs)]
    all_gather x0 -> x1, waiting for transfers between devices: none -> 17.3 us  [on_device(): pieces = lax.all_gather(piece, ('e', 'l'), axis=0, tiled=False)]
    all_gather x1, blocking collectives: 14.2 us -> 30.5 us  [on_device(): rows = lax.all_gather(rows, ('h', 'e'), axis=0, tiled=True)]
    all_to_all x0 -> x3, starting transfers between devices: none -> 11.7 us  [the longest x2 6.96 us: scatter_sum(): parts = lax.all_to_all(values, axis, 0, 0, tiled=True)]
  transfers between devices with their start and end apart: 3 -> 4, of which waited for: 3 -> 4; matrix products, arithmetic and copies ran while one was open for 2% -> 3% of each run, Pallas kernels for 0% -> 0%
where the time goes in v2:
time: 266 us; the launch traced here: 265 us
  blocking collectives  151 us (57%)
  waiting for transfers between devices  61.1 us (23%)
  between operations  14.3 us (5%)
  starting transfers between devices  11.8 us (4%)
  matrix products  11.8 us (4%)
  local copies, waits for them, and re-layouts  8.92 us (3%)
  other arithmetic  6.77 us (3%)
    all_to_all x4, blocking collectives, scatter_sum(): parts = lax.all_to_all(values, axis, 0, 0, tiled=True)  91.4 us
    all_gather x1, blocking collectives, on_device(): rows = lax.all_gather(rows, ('h', 'e'), axis=0, tiled=True)  30.5 us
    all_to_all x2, blocking collectives, spread(): lax.all_to_all(copies.reshape((-1,) + values.shape[1:]), axis, 0, 0, tile...  28.7 us
    all_to_all x2, waiting for transfers between devices, scatter_sum(): parts = lax.all_to_all(values, axis, 0, 0, tiled=True)  28.7 us
    all_gather x1, waiting for transfers between devices, on_device(): pieces = lax.all_gather(piece, ('e', 'l'), axis=0, tiled=False)  17.3 us
    all_to_all x1, waiting for transfers between devices, spread(): lax.all_to_all(copies.reshape((-1,) + values.shape[1:]), axis, 0, 0, tile...  15.1 us
    dot_general x6, matrix products, contract(): lax.dot_general(left, right, (dims, ((), ())), preferred_element_type=F32)  11.8 us
    all_to_all x2, starting transfers between devices, scatter_sum(): parts = lax.all_to_all(values, axis, 0, 0, tiled=True)  6.96 us
  transfers between devices with their start and end apart: 4, of which 4 were waited for; matrix products, arithmetic and copies ran while one was open for 3% of the time, Pallas kernels for 0%

profile of v2, /device:TPU:6, one launch (start us, length us, event | category | flops | bytes accessed | tf_op | source)
XLA Modules:
  0.0 265.1 jit_solution(7350936934561122500)
XLA Ops:
  7.2 0.0 copy-start
  7.2 0.9 pad_maximum_fusion.4
  8.1 30.5 %all_gather.9 = bf16[256,768]{1,0:T(8,128)(2,1)S(1)} all-gather(bf16[64,768]{1,0:T(8,128)(2,1)S(1)} %pad_maximum_fusion.4), channel_id=1, replica_groups=mesh['x'=4,'h'=2,'y'=4,'k'=2,'e'=2,'l'=4] {'h','e'}, dimensions={0}, use_global_device_ids=true | all-gather | bytes 491520 | tf_op jit(solution)/shard_map/all_gather | solution.py:48
  38.6 1.3 broadcast_in_dim.8
  39.9 4.8 %all-to-all-start = ((bf16[4,256,768]{2,1,0:T(8,128)(2,1)}), bf16[4,256,768]{2,1,0:T(8,128)(2,1)S(1)}, u32[]{:S(2)}, u32[]{:S(2)}) async-start(bf16[4,256,768]{2,1,0:T(8,128)(2,1)} %broadcast_in_dim.8), calls=%async_computation | async-start | bytes 3145728 | tf_op jit(solution)/shard_map/all_to_all | solution.py:36
  44.7 15.1 %all-to-all-done = bf16[4,256,768]{2,1,0:T(8,128)(2,1)S(1)} async-done(((bf16[4,256,768]{2,1,0:T(8,128)(2,1)}), bf16[4,256,768]{2,1,0:T(8,128)(2,1)S(1)}, u32[]{:S(2)}, u32[]{:S(2)}) %all-to-all-start) | async-done | bytes 1572896 | tf_op jit(solution)/shard_map/all_to_all | solution.py:36
  59.8 2.5 convolution_convert_fusion
  62.3 1.0 convolution_convert_fusion.1
  63.3 0.3 pad_maximum_fusion
  63.6 0.2 copy.39
  63.8 7.2 %all_to_all.78 = bf16[2,512,1536]{1,2,0:T(8,128)(2,1)} all-to-all(bf16[2,512,1536]{1,2,0:T(8,128)(2,1)S(1)} %bitcast.26), channel_id=1, replica_groups=mesh['x'=4,'h'=2,'y'=4,'k'=2,'e'=2,'l'=4] {'k'}, dimensions={0} | all-to-all | bytes 6291456 | tf_op jit(solution)/shard_map/all_to_all | solution.py:28
  71.1 3.5 %reduce_sum.69 = bf16[512,1536]{0,1:T(8,128)(2,1)S(1)} reduce(bf16[2,512,1536]{1,2,0:T(8,128)(2,1)} %all_to_all.78, bf16[]{:T(256)} %constant.12.clone.1), dimensions={0}, to_apply=%region_0.0 | reduce | flops 786432 | bytes 4718594 | tf_op jit(solution)/shard_map/reduce_sum | solution.py:30
  74.6 0.3 copy_bitcast_fusion.2
  74.9 25.3 %all_to_all.79 = bf16[4,128,1536]{1,2,0:T(8,128)(2,1)S(1)} all-to-all(bf16[4,128,1536]{1,2,0:T(8,128)(2,1)S(1)} %copy_bitcast_fusion.2), channel_id=1, replica_groups=mesh['x'=4,'h'=2,'y'=4,'k'=2,'e'=2,'l'=4] {'y'}, dimensions={0} | all-to-all | bytes 3145728 | tf_op jit(solution)/shard_map/all_to_all | solution.py:28
  100.1 0.2 convert_reduce_fusion
  100.4 0.2 fusion.19
  100.6 0.2 copy.24
  100.8 0.1 broadcast_in_dim.9
  100.9 22.3 %all_to_all.80 = bf16[4,128,1536]{2,1,0:T(8,128)(2,1)S(1)} all-to-all(bf16[4,128,1536]{2,1,0:T(8,128)(2,1)S(1)} %broadcast_in_dim.9), channel_id=1, replica_groups=mesh['x'=4,'h'=2,'y'=4,'k'=2,'e'=2,'l'=4] {'y'}, dimensions={0} | all-to-all | bytes 3145728 | tf_op jit(solution)/shard_map/all_to_all | solution.py:36
  123.2 0.2 broadcast_in_dim.11
  123.4 0.0 copy-start.4
  123.5 6.4 %all_to_all.81 = bf16[2,512,1536]{2,1,0:T(8,128)(2,1)S(1)} all-to-all(bf16[2,512,1536]{2,1,0:T(8,128)(2,1)S(1)} %broadcast_in_dim.11), channel_id=1, replica_groups=mesh['x'=4,'h'=2,'y'=4,'k'=2,'e'=2,'l'=4] {'k'}, dimensions={0} | all-to-all | bytes 6291456 | tf_op jit(solution)/shard_map/all_to_all | solution.py:36
  129.9 1.8 fusion.4
  131.7 3.5 %all-to-all-start.7 = ((bf16[4,96,768]{2,1,0:T(8,128)(2,1)}), bf16[4,96,768]{2,1,0:T(8,128)(2,1)S(1)}, u32[]{:S(2)}, u32[]{:S(2)}) async-start(bf16[4,96,768]{2,1,0:T(8,128)(2,1)} %bitcast.44), calls=%async_computation.7 | async-start | bytes 1179648 | tf_op jit(solution)/shard_map/all_to_all | solution.py:28
  135.2 3.2 %fusion.7 = bf16[768,384]{1,0:T(8,128)(2,1)} fusion(bf16[1024,1536]{1,0:T(8,128)(2,1)} %bitcast.33, bf16[1024,768]{1,0:T(8,128)(2,1)S(1)} %bitcast.40), kind=kOutput, calls=%fused_computation.17 | convolution fusion | flops 604569600 | bytes 2949120 | tf_op jit(solution)/shard_map/dot_general | solution.py:23
  138.4 13.2 %all-to-all-done.7 = bf16[4,96,768]{2,1,0:T(8,128)(2,1)S(1)} async-done(((bf16[4,96,768]{2,1,0:T(8,128)(2,1)}), bf16[4,96,768]{2,1,0:T(8,128)(2,1)S(1)}, u32[]{:S(2)}, u32[]{:S(2)}) %all-to-all-start.7) | async-done | bytes 589856 | tf_op jit(solution)/shard_map/all_to_all | solution.py:28
  151.6 3.5 %all-to-all-start.8 = ((bf16[4,192,384]{2,1,0:T(8,128)(2,1)}), bf16[4,192,384]{2,1,0:T(8,128)(2,1)S(1)}, u32[]{:S(2)}, u32[]{:S(2)}) async-start(bf16[4,192,384]{2,1,0:T(8,128)(2,1)} %bitcast.43), calls=%async_computation.8 | async-start | bytes 1179648 | tf_op jit(solution)/shard_map/all_to_all | solution.py:28
  155.1 0.0 all-gather.3.cloned.1.call-start
  155.2 0.1 reduce_sum.73
  155.3 15.4 %all-to-all-done.8 = bf16[4,192,384]{2,1,0:T(8,128)(2,1)S(1)} async-done(((bf16[4,192,384]{2,1,0:T(8,128)(2,1)}), bf16[4,192,384]{2,1,0:T(8,128)(2,1)S(1)}, u32[]{:S(2)}, u32[]{:S(2)}) %all-to-all-start.8) | async-done | bytes 589856 | tf_op jit(solution)/shard_map/all_to_all | solution.py:28
  170.7 0.1 reduce_sum.74
  170.8 0.7 pad_maximum_fusion.3
  171.6 0.0 all-gather.3.cloned.1.call-update
  171.6 2.4 convolution_convert_fusion.2
  174.0 0.3 copy-done.2
  174.3 0.8 convolution_convert_fusion.3
  175.1 0.1 pad_maximum_fusion.1
  175.3 0.1 copy.40
  175.4 22.6 %all_to_all.82 = bf16[4,256,768]{1,2,0:T(8,128)(2,1)S(1)} all-to-all(bf16[4,256,768]{1,2,0:T(8,128)(2,1)S(1)} %bitcast.28), channel_id=1, replica_groups=mesh['x'=4,'h'=2,'y'=4,'k'=2,'e'=2,'l'=4] {'x'}, dimensions={0} | all-to-all | bytes 3145728 | tf_op jit(solution)/shard_map/all_to_all | solution.py:28
  198.0 0.4 reduce_sum.71
  198.5 0.2 copy.27
  198.7 36.2 %all_to_all.83 = bf16[4,64,768]{2,1,0:T(8,128)(2,1)S(1)} all-to-all(bf16[4,64,768]{2,1,0:T(8,128)(2,1)S(1)} %bitcast.41), channel_id=1, replica_groups=mesh['x'=4,'h'=2,'y'=4,'k'=2,'e'=2,'l'=4] {'h','e'}, dimensions={0} | all-to-all | bytes 786432 | tf_op jit(solution)/shard_map/all_to_all | solution.py:28
  234.9 0.1 reduce_sum.72
  235.0 0.6 fusion.33
  235.6 17.3 %all-gather.3.cloned.1.call-done = bf16[3072,384]{1,0:T(8,128)(2,1)} async-done(((bf16[384,384]{1,0:T(8,128)(2,1)}), bf16[3072,384]{1,0:T(8,128)(2,1)}) %all-gather.3.cloned.1.call-update) | async-done | bytes 2359312 | tf_op jit(solution)/shard_map/all_gather | solution.py:73
  252.9 2.9 %fusion.31 = (bf16[2,4,192,384]{3,2,1,0:T(8,128)(2,1)}, bf16[2,4,192,384]{3,2,1,0:T(8,128)(2,1)S(1)}) fusion(bf16[2,4,384,384]{3,2,1,0:T(8,128)(2,1)} %bitcast.36), kind=kLoop, calls=%fused_computation.49 | loop fusion | bytes 4718592 | tf_op jit(solution)/shard_map/slice | solution.py:78
  255.8 0.9 copy.41
  256.7 1.6 reshape.62
  (11 shorter events, 0.1 us)
Async XLA Ops:
  7.2 55.1 %copy-start = (bf16[384,1536]{1,0:T(8,128)(2,1)S(1)}, bf16[384,1536]{1,0:T(8,128)(2,1)}, u32[]{:S(2)}) copy-start(bf16[384,1536]{1,0:T(8,128)(2,1)} %param.5) | copy-start | bytes 3538948
  39.9 19.9 %all-to-all-start = ((bf16[4,256,768]{2,1,0:T(8,128)(2,1)}), bf16[4,256,768]{2,1,0:T(8,128)(2,1)S(1)}, u32[]{:S(2)}, u32[]{:S(2)}) async-start(bf16[4,256,768]{2,1,0:T(8,128)(2,1)} %broadcast_in_dim.8), calls=%async_computation | async-start | bytes 3145728 | tf_op jit(solution)/shard_map/all_to_all | solution.py:36
  59.8 3.5 %copy-start.3 = (bf16[4,256,768]{2,1,0:T(8,128)(2,1)}, bf16[4,256,768]{2,1,0:T(8,128)(2,1)S(1)}, u32[]{:S(2)}) copy-start(bf16[4,256,768]{2,1,0:T(8,128)(2,1)S(1)} %all-to-all-done) | copy-start | bytes 4718596
  123.4 6.4 %copy-start.4 = (bf16[4,256,768]{2,1,0:T(8,128)(2,1)S(1)}, bf16[4,256,768]{2,1,0:T(8,128)(2,1)}, u32[]{:S(2)}) copy-start(bf16[4,256,768]{2,1,0:T(8,128)(2,1)} %copy-done.3) | copy-start | bytes 4718596
  129.8 1.9 copy-start.1
  131.7 19.9 %all-to-all-start.7 = ((bf16[4,96,768]{2,1,0:T(8,128)(2,1)}), bf16[4,96,768]{2,1,0:T(8,128)(2,1)S(1)}, u32[]{:S(2)}, u32[]{:S(2)}) async-start(bf16[4,96,768]{2,1,0:T(8,128)(2,1)} %bitcast.44), calls=%async_computation.7 | async-start | bytes 1179648 | tf_op jit(solution)/shard_map/all_to_all | solution.py:28
  151.6 19.1 %all-to-all-start.8 = ((bf16[4,192,384]{2,1,0:T(8,128)(2,1)}), bf16[4,192,384]{2,1,0:T(8,128)(2,1)S(1)}, u32[]{:S(2)}, u32[]{:S(2)}) async-start(bf16[4,192,384]{2,1,0:T(8,128)(2,1)} %bitcast.43), calls=%async_computation.8 | async-start | bytes 1179648 | tf_op jit(solution)/shard_map/all_to_all | solution.py:28
  155.1 97.8 %all-gather.3.cloned.1.call-start = ((), (), s32[]{:S(2)}) async-start(), calls=%async_computation.9 | async-start | bytes 2654208 | tf_op jit(solution)/shard_map/all_gather | solution.py:73
  171.6 2.4 copy-start.5
  171.6 2.7 %copy-start.2 = (bf16[2,512,1536]{2,1,0:T(8,128)(2,1)S(1)}, bf16[2,512,1536]{2,1,0:T(8,128)(2,1)}, u32[]{:S(2)}) copy-start(bf16[2,512,1536]{2,1,0:T(8,128)(2,1)} %copy-done.1) | copy-start | bytes 9437188
Sparse Core Ops, SparseCore 0:
  171.7 81.1 all-gather.2

commit v3 on v2

v3 whole, which is shorter than its diff:
```python
import jax
import jax.numpy as jnp
from jax import lax
from jax.experimental import pallas as pl
from jax.experimental.pallas import tpu as pltpu
from jax.sharding import Mesh
from jax.sharding import PartitionSpec as P

F32 = jnp.float32
BF16 = jnp.bfloat16

FOLDED = [0, 2, 4, 6, 7, 5, 3, 1]


def gelu_value(wide):
    return 0.5 * wide * (1.0 + jax.scipy.special.erf(wide * 0.7071067811865476))


def gelu_slope(wide):
    return (
        0.5 * (1.0 + jax.scipy.special.erf(wide * 0.7071067811865476))
        + wide * jnp.exp(-0.5 * wide * wide) * 0.3989422804014327
    )


def contract(left, right, dims):
    return lax.dot_general(left, right, (dims, ((), ())), preferred_element_type=F32)


def scatter_sum(values, axis):
    count = lax.axis_size(axis)
    parts = lax.all_to_all(values, axis, 0, 0, tiled=True)
    parts = parts.reshape((count, parts.shape[0] // count) + parts.shape[1:])
    return jnp.sum(parts.astype(F32), axis=0)


def gather(values, axis):
    return lax.all_gather(values, axis, axis=0, tiled=True)


def other_core(values):
    return lax.ppermute(values, "k", [(0, 1), (1, 0)])


def after(values, earlier):
    return lax.optimization_barrier((values, earlier))[0]


def place_kernel(pieces, up, down, sems):
    copies = []
    features = down.shape[1]
    quarter = features // 4
    for slot, source in enumerate(FOLDED):
        e, l = source // 4, source % 4
        for side in range(2):
            rows, cols = l * quarter, (2 * e + side) * features
            copies.append(
                (
                    pieces.at[slot, pl.ds(side * quarter, quarter)],
                    up.at[pl.ds(rows, quarter), pl.ds(cols, features)],
                )
            )
        copies.append(
            (
                pieces.at[slot, pl.ds(2 * quarter, 2 * quarter)],
                down.at[pl.ds(source * 2 * quarter, 2 * quarter)],
            )
        )
    copies = [pltpu.make_async_copy(*pair, sems.at[i]) for i, pair in enumerate(copies)]
    for copy in copies:
        copy.start()
    for copy in copies:
        copy.wait()


def place(pieces):
    features = pieces.shape[2]
    vmem = pl.BlockSpec(memory_space=pltpu.VMEM)
    return pl.pallas_call(
        place_kernel,
        out_shape=(
            jax.ShapeDtypeStruct((features, 4 * features), BF16),
            jax.ShapeDtypeStruct((4 * features, features), BF16),
        ),
        in_specs=[pl.BlockSpec(memory_space=pl.ANY)],
        out_specs=(vmem, vmem),
        scratch_shapes=[pltpu.SemaphoreType.DMA((3 * len(FOLDED),))],
    )(pieces)


def on_device(inputs, up_weight, down_weight, out_grad):
    own, features = inputs.shape
    core = lax.axis_index("k")
    half = up_weight.shape[1] // 2
    start = lax.axis_index("e") * half
    up_half = lax.dynamic_slice_in_dim(up_weight, start, half, 1)
    down_half = lax.dynamic_slice_in_dim(down_weight, start, half, 0)
    loss_scale = float(own * 64) ** (-0.5)

    rows = jnp.concatenate([inputs, out_grad], axis=1)
    swapped = jnp.concatenate([rows[own // 2 :], rows[: own // 2]], axis=0)
    rows = gather(jnp.where(core == 0, rows, swapped), ("h", "e"))

    def split(gathered):
        blocks = gathered.reshape(-1, 2, own // 2, features)
        return [blocks[:, side].reshape(-1, features) for side in range(2)]

    my_input, far_input = split(gather(rows[:, :features], "x"))

    far = contract(far_input, up_half, ((1,), (0,))).astype(BF16)
    part = contract(my_input, up_half, ((1,), (0,))) + other_core(far).astype(F32)
    part = part.astype(BF16)
    preact_sum = scatter_sum(part, "y")

    grad_rows = after(rows[:, features:], part)
    my_grad, far_grad = split(after(gather(grad_rows, "x"), preact_sum))
    far = contract(far_grad, down_half, ((1,), (1,))).astype(BF16)
    part = contract(my_grad, down_half, ((1,), (1,))) + other_core(far).astype(F32)
    part = part.astype(BF16)
    act_grad = scatter_sum(part, "y")

    preact = preact_sum.astype(BF16).astype(F32)
    my_act, act_grad, preact = lax.optimization_barrier(
        (gather(gelu_value(preact).astype(BF16), "y"), act_grad, preact)
    )
    far_act = other_core(my_act)
    down_term = loss_scale * (
        contract(my_act, my_grad, ((0,), (0,))) + contract(far_act, far_grad, ((0,), (0,)))
    )
    down_term = down_term.astype(BF16)
    down_piece = scatter_sum(down_term, "l").astype(BF16)

    hidden_grad = (act_grad * gelu_slope(preact)).astype(BF16)
    my_hidden = gather(after(hidden_grad, down_term), "y")
    far_hidden = other_core(my_hidden)
    up_term = loss_scale * (
        contract(my_input, my_hidden, ((0,), (0,))) + contract(far_input, far_hidden, ((0,), (0,)))
    )
    up_piece = scatter_sum(up_term.astype(BF16), "l").astype(BF16)

    piece = jnp.concatenate([up_piece[:, :features], up_piece[:, features:], down_piece], axis=0)
    pieces = lax.all_gather(piece, ("e", "l"), axis_index_groups=[FOLDED])
    up_grad, down_grad = place(pieces)
    my_act, my_hidden, far_act, far_hidden, _ = lax.optimization_barrier(
        (my_act, my_hidden, far_act, far_hidden, piece)
    )

    blocks = 16
    sides = []
    for act, hidden in ((my_act, my_hidden), (far_act, far_hidden)):
        side = jnp.concatenate(
            [
                contract(act, down_half, ((1,), (0,))).astype(BF16),
                contract(hidden, up_half, ((1,), (1,))).astype(BF16),
            ],
            axis=1,
        )
        sides.append(side.reshape(blocks, own // 2, 2 * features))
    total = jnp.stack(sides, axis=1).reshape(blocks * own, 2 * features)
    total = scatter_sum(total, "x").astype(BF16)
    total = scatter_sum(total, ("h", "e")).astype(BF16)
    swapped = jnp.concatenate([total[own // 2 :], total[: own // 2]], axis=0)
    total = jnp.where(core == 0, total, swapped)
    return total[:, :features], total[:, features:], up_grad, down_grad


def solution(mesh):
    split = Mesh(mesh.devices.reshape(4, 2, 4, 2, 2, 4), ("x", "h", "y", "k", "e", "l"))
    rows = P(("e", "l", "x", "h"), ("y", "k"))
    up = P(("y", "k"), ("x", "h"))
    down = P(("x", "h"), ("y", "k"))
    return jax.shard_map(
        on_device,
        mesh=split,
        in_specs=(rows, up, down, rows),
        out_specs=(rows, rows, up, down),
        check_vma=False,
    )
```

time: 266 us -> 255 us (0.959)
  waiting for transfers between devices: 61.1 us -> 33 us
  starting transfers between devices: 11.8 us -> 25.4 us
  Pallas kernels: 0 us -> 3.3 us
    all_gather x1 -> x5, blocking collectives: 30.5 us -> 93.4 us  [gather(): return lax.all_gather(values, axis, axis=0, tiled=True)]
    all_to_all x4 -> x2, blocking collectives: 91.4 us -> 56.8 us  [scatter_sum(): parts = lax.all_to_all(values, axis, 0, 0, tiled=True)]
    all_to_all x2 -> x0, blocking collectives: 28.7 us -> none  [spread(): lax.all_to_all(copies.reshape((-1,) + values.shape[1:]), axis, 0, 0, tile...]
    all_to_all x1 -> x0, waiting for transfers between devices: 15.1 us -> none  [spread(): lax.all_to_all(copies.reshape((-1,) + values.shape[1:]), axis, 0, 0, tile...]
    all_to_all x2 -> x4, waiting for transfers between devices: 28.7 us -> 15.4 us  [scatter_sum(): parts = lax.all_to_all(values, axis, 0, 0, tiled=True)]
    all_to_all x2 -> x4, starting transfers between devices: 6.96 us -> 17.7 us  [scatter_sum(): parts = lax.all_to_all(values, axis, 0, 0, tiled=True)]
    ppermute x0 -> x4, waiting for transfers between devices: none -> 7.9 us  [other_core(): return lax.ppermute(values, 'k', [(0, 1), (1, 0)])]
    ppermute x0 -> x4, starting transfers between devices: none -> 7.66 us  [other_core(): return lax.ppermute(values, 'k', [(0, 1), (1, 0)])]
  transfers between devices with their start and end apart: 4 -> 9, of which waited for: 4 -> 6; matrix products, arithmetic and copies ran while one was open for 3% -> 5% of each run, Pallas kernels for 0% -> 0%
where the time goes in v3:
time: 255 us; the launch traced here: 253 us
  blocking collectives  150 us (59%)
  waiting for transfers between devices  33 us (13%)
  starting transfers between devices  25.4 us (10%)
  between operations  14.3 us (6%)
  matrix products  12.1 us (5%)
  other arithmetic  7.83 us (3%)
  local copies, waits for them, and re-layouts  6.49 us (3%)
  Pallas kernels  3.3 us (1%)
    all_gather x5, blocking collectives, gather(): return lax.all_gather(values, axis, axis=0, tiled=True)  93.4 us
    all_to_all x2, blocking collectives, scatter_sum(): parts = lax.all_to_all(values, axis, 0, 0, tiled=True)  56.8 us
    all_to_all x4, starting transfers between devices, scatter_sum(): parts = lax.all_to_all(values, axis, 0, 0, tiled=True)  17.7 us
    all_to_all x4, waiting for transfers between devices, scatter_sum(): parts = lax.all_to_all(values, axis, 0, 0, tiled=True)  15.4 us
    dot_general x12, matrix products, contract(): lax.dot_general(left, right, (dims, ((), ())), preferred_element_type=F32)  12.1 us
    all_gather x1, waiting for transfers between devices, on_device(): pieces = lax.all_gather(piece, ('e', 'l'), axis_index_groups=[FOLDED])  9.68 us
    ppermute x4, waiting for transfers between devices, other_core(): return lax.ppermute(values, 'k', [(0, 1), (1, 0)])  7.9 us
    ppermute x4, starting transfers between devices, other_core(): return lax.ppermute(values, 'k', [(0, 1), (1, 0)])  7.66 us
  transfers between devices with their start and end apart: 9, of which 6 were waited for; matrix products, arithmetic and copies ran while one was open for 5% of the time, Pallas kernels for 0%

profile of v3, /device:TPU:6, one launch (start us, length us, event | category | flops | bytes accessed | tf_op | source)
XLA Modules:
  0.0 252.7 jit_solution(3374726022709252954)
XLA Ops:
  7.2 0.9 constant_dynamic-update-slice_fusion.1
  8.1 0.8 constant_dynamic-update-slice_fusion
  8.9 30.5 %all_gather.21 = bf16[256,768]{1,0:T(8,128)(2,1)S(1)} all-gather(bf16[64,768]{1,0:T(8,128)(2,1)S(1)} %maximum_select_fusion), channel_id=1, replica_groups=mesh['x'=4,'h'=2,'y'=4,'k'=2,'e'=2,'l'=4] {'h','e'}, dimensions={0}, use_global_device_ids=true | all-gather | bytes 491520 | tf_op jit(solution)/shard_map/all_gather | solution.py:38
  39.5 14.0 %all_gather.22 = bf16[1024,384]{1,0:T(8,128)(2,1)S(1)} all-gather(bf16[256,384]{1,0:T(8,128)(2,1)S(1)} %get-tuple-element.33), channel_id=1, replica_groups=mesh['x'=4,'h'=2,'y'=4,'k'=2,'e'=2,'l'=4] {'x'}, dimensions={0}, use_global_device_ids=true | all-gather | bytes 983040 | tf_op jit(solution)/shard_map/all_gather | solution.py:38
  53.6 0.6 convolution_convert_fusion.1
  54.2 1.9 collective-permute-start
  56.1 2.3 collective-permute-done
  58.4 1.5 add_convert_fusion.1
  59.8 4.5 %all-to-all-start = ((bf16[4,128,768]{2,1,0:T(8,128)(2,1)}), bf16[4,128,768]{2,1,0:T(8,128)(2,1)S(1)}, u32[]{:S(2)}, u32[]{:S(2)}) async-start(bf16[4,128,768]{2,1,0:T(8,128)(2,1)} %bitcast.3), calls=%async_computation | async-start | bytes 1572864 | tf_op jit(solution)/shard_map/all_to_all | solution.py:32
  64.3 14.8 %all_gather.24 = bf16[1024,384]{1,0:T(8,128)(2,1)} all-gather(bf16[256,384]{1,0:T(8,128)(2,1)S(1)} %get-tuple-element.16), channel_id=1, replica_groups=mesh['x'=4,'h'=2,'y'=4,'k'=2,'e'=2,'l'=4] {'x'}, dimensions={0}, use_global_device_ids=true | all-gather | bytes 983040 | tf_op jit(solution)/shard_map/all_gather | solution.py:38
  79.1 0.8 convert_reduce_fusion.1
  80.7 0.6 convolution_convert_fusion
  81.3 1.9 collective-permute-start.1
  83.2 2.3 collective-permute-done.1
  85.5 1.5 add_convert_fusion
  86.9 4.8 %all-to-all-start.1 = ((bf16[4,128,768]{2,1,0:T(8,128)(2,1)}), bf16[4,128,768]{2,1,0:T(8,128)(2,1)S(1)}, u32[]{:S(2)}, u32[]{:S(2)}) async-start(bf16[4,128,768]{2,1,0:T(8,128)(2,1)} %bitcast.42), calls=%async_computation.1 | async-start | bytes 1572864 | tf_op jit(solution)/shard_map/all_to_all | solution.py:32
  91.7 1.7 convert_element_type.102
  93.4 1.0 multiply_convert_fusion
  94.4 19.9 %all_gather.23 = bf16[512,768]{1,0:T(8,128)(2,1)} all-gather(bf16[128,768]{1,0:T(8,128)(2,1)S(1)} %multiply_convert_fusion), channel_id=1, replica_groups=mesh['x'=4,'h'=2,'y'=4,'k'=2,'e'=2,'l'=4] {'y'}, dimensions={0}, use_global_device_ids=true | all-gather | bytes 983040 | tf_op jit(solution)/shard_map/all_gather | solution.py:38
  114.4 0.9 convert_reduce_fusion
  115.2 0.4 copy-done.2
  115.6 1.9 collective-permute-start.2
  117.6 0.6 fusion.39
  118.2 1.6 collective-permute-done.2
  119.8 1.4 fusion.2
  121.2 3.6 %all-to-all-start.3 = ((bf16[4,192,384]{2,1,0:T(8,128)(2,1)}), bf16[4,192,384]{2,1,0:T(8,128)(2,1)S(1)}, u32[]{:S(2)}, u32[]{:S(2)}) async-start(bf16[4,192,384]{2,1,0:T(8,128)(2,1)} %bitcast.9), calls=%async_computation.3 | async-start | bytes 1179648 | tf_op jit(solution)/shard_map/all_to_all | solution.py:32
  125.0 14.2 %all_gather.25 = bf16[512,768]{1,0:T(8,128)(2,1)S(1)} all-gather(bf16[128,768]{1,0:T(8,128)(2,1)S(1)} %fusion.9), channel_id=1, replica_groups=mesh['x'=4,'h'=2,'y'=4,'k'=2,'e'=2,'l'=4] {'y'}, dimensions={0}, use_global_device_ids=true | all-gather | bytes 983040 | tf_op jit(solution)/shard_map/all_gather | solution.py:38
  139.2 1.9 collective-permute-start.3
  141.1 0.5 fusion.40
  141.6 1.8 collective-permute-done.3
  143.4 0.9 copy-done.9
  144.3 1.3 fusion.3
  145.6 4.9 %all-to-all-start.2 = ((bf16[4,96,768]{2,1,0:T(8,128)(2,1)}), bf16[4,96,768]{2,1,0:T(8,128)(2,1)S(1)}, u32[]{:S(2)}, u32[]{:S(2)}) async-start(bf16[4,96,768]{2,1,0:T(8,128)(2,1)} %bitcast.46), calls=%async_computation.2 | async-start | bytes 1179648 | tf_op jit(solution)/shard_map/all_to_all | solution.py:32
  150.5 0.8 reduce_sum.69
  151.3 15.4 %all-to-all-done.2 = bf16[4,96,768]{2,1,0:T(8,128)(2,1)S(1)} async-done(((bf16[4,96,768]{2,1,0:T(8,128)(2,1)}), bf16[4,96,768]{2,1,0:T(8,128)(2,1)S(1)}, u32[]{:S(2)}, u32[]{:S(2)}) %all-to-all-start.2) | async-done | bytes 589856 | tf_op jit(solution)/shard_map/all_to_all | solution.py:32
  166.8 1.7 pad_maximum_fusion.3
  168.5 0.5 convolution_convert_fusion.2
  169.0 0.6 copy-done.8
  169.6 1.6 convolution_convert_fusion.3
  171.5 0.5 convolution_convert_fusion.4
  172.1 0.6 copy-done.3
  172.7 1.6 convolution_convert_fusion.5
  174.9 22.2 %all_to_all.54 = bf16[4,256,768]{2,1,0:T(8,128)(2,1)S(1)} all-to-all(bf16[4,256,768]{2,1,0:T(8,128)(2,1)S(1)} %bitcast.31), channel_id=1, replica_groups=mesh['x'=4,'h'=2,'y'=4,'k'=2,'e'=2,'l'=4] {'x'}, dimensions={0} | all-to-all | bytes 3145728 | tf_op jit(solution)/shard_map/all_to_all | solution.py:32
  197.1 0.4 reduce_sum.70
  197.5 34.6 %all_to_all.55 = bf16[4,64,768]{2,1,0:T(8,128)(2,1)S(1)} all-to-all(bf16[4,64,768]{2,1,0:T(8,128)(2,1)S(1)} %bitcast.47), channel_id=1, replica_groups=mesh['x'=4,'h'=2,'y'=4,'k'=2,'e'=2,'l'=4] {'h','e'}, dimensions={0} | all-to-all | bytes 786432 | tf_op jit(solution)/shard_map/all_to_all | solution.py:32
  232.2 0.6 fusion.36
  232.9 9.7 %all-gather.3.cloned.1.call-done = bf16[3072,384]{1,0:T(8,128)(2,1)} async-done(((bf16[384,384]{1,0:T(8,128)(2,1)}), bf16[3072,384]{1,0:T(8,128)(2,1)}) %all-gather.3.cloned.1.call-update) | async-done | bytes 2359312 | tf_op jit(solution)/shard_map/all_gather | solution.py:142
  242.5 3.3 %shard_map.75 = (bf16[384,1536]{1,0:T(8,128)(2,1)}, bf16[1536,384]{1,0:T(8,128)(2,1)}) custom-call(bf16[8,384,384]{2,1,0:T(8,128)(2,1)} %bitcast.45), custom_call_target="tpu_custom_call" | custom-call | tf_op jit(solution)/shard_map/pallas_call | solution.py:79
  (40 shorter events, 2.3 us)
Async XLA Ops:
  7.2 46.5 %copy-start = (bf16[384,1536]{1,0:T(8,128)(2,1)S(1)}, bf16[384,1536]{1,0:T(8,128)(2,1)}, u32[]{:S(2)}) copy-start(bf16[384,1536]{1,0:T(8,128)(2,1)} %param.5) | copy-start | bytes 3538948
  54.2 4.2 %collective-permute-start = (bf16[512,768]{1,0:T(8,128)(2,1)S(1)}, bf16[512,768]{1,0:T(8,128)(2,1)S(1)}, u32[]{:S(2)}, u32[]{:S(2)}) collective-permute-start(bf16[512,768]{1,0:T(8,128)(2,1)S(1)} %convolution_convert_fusion.1), channel_id=1, source_target_pairs={{0,8},{8,0},{1,9},{9,1},{2,10},{10,2},{3,11},{11,3},{4,12},{12,4},... | collective-permute-start | bytes 2359304 | tf_op jit(solution)/shard_map/ppermute | solution.py:42
  59.8 19.3 %all-to-all-start = ((bf16[4,128,768]{2,1,0:T(8,128)(2,1)}), bf16[4,128,768]{2,1,0:T(8,128)(2,1)S(1)}, u32[]{:S(2)}, u32[]{:S(2)}) async-start(bf16[4,128,768]{2,1,0:T(8,128)(2,1)} %bitcast.3), calls=%async_computation | async-start | bytes 1572864 | tf_op jit(solution)/shard_map/all_to_all | solution.py:32
  79.1 1.2 copy-start.1
  79.1 1.6 copy-start.6
  81.3 4.2 %collective-permute-start.1 = (bf16[512,768]{1,0:T(8,128)(2,1)S(1)}, bf16[512,768]{1,0:T(8,128)(2,1)S(1)}, u32[]{:S(2)}, u32[]{:S(2)}) collective-permute-start(bf16[512,768]{1,0:T(8,128)(2,1)S(1)} %convolution_convert_fusion), channel_id=1, source_target_pairs={{0,8},{8,0},{1,9},{9,1},{2,10},{10,2},{3,11},{11,3},{4,12},{12,4},... | collective-permute-start | bytes 2359304 | tf_op jit(solution)/shard_map/ppermute | solution.py:42
  86.9 27.4 %all-to-all-start.1 = ((bf16[4,128,768]{2,1,0:T(8,128)(2,1)}), bf16[4,128,768]{2,1,0:T(8,128)(2,1)S(1)}, u32[]{:S(2)}, u32[]{:S(2)}) async-start(bf16[4,128,768]{2,1,0:T(8,128)(2,1)} %bitcast.42), calls=%async_computation.1 | async-start | bytes 1572864 | tf_op jit(solution)/shard_map/all_to_all | solution.py:32
  114.4 1.3 copy-start.2
  115.6 4.2 %collective-permute-start.2 = (bf16[512,768]{1,0:T(8,128)(2,1)S(1)}, bf16[512,768]{1,0:T(8,128)(2,1)S(1)}, u32[]{:S(2)}, u32[]{:S(2)}) collective-permute-start(bf16[512,768]{1,0:T(8,128)(2,1)S(1)} %copy-done.2), channel_id=1, source_target_pairs={{0,8},{8,0},{1,9},{9,1},{2,10},{10,2},{3,11},{11,3},{4,12},{12,4},... | collective-permute-start | bytes 2359304 | tf_op jit(solution)/shard_map/ppermute | solution.py:42
  119.8 1.4 copy-start.7
  121.2 3.6 %copy-start.4 = (f32[128,768]{1,0:T(8,128)S(1)}, f32[128,768]{1,0:T(8,128)}, u32[]{:S(2)}) copy-start(f32[128,768]{1,0:T(8,128)} %convert_element_type.102) | copy-start | bytes 1179652
  121.2 3.6 %copy-start.5 = (f32[128,768]{1,0:T(8,128)S(1)}, f32[128,768]{1,0:T(8,128)}, u32[]{:S(2)}) copy-start(f32[128,768]{1,0:T(8,128)} %convert_reduce_fusion) | copy-start | bytes 1179652
  121.2 24.4 %all-to-all-start.3 = ((bf16[4,192,384]{2,1,0:T(8,128)(2,1)}), bf16[4,192,384]{2,1,0:T(8,128)(2,1)S(1)}, u32[]{:S(2)}, u32[]{:S(2)}) async-start(bf16[4,192,384]{2,1,0:T(8,128)(2,1)} %bitcast.9), calls=%async_computation.3 | async-start | bytes 1179648 | tf_op jit(solution)/shard_map/all_to_all | solution.py:32
  139.2 4.2 %collective-permute-start.3 = (bf16[512,768]{1,0:T(8,128)(2,1)S(1)}, bf16[512,768]{1,0:T(8,128)(2,1)S(1)}, u32[]{:S(2)}, u32[]{:S(2)}) collective-permute-start(bf16[512,768]{1,0:T(8,128)(2,1)S(1)} %all_gather.25), channel_id=1, source_target_pairs={{0,8},{8,0},{1,9},{9,1},{2,10},{10,2},{3,11},{11,3},{4,12},{12,4},... | collective-permute-start | bytes 2359304 | tf_op jit(solution)/shard_map/ppermute | solution.py:42
  143.4 0.9 copy-start.9
  145.6 21.1 %all-to-all-start.2 = ((bf16[4,96,768]{2,1,0:T(8,128)(2,1)}), bf16[4,96,768]{2,1,0:T(8,128)(2,1)S(1)}, u32[]{:S(2)}, u32[]{:S(2)}) async-start(bf16[4,96,768]{2,1,0:T(8,128)(2,1)} %bitcast.46), calls=%async_computation.2 | async-start | bytes 1179648 | tf_op jit(solution)/shard_map/all_to_all | solution.py:32
  150.5 92.0 %all-gather.3.cloned.1.call-start = ((), (), s32[]{:S(2)}) async-start(), calls=%async_computation.6 | async-start | bytes 2654208 | tf_op jit(solution)/shard_map/all_gather | solution.py:142
  151.3 17.2 %copy-start.10 = (bf16[512,768]{1,0:T(8,128)(2,1)S(1)}, bf16[512,768]{1,0:T(8,128)(2,1)}, u32[]{:S(2)}) copy-start(bf16[512,768]{1,0:T(8,128)(2,1)} %copy-done.9) | copy-start | bytes 2359300
  168.5 1.1 copy-start.8
  171.5 1.1 copy-start.3
Sparse Core Ops, SparseCore 0:
  168.6 73.8 all-gather.2

commit v4 on v3

--- a/solution.py
+++ b/solution.py
@@ -90,77 +90,87 @@
 
 def on_device(inputs, up_weight, down_weight, out_grad):
     own, features = inputs.shape
-    core = lax.axis_index("k")
+    side = lax.axis_index("k")
     half = up_weight.shape[1] // 2
     start = lax.axis_index("e") * half
     up_half = lax.dynamic_slice_in_dim(up_weight, start, half, 1)
     down_half = lax.dynamic_slice_in_dim(down_weight, start, half, 0)
     loss_scale = float(own * 64) ** (-0.5)
 
-    rows = jnp.concatenate([inputs, out_grad], axis=1)
-    swapped = jnp.concatenate([rows[own // 2 :], rows[: own // 2]], axis=0)
-    rows = gather(jnp.where(core == 0, rows, swapped), ("h", "e"))
+    def half_rows(which):
+        return jnp.concatenate(
+            [
+                lax.dynamic_slice_in_dim(values, which * (own // 2), own // 2, 0)
+                for values in (inputs, out_grad)
+            ],
+            axis=1,
+        )
 
-    def split(gathered):
-        blocks = gathered.reshape(-1, 2, own // 2, features)
-        return [blocks[:, side].reshape(-1, features) for side in range(2)]
+    kept, received = half_rows(side), other_core(half_rows(1 - side))
+    up_half, down_half = after((up_half, down_half), received)
+    up_both = jnp.concatenate([up_half, other_core(up_half)], axis=0)
+    down_far = other_core(down_half)
+    rows = jnp.concatenate(
+        [
+            kept[:, :features],
+            received[:, :features],
+            kept[:, features:],
+            received[:, features:],
+        ],
+        axis=1,
+    )
+    rows = gather(after(rows, (up_half, down_half)), ("h", "e"))
 
-    my_input, far_input = split(gather(rows[:, :features], "x"))
-
-    far = contract(far_input, up_half, ((1,), (0,))).astype(BF16)
-    part = contract(my_input, up_half, ((1,), (0,))) + other_core(far).astype(F32)
-    part = part.astype(BF16)
+    every_input = gather(rows[:, : 2 * features], "x")
+    part = contract(every_input, up_both, ((1,), (0,))).astype(BF16)
     preact_sum = scatter_sum(part, "y")
 
-    grad_rows = after(rows[:, features:], part)
-    my_grad, far_grad = split(after(gather(grad_rows, "x"), preact_sum))
-    far = contract(far_grad, down_half, ((1,), (1,))).astype(BF16)
-    part = contract(my_grad, down_half, ((1,), (1,))) + other_core(far).astype(F32)
+    every_grad = after(gather(after(rows[:, 2 * features :], part), "x"), preact_sum)
+    my_grad, far_grad = every_grad[:, :features], every_grad[:, features:]
+    part = contract(my_grad, down_half, ((1,), (1,))) + contract(far_grad, down_far, ((1,), (1,)))
     part = part.astype(BF16)
     act_grad = scatter_sum(part, "y")
 
     preact = preact_sum.astype(BF16).astype(F32)
-    my_act, act_grad, preact = lax.optimization_barrier(
+    act, act_grad, preact = lax.optimization_barrier(
         (gather(gelu_value(preact).astype(BF16), "y"), act_grad, preact)
     )
-    far_act = other_core(my_act)
-    down_term = loss_scale * (
-        contract(my_act, my_grad, ((0,), (0,))) + contract(far_act, far_grad, ((0,), (0,)))
-    )
-    down_term = down_term.astype(BF16)
+    far = contract(act, far_grad, ((0,), (0,))).astype(BF16)
+    down_term = contract(act, my_grad, ((0,), (0,))) + other_core(far).astype(F32)
+    down_term = (loss_scale * down_term).astype(BF16)
     down_piece = scatter_sum(down_term, "l").astype(BF16)
 
     hidden_grad = (act_grad * gelu_slope(preact)).astype(BF16)
-    my_hidden = gather(after(hidden_grad, down_term), "y")
-    far_hidden = other_core(my_hidden)
-    up_term = loss_scale * (
-        contract(my_input, my_hidden, ((0,), (0,))) + contract(far_input, far_hidden, ((0,), (0,)))
-    )
-    up_piece = scatter_sum(up_term.astype(BF16), "l").astype(BF16)
+    hidden = gather(after(hidden_grad, down_term), "y")
+    far = contract(every_input[:, features:], hidden, ((0,), (0,))).astype(BF16)
+    up_term = contract(every_input[:, :features], hidden, ((0,), (0,))) + other_core(far).astype(F32)
+    up_term = (loss_scale * up_term).astype(BF16)
+    up_piece = scatter_sum(up_term, "l").astype(BF16)
 
     piece = jnp.concatenate([up_piece[:, :features], up_piece[:, features:], down_piece], axis=0)
     pieces = lax.all_gather(piece, ("e", "l"), axis_index_groups=[FOLDED])
     up_grad, down_grad = place(pieces)
-    my_act, my_hidden, far_act, far_hidden, _ = lax.optimization_barrier(
-        (my_act, my_hidden, far_act, far_hidden, piece)
+
+    act, hidden, _ = lax.optimization_barrier((act, hidden, up_term))
+    total = jnp.concatenate(
+        [
+            contract(act, down_half, ((1,), (0,))).astype(BF16),
+            contract(act, down_far, ((1,), (0,))).astype(BF16),
+            contract(hidden, up_both, ((1,), (1,))).astype(BF16),
+        ],
+        axis=1,
     )
-
-    blocks = 16
-    sides = []
-    for act, hidden in ((my_act, my_hidden), (far_act, far_hidden)):
-        side = jnp.concatenate(
-            [
-                contract(act, down_half, ((1,), (0,))).astype(BF16),
-                contract(hidden, up_half, ((1,), (1,))).astype(BF16),
-            ],
-            axis=1,
-        )
-        sides.append(side.reshape(blocks, own // 2, 2 * features))
-    total = jnp.stack(sides, axis=1).reshape(blocks * own, 2 * features)
-    total = scatter_sum(total, "x").astype(BF16)
+    total = scatter_sum(after(total, piece), "x").astype(BF16)
     total = scatter_sum(total, ("h", "e")).astype(BF16)
-    swapped = jnp.concatenate([total[own // 2 :], total[: own // 2]], axis=0)
-    total = jnp.where(core == 0, total, swapped)
+    kept = jnp.concatenate([total[:, :features], total[:, 2 * features : 3 * features]], axis=1)
+    received = other_core(
+        jnp.concatenate([total[:, features : 2 * features], total[:, 3 * features :]], axis=1)
+    )
+    total = jnp.where(
+        side == 0,
+        jnp.concatenate([kept, received], axis=0),
+        jnp.concatenate([received, kept], axis=0),
+    )
     return total[:, :features], total[:, features:], up_grad, down_grad
 
 

time: 255 us -> 248 us (0.973)
  starting transfers between devices: 25.4 us -> 31 us
  other arithmetic: 7.83 us -> 3.38 us
  waiting for transfers between devices: 33 us -> 29.6 us
  local copies, waits for them, and re-layouts: 6.49 us -> 3.19 us
    ppermute x4 -> x6, starting transfers between devices: 7.66 us -> 11.6 us  [other_core(): return lax.ppermute(values, 'k', [(0, 1), (1, 0)])]
    unnamed x23 -> x21, local copies, waits for them, and re-layouts: 4.13 us -> 0.95 us
    ppermute x4 -> x6, waiting for transfers between devices: 7.9 us -> 6.18 us  [other_core(): return lax.ppermute(values, 'k', [(0, 1), (1, 0)])]
    dot_general x12 -> x10, matrix products: 12.1 us -> 13.1 us  [contract(): lax.dot_general(left, right, (dims, ((), ())), preferred_element_type=F32)]
  transfers between devices with their start and end apart: 9 -> 11, of which waited for: 6 -> 6; matrix products, arithmetic and copies ran while one was open for 5% -> 4% of each run, Pallas kernels for 0% -> 0%
where the time goes in v4:
time: 248 us; the launch traced here: 247 us
  blocking collectives  149 us (60%)
  starting transfers between devices  31 us (12%)
  waiting for transfers between devices  29.6 us (12%)
  between operations  14.4 us (6%)
  matrix products  13.1 us (5%)
  other arithmetic  3.38 us (1%)
  Pallas kernels  3.3 us (1%)
  local copies, waits for them, and re-layouts  3.19 us (1%)
    all_gather x5, blocking collectives, gather(): return lax.all_gather(values, axis, axis=0, tiled=True)  90.9 us
    all_to_all x2, blocking collectives, scatter_sum(): parts = lax.all_to_all(values, axis, 0, 0, tiled=True)  57.9 us
    all_to_all x4, starting transfers between devices, scatter_sum(): parts = lax.all_to_all(values, axis, 0, 0, tiled=True)  19.4 us
    all_to_all x4, waiting for transfers between devices, scatter_sum(): parts = lax.all_to_all(values, axis, 0, 0, tiled=True)  16.1 us
    dot_general x10, matrix products, contract(): lax.dot_general(left, right, (dims, ((), ())), preferred_element_type=F32)  13.1 us
    ppermute x6, starting transfers between devices, other_core(): return lax.ppermute(values, 'k', [(0, 1), (1, 0)])  11.6 us
    all_gather x1, waiting for transfers between devices, on_device(): pieces = lax.all_gather(piece, ('e', 'l'), axis_index_groups=[FOLDED])  7.27 us
    ppermute x6, waiting for transfers between devices, other_core(): return lax.ppermute(values, 'k', [(0, 1), (1, 0)])  6.18 us
  transfers between devices with their start and end apart: 11, of which 6 were waited for; matrix products, arithmetic and copies ran while one was open for 4% of the time, Pallas kernels for 0%

profile of v4, /device:TPU:6, one launch (start us, length us, event | category | flops | bytes accessed | tf_op | source)
XLA Modules:
  0.0 246.7 jit_solution(702580670176292934)
XLA Ops:
  7.2 1.0 constant_dynamic-slice_fusion.2
  8.2 1.9 collective-permute-start
  10.3 1.0 collective-permute-done
  11.3 2.1 collective-permute-start.1
  13.4 29.0 %all_gather.21 = bf16[128,1536]{1,0:T(8,128)(2,1)S(1)} all-gather(bf16[32,1536]{1,0:T(8,128)(2,1)S(1)} %pad_maximum_fusion.2), channel_id=1, replica_groups=mesh['x'=4,'h'=2,'y'=4,'k'=2,'e'=2,'l'=4] {'h','e'}, dimensions={0}, use_global_device_ids=true | all-gather | bytes 491520 | tf_op jit(solution)/shard_map/all_gather | solution.py:38
  42.5 14.3 %all_gather.22 = bf16[512,768]{1,0:T(8,128)(2,1)S(1)} all-gather(bf16[128,768]{1,0:T(8,128)(2,1)S(1)} %get-tuple-element.33), channel_id=1, replica_groups=mesh['x'=4,'h'=2,'y'=4,'k'=2,'e'=2,'l'=4] {'x'}, dimensions={0}, use_global_device_ids=true | all-gather | bytes 983040 | tf_op jit(solution)/shard_map/all_gather | solution.py:38
  56.8 1.7 convolution_convert_fusion.1
  58.5 4.5 %all-to-all-start = ((bf16[4,128,768]{2,1,0:T(8,128)(2,1)}), bf16[4,128,768]{2,1,0:T(8,128)(2,1)S(1)}, u32[]{:S(2)}, u32[]{:S(2)}) async-start(bf16[4,128,768]{2,1,0:T(8,128)(2,1)} %bitcast), calls=%async_computation | async-start | bytes 1572864 | tf_op jit(solution)/shard_map/all_to_all | solution.py:32
  63.0 1.9 collective-permute-start.2
  64.9 14.5 %all_gather.24 = bf16[512,768]{1,0:T(8,128)(2,1)S(1)} all-gather(bf16[128,768]{1,0:T(8,128)(2,1)S(1)} %get-tuple-element.21), channel_id=1, replica_groups=mesh['x'=4,'h'=2,'y'=4,'k'=2,'e'=2,'l'=4] {'x'}, dimensions={0}, use_global_device_ids=true | all-gather | bytes 983040 | tf_op jit(solution)/shard_map/all_gather | solution.py:38
  79.4 0.1 convert_reduce_fusion.1
  79.6 1.7 fusion.12
  81.2 1.5 add_convert_fusion
  82.7 4.8 %all-to-all-start.1 = ((bf16[4,128,768]{2,1,0:T(8,128)(2,1)}), bf16[4,128,768]{2,1,0:T(8,128)(2,1)S(1)}, u32[]{:S(2)}, u32[]{:S(2)}) async-start(bf16[4,128,768]{2,1,0:T(8,128)(2,1)} %bitcast.1), calls=%async_computation.1 | async-start | bytes 1572864 | tf_op jit(solution)/shard_map/all_to_all | solution.py:32
  87.5 0.8 convert_element_type.97
  88.4 19.4 %all_gather.23 = bf16[512,768]{1,0:T(8,128)(2,1)} all-gather(bf16[128,768]{1,0:T(8,128)(2,1)S(1)} %multiply_convert_fusion.2), channel_id=1, replica_groups=mesh['x'=4,'h'=2,'y'=4,'k'=2,'e'=2,'l'=4] {'y'}, dimensions={0}, use_global_device_ids=true | all-gather | bytes 983040 | tf_op jit(solution)/shard_map/all_gather | solution.py:38
  107.8 0.9 convert_reduce_fusion
  108.6 0.4 copy-done.3
  109.0 0.6 convolution_convert_fusion.3
  109.6 1.9 collective-permute-start.3
  111.6 2.0 collective-permute-done.3
  113.5 1.4 multiply_convert_fusion.1
  115.0 4.7 %all-to-all-start.3 = ((bf16[4,192,384]{2,1,0:T(8,128)(2,1)}), bf16[4,192,384]{2,1,0:T(8,128)(2,1)S(1)}, u32[]{:S(2)}, u32[]{:S(2)}) async-start(bf16[4,192,384]{2,1,0:T(8,128)(2,1)} %bitcast.24), calls=%async_computation.3 | async-start | bytes 1179648 | tf_op jit(solution)/shard_map/all_to_all | solution.py:32
  119.6 0.2 fusion.5
  119.8 13.7 %all_gather.25 = bf16[512,768]{1,0:T(8,128)(2,1)S(1)} all-gather(bf16[128,768]{1,0:T(8,128)(2,1)S(1)} %fusion.5), channel_id=1, replica_groups=mesh['x'=4,'h'=2,'y'=4,'k'=2,'e'=2,'l'=4] {'y'}, dimensions={0}, use_global_device_ids=true | all-gather | bytes 983040 | tf_op jit(solution)/shard_map/all_gather | solution.py:38
  133.5 0.5 convolution_convert_fusion.2
  134.0 1.9 collective-permute-start.4
  135.9 2.0 collective-permute-done.4
  137.9 1.3 multiply_convert_fusion
  139.2 5.4 %all-to-all-start.2 = ((bf16[4,96,768]{2,1,0:T(8,128)(2,1)}), bf16[4,96,768]{2,1,0:T(8,128)(2,1)S(1)}, u32[]{:S(2)}, u32[]{:S(2)}) async-start(bf16[4,96,768]{2,1,0:T(8,128)(2,1)} %bitcast.2), calls=%async_computation.2 | async-start | bytes 1179648 | tf_op jit(solution)/shard_map/all_to_all | solution.py:32
  144.8 16.1 %all-to-all-done.2 = bf16[4,96,768]{2,1,0:T(8,128)(2,1)S(1)} async-done(((bf16[4,96,768]{2,1,0:T(8,128)(2,1)}), bf16[4,96,768]{2,1,0:T(8,128)(2,1)S(1)}, u32[]{:S(2)}, u32[]{:S(2)}) %all-to-all-start.2) | async-done | bytes 589856 | tf_op jit(solution)/shard_map/all_to_all | solution.py:32
  160.9 0.1 reduce_sum.68
  161.0 0.7 pad_maximum_fusion.1
  161.8 0.4 copy-done.4
  162.2 1.6 convolution_convert_fusion.4
  163.8 0.2 copy.11
  164.0 0.5 convolution_convert_fusion.5
  164.5 0.2 copy.10
  164.7 2.3 convolution_convert_fusion
  167.1 0.1 pad_maximum_fusion
  167.2 22.2 %all_to_all.54 = bf16[4,128,1536]{2,1,0:T(8,128)(2,1)S(1)} all-to-all(bf16[4,128,1536]{2,1,0:T(8,128)(2,1)S(1)} %bitcast.21), channel_id=1, replica_groups=mesh['x'=4,'h'=2,'y'=4,'k'=2,'e'=2,'l'=4] {'x'}, dimensions={0} | all-to-all | bytes 3145728 | tf_op jit(solution)/shard_map/all_to_all | solution.py:32
  189.4 0.3 reduce_sum.70
  189.7 35.7 %all_to_all.55 = bf16[4,32,1536]{2,1,0:T(8,128)(2,1)S(1)} all-to-all(bf16[4,32,1536]{2,1,0:T(8,128)(2,1)S(1)} %bitcast.23), channel_id=1, replica_groups=mesh['x'=4,'h'=2,'y'=4,'k'=2,'e'=2,'l'=4] {'h','e'}, dimensions={0} | all-to-all | bytes 786432 | tf_op jit(solution)/shard_map/all_to_all | solution.py:32
  225.4 1.9 collective-permute-start.5
  227.4 1.2 collective-permute-done.5
  228.6 0.6 fusion.21
  229.2 7.3 %all-gather.3.cloned.1.call-done = bf16[3072,384]{1,0:T(8,128)(2,1)} async-done(((bf16[384,384]{1,0:T(8,128)(2,1)}), bf16[3072,384]{1,0:T(8,128)(2,1)}) %all-gather.3.cloned.1.call-update) | async-done | bytes 2359312 | tf_op jit(solution)/shard_map/all_gather | solution.py:151
  236.5 3.3 %shard_map.75 = (bf16[384,1536]{1,0:T(8,128)(2,1)}, bf16[1536,384]{1,0:T(8,128)(2,1)}) custom-call(bf16[8,384,384]{2,1,0:T(8,128)(2,1)} %bitcast.22), custom_call_target="tpu_custom_call" | custom-call | tf_op jit(solution)/shard_map/pallas_call | solution.py:79
  (40 shorter events, 0.6 us)
Async XLA Ops:
  7.2 2.9 %copy-start = (bf16[384,1536]{1,0:T(8,128)(2,1)S(1)}, bf16[384,1536]{1,0:T(8,128)(2,1)}, u32[]{:S(2)}) copy-start(bf16[384,1536]{1,0:T(8,128)(2,1)} %param.5) | copy-start | bytes 3538948
  7.2 3.0 %copy-start.8 = (bf16[1536,384]{1,0:T(8,128)(2,1)S(1)}, bf16[1536,384]{1,0:T(8,128)(2,1)}, u32[]{:S(2)}) copy-start(bf16[1536,384]{1,0:T(8,128)(2,1)} %param.6) | copy-start | bytes 3538948
  8.2 3.1 %collective-permute-start = (bf16[32,768]{1,0:T(8,128)(2,1)S(1)}, bf16[32,768]{1,0:T(8,128)(2,1)S(1)}, u32[]{:S(2)}, u32[]{:S(2)}) collective-permute-start(bf16[32,768]{1,0:T(8,128)(2,1)S(1)} %pad_maximum_fusion.3), channel_id=1, source_target_pairs={{0,8},{8,0},{1,9},{9,1},{2,10},{10,2},{3,11},{11,3},{4,12},{12,4},... | collective-permute-start | bytes 147464 | tf_op jit(solution)/shard_map/ppermute | solution.py:42
  11.3 45.5 %collective-permute-start.1 = (bf16[384,768]{1,0:T(8,128)(2,1)S(1)}, bf16[384,768]{1,0:T(8,128)(2,1)S(1)}, u32[]{:S(2)}, u32[]{:S(2)}) collective-permute-start(bf16[384,768]{1,0:T(8,128)(2,1)S(1)} %constant_dynamic-slice_fusion.1), channel_id=1, source_target_pairs={{0,8},{8,0},{1,9},{9,1},{2,10},{10,2},{3,11},{11,3},{4,12},{12,4},... | collective-permute-start | bytes 1769480 | tf_op jit(solution)/shard_map/ppermute | solution.py:42
  56.8 1.7 copy-start.5
  56.8 1.7 copy-start.9
  58.5 20.9 %all-to-all-start = ((bf16[4,128,768]{2,1,0:T(8,128)(2,1)}), bf16[4,128,768]{2,1,0:T(8,128)(2,1)S(1)}, u32[]{:S(2)}, u32[]{:S(2)}) async-start(bf16[4,128,768]{2,1,0:T(8,128)(2,1)} %bitcast), calls=%async_computation | async-start | bytes 1572864 | tf_op jit(solution)/shard_map/all_to_all | solution.py:32
  63.0 16.6 %collective-permute-start.2 = (bf16[768,384]{1,0:T(8,128)(2,1)S(1)}, bf16[768,384]{1,0:T(8,128)(2,1)}, u32[]{:S(2)}, u32[]{:S(2)}) collective-permute-start(bf16[768,384]{1,0:T(8,128)(2,1)S(1)} %constant_dynamic-slice_fusion), channel_id=1, source_target_pairs={{0,8},{8,0},{1,9},{9,1},{2,10},{10,2},{3,11},{11,3},{4,12},{12,4},... | collective-permute-start | bytes 1769480 | tf_op jit(solution)/shard_map/ppermute | solution.py:42
  82.7 25.0 %all-to-all-start.1 = ((bf16[4,128,768]{2,1,0:T(8,128)(2,1)}), bf16[4,128,768]{2,1,0:T(8,128)(2,1)S(1)}, u32[]{:S(2)}, u32[]{:S(2)}) async-start(bf16[4,128,768]{2,1,0:T(8,128)(2,1)} %bitcast.1), calls=%async_computation.1 | async-start | bytes 1572864 | tf_op jit(solution)/shard_map/all_to_all | solution.py:32
  107.7 1.3 copy-start.3
  109.6 3.9 %collective-permute-start.3 = (bf16[768,384]{1,0:T(8,128)(2,1)S(1)}, bf16[768,384]{1,0:T(8,128)(2,1)S(1)}, u32[]{:S(2)}, u32[]{:S(2)}) collective-permute-start(bf16[768,384]{1,0:T(8,128)(2,1)S(1)} %convolution_convert_fusion.3), channel_id=1, source_target_pairs={{0,8},{8,0},{1,9},{9,1},{2,10},{10,2},{3,11},{11,3},{4,12},{12,4},... | collective-permute-start | bytes 1769480 | tf_op jit(solution)/shard_map/ppermute | solution.py:42
  115.0 4.7 %copy-start.1 = (f32[128,768]{1,0:T(8,128)S(1)}, f32[128,768]{1,0:T(8,128)}, u32[]{:S(2)}) copy-start(f32[128,768]{1,0:T(8,128)} %convert_element_type.97) | copy-start | bytes 1179652
  115.0 4.7 %copy-start.2 = (f32[128,768]{1,0:T(8,128)S(1)}, f32[128,768]{1,0:T(8,128)}, u32[]{:S(2)}) copy-start(f32[128,768]{1,0:T(8,128)} %convert_reduce_fusion) | copy-start | bytes 1179652
  115.0 24.3 %all-to-all-start.3 = ((bf16[4,192,384]{2,1,0:T(8,128)(2,1)}), bf16[4,192,384]{2,1,0:T(8,128)(2,1)S(1)}, u32[]{:S(2)}, u32[]{:S(2)}) async-start(bf16[4,192,384]{2,1,0:T(8,128)(2,1)} %bitcast.24), calls=%async_computation.3 | async-start | bytes 1179648 | tf_op jit(solution)/shard_map/all_to_all | solution.py:32
  119.6 13.9 %copy-start.6 = (bf16[512,768]{1,0:T(8,128)(2,1)S(1)}, bf16[512,768]{1,0:T(8,128)(2,1)}, u32[]{:S(2)}) copy-start(bf16[512,768]{1,0:T(8,128)(2,1)} %copy-done.5) | copy-start | bytes 2359300
  133.5 4.4 %copy-start.7 = (bf16[512,768]{1,0:T(8,128)(2,1)}, bf16[512,768]{1,0:T(8,128)(2,1)S(1)}, u32[]{:S(2)}) copy-start(bf16[512,768]{1,0:T(8,128)(2,1)S(1)} %all_gather.25) | copy-start | bytes 2359300
  134.0 3.9 %collective-permute-start.4 = (bf16[384,768]{1,0:T(8,128)(2,1)S(1)}, bf16[384,768]{1,0:T(8,128)(2,1)S(1)}, u32[]{:S(2)}, u32[]{:S(2)}) collective-permute-start(bf16[384,768]{1,0:T(8,128)(2,1)S(1)} %convolution_convert_fusion.2), channel_id=1, source_target_pairs={{0,8},{8,0},{1,9},{9,1},{2,10},{10,2},{3,11},{11,3},{4,12},{12,4},... | collective-permute-start | bytes 1769480 | tf_op jit(solution)/shard_map/ppermute | solution.py:42
  139.2 21.6 %all-to-all-start.2 = ((bf16[4,96,768]{2,1,0:T(8,128)(2,1)}), bf16[4,96,768]{2,1,0:T(8,128)(2,1)S(1)}, u32[]{:S(2)}, u32[]{:S(2)}) async-start(bf16[4,96,768]{2,1,0:T(8,128)(2,1)} %bitcast.2), calls=%async_computation.2 | async-start | bytes 1179648 | tf_op jit(solution)/shard_map/all_to_all | solution.py:32
  144.7 91.8 %all-gather.3.cloned.1.call-start = ((), (), s32[]{:S(2)}) async-start(), calls=%async_computation.6 | async-start | bytes 2654208 | tf_op jit(solution)/shard_map/all_gather | solution.py:151
  161.0 1.2 copy-start.4
  225.4 3.1 %collective-permute-start.5 = (bf16[32,768]{1,0:T(8,128)(2,1)S(1)}, bf16[32,768]{1,0:T(8,128)(2,1)S(1)}, u32[]{:S(2)}, u32[]{:S(2)}) collective-permute-start(bf16[32,768]{1,0:T(8,128)(2,1)S(1)} %pad_maximum_fusion.4), channel_id=1, source_target_pairs={{0,8},{8,0},{1,9},{9,1},{2,10},{10,2},{3,11},{11,3},{4,12},{12,4},... | collective-permute-start | bytes 147464 | tf_op jit(solution)/shard_map/ppermute | solution.py:42
Sparse Core Ops, SparseCore 0:
  161.9 74.5 all-gather.2

commit v5 on v4

--- a/solution.py
+++ b/solution.py
@@ -8,6 +8,7 @@
 
 F32 = jnp.float32
 BF16 = jnp.bfloat16
+F16 = jnp.float16
 
 FOLDED = [0, 2, 4, 6, 7, 5, 3, 1]
 
@@ -44,6 +45,55 @@
 
 def after(values, earlier):
     return lax.optimization_barrier((values, earlier))[0]
+
+
+def feature_kernel(act, hidden, down, up, *rest):
+    out = rest[-1]
+    features = down.shape[1]
+    rows = act.shape[0] // 4
+    for block in range(4):
+        here = pl.ds(block * rows, rows)
+        values = (
+            contract(act[here], down[...], ((1,), (0,))).astype(BF16),
+            contract(hidden[here], up[...], ((1,), (1,))).astype(BF16),
+        )
+        for side, value in enumerate(values):
+            columns = pl.ds(side * features, features)
+            if len(rest) == 1:
+                out[here, columns] = value
+            else:
+                out[block, pl.ds(0, rows), columns] = value
+        if len(rest) == 2:
+            out[block, pl.ds(rows, rows)] = rest[0][here]
+
+
+def feature_values(act, hidden, down, up, *more):
+    rows, depth = act.shape
+    features = down.shape[1]
+    shape = (4, rows // 2, 2 * features) if more else (rows, 2 * features)
+    return pl.pallas_call(
+        feature_kernel,
+        out_shape=jax.ShapeDtypeStruct(shape, BF16),
+        cost_estimate=pl.CostEstimate(
+            flops=4 * rows * depth * features,
+            bytes_accessed=4 * rows * depth + 8 * depth * features,
+            transcendentals=0,
+        ),
+    )(act, hidden, down, up, *more)
+
+
+def pack(piece):
+    wide = piece.astype(F32)
+    top = jnp.maximum(jnp.max(jnp.abs(wide)), 1e-37)
+    power = jnp.clip(14.0 - jnp.ceil(jnp.log2(top)), -20.0, 120.0)
+    scaled = (wide * jnp.exp2(power)).astype(F16)
+    return jnp.concatenate([scaled, jnp.full((16, piece.shape[1]), power).astype(F16)], axis=0)
+
+
+def unpack(packed):
+    rows = packed.shape[1] - 16
+    power = packed[:, rows:, :1].astype(F32)[:, :1]
+    return (packed[:, :rows].astype(F32) * jnp.exp2(-power)).astype(BF16)
 
 
 def place_kernel(pieces, up, down, sems):
@@ -108,7 +158,8 @@
 
     kept, received = half_rows(side), other_core(half_rows(1 - side))
     up_half, down_half = after((up_half, down_half), received)
-    up_both = jnp.concatenate([up_half, other_core(up_half)], axis=0)
+    up_far = other_core(up_half)
+    up_both = jnp.concatenate([up_half, up_far], axis=0)
     down_far = other_core(down_half)
     rows = jnp.concatenate(
         [
@@ -145,32 +196,25 @@
     far = contract(every_input[:, features:], hidden, ((0,), (0,))).astype(BF16)
     up_term = contract(every_input[:, :features], hidden, ((0,), (0,))) + other_core(far).astype(F32)
     up_term = (loss_scale * up_term).astype(BF16)
-    up_piece = scatter_sum(up_term, "l").astype(BF16)
-
+
+    act, hidden = after((act, hidden), up_term)
+    far = other_core(feature_values(act, hidden, down_far, up_far))
+    total = feature_values(act, hidden, down_half, up_half, far)
+    total = total.reshape(16 * own, 2 * features)
+    up_parts = after(lax.all_to_all(up_term, "l", 0, 0, tiled=True), total)
+    up_piece = jnp.sum(up_parts.reshape(4, -1, half).astype(F32), axis=0).astype(BF16)
     piece = jnp.concatenate([up_piece[:, :features], up_piece[:, features:], down_piece], axis=0)
-    pieces = lax.all_gather(piece, ("e", "l"), axis_index_groups=[FOLDED])
-    up_grad, down_grad = place(pieces)
-
-    act, hidden, _ = lax.optimization_barrier((act, hidden, up_term))
-    total = jnp.concatenate(
-        [
-            contract(act, down_half, ((1,), (0,))).astype(BF16),
-            contract(act, down_far, ((1,), (0,))).astype(BF16),
-            contract(hidden, up_both, ((1,), (1,))).astype(BF16),
-        ],
-        axis=1,
-    )
-    total = scatter_sum(after(total, piece), "x").astype(BF16)
-    total = scatter_sum(total, ("h", "e")).astype(BF16)
-    kept = jnp.concatenate([total[:, :features], total[:, 2 * features : 3 * features]], axis=1)
-    received = other_core(
-        jnp.concatenate([total[:, features : 2 * features], total[:, 3 * features :]], axis=1)
-    )
-    total = jnp.where(
-        side == 0,
-        jnp.concatenate([kept, received], axis=0),
-        jnp.concatenate([received, kept], axis=0),
-    )
+    packed = pack(piece)
+    pieces = lax.all_gather(packed, ("e", "l"), axis_index_groups=[FOLDED])
+    total, pieces = lax.optimization_barrier(
+        (scatter_sum(after(total, packed), "x").astype(BF16), pieces)
+    )
+    up_grad, down_grad = place(unpack(pieces))
+    total = total.reshape(2, 4, own // 2, 2 * features).transpose(1, 0, 2, 3)
+    total = scatter_sum(total.reshape(4 * own, 2 * features), ("h", "e")).astype(BF16)
+    total = after(total, (up_grad, down_grad))
+    swapped = jnp.concatenate([total[own // 2 :], total[: own // 2]], axis=0)
+    total = jnp.where(side == 0, total, swapped)
     return total[:, :features], total[:, features:], up_grad, down_grad
 
 

time: 248 us -> 245 us (0.988)
  the two profiles are of different devices: /device:TPU:6 before, /device:TPU:10 now
where the time goes in v5:
time: 245 us; the launch traced here: 244 us
  blocking collectives  137 us (56%)
  starting transfers between devices  42.9 us (18%)
  waiting for transfers between devices  27.3 us (11%)
  Pallas kernels  11.5 us (5%)
  other arithmetic  11 us (4%)
  matrix products  8.65 us (4%)
  local copies, waits for them, and re-layouts  3.53 us (1%)
    all_gather x5, blocking collectives, gather(): return lax.all_gather(values, axis, axis=0, tiled=True)  88.4 us
    all_gather x1, blocking collectives, on_device(): pieces = lax.all_gather(packed, ('e', 'l'), axis_index_groups=[FOLDED])  48.8 us
    all_to_all x5, starting transfers between devices, scatter_sum(): parts = lax.all_to_all(values, axis, 0, 0, tiled=True)  25.7 us
    all_to_all x5, waiting for transfers between devices, scatter_sum(): parts = lax.all_to_all(values, axis, 0, 0, tiled=True)  17.2 us
    ppermute x6, starting transfers between devices, other_core(): return lax.ppermute(values, 'k', [(0, 1), (1, 0)])  11.6 us
    dot_general x7, matrix products, contract(): lax.dot_general(left, right, (dims, ((), ())), preferred_element_type=F32)  8.65 us
    pallas_call x2, Pallas kernels, feature_values(): pl.pallas_call(feature_kernel, out_shape=jax.ShapeDtypeStruct(shape, BF16...  8.15 us
    ppermute x6, waiting for transfers between devices, other_core(): return lax.ppermute(values, 'k', [(0, 1), (1, 0)])  7.43 us
  transfers between devices with their start and end apart: 12, of which 6 were waited for; matrix products, arithmetic and copies ran while one was open for 4% of the time, Pallas kernels for 5%

profile of v5, /device:TPU:10, one launch (start us, length us, event | category | flops | bytes accessed | tf_op | source)
XLA Modules:
  0.0 243.8 jit_solution(14236594731842933670)
XLA Ops:
  0.7 1.0 constant_dynamic-slice_fusion.2
  1.6 1.9 collective-permute-start
  3.7 1.0 collective-permute-done
  4.8 2.1 collective-permute-start.1
  6.9 29.0 %all_gather.21 = bf16[128,1536]{1,0:T(8,128)(2,1)S(1)} all-gather(bf16[32,1536]{1,0:T(8,128)(2,1)S(1)} %pad_maximum_fusion.1), channel_id=1, replica_groups=mesh['x'=4,'h'=2,'y'=4,'k'=2,'e'=2,'l'=4] {'h','e'}, dimensions={0}, use_global_device_ids=true | all-gather | bytes 491520 | tf_op jit(solution)/shard_map/all_gather | solution.py:39
  35.9 14.4 %all_gather.22 = bf16[512,768]{1,0:T(8,128)(2,1)S(1)} all-gather(bf16[128,768]{1,0:T(8,128)(2,1)S(1)} %get-tuple-element.41), channel_id=1, replica_groups=mesh['x'=4,'h'=2,'y'=4,'k'=2,'e'=2,'l'=4] {'x'}, dimensions={0}, use_global_device_ids=true | all-gather | bytes 983040 | tf_op jit(solution)/shard_map/all_gather | solution.py:39
  50.3 1.7 convolution_convert_fusion
  51.9 4.9 %all-to-all-start = ((bf16[4,128,768]{2,1,0:T(8,128)(2,1)}), bf16[4,128,768]{2,1,0:T(8,128)(2,1)S(1)}, u32[]{:S(2)}, u32[]{:S(2)}) async-start(bf16[4,128,768]{2,1,0:T(8,128)(2,1)} %bitcast), calls=%async_computation | async-start | bytes 1572864 | tf_op jit(solution)/shard_map/all_to_all | solution.py:33
  56.9 1.9 collective-permute-start.2
  58.8 14.5 %all_gather.24 = bf16[512,768]{1,0:T(8,128)(2,1)S(1)} all-gather(bf16[128,768]{1,0:T(8,128)(2,1)S(1)} %get-tuple-element.25), channel_id=1, replica_groups=mesh['x'=4,'h'=2,'y'=4,'k'=2,'e'=2,'l'=4] {'x'}, dimensions={0}, use_global_device_ids=true | all-gather | bytes 983040 | tf_op jit(solution)/shard_map/all_gather | solution.py:39
  73.3 0.1 convert_reduce_fusion.1
  73.4 1.7 fusion.17
  75.1 1.5 add_convert_fusion
  76.6 4.8 %all-to-all-start.1 = ((bf16[4,128,768]{2,1,0:T(8,128)(2,1)}), bf16[4,128,768]{2,1,0:T(8,128)(2,1)}, u32[]{:S(2)}, u32[]{:S(2)}) async-start(bf16[4,128,768]{2,1,0:T(8,128)(2,1)} %bitcast.1), calls=%async_computation.1 | async-start | bytes 1572864 | tf_op jit(solution)/shard_map/all_to_all | solution.py:33
  81.4 0.8 convert_element_type.113
  82.3 17.2 %all_gather.23.act = bf16[512,768]{1,0:T(8,128)(2,1)S(1)} all-gather(bf16[128,768]{1,0:T(8,128)(2,1)S(1)} %multiply_convert_fusion.3), channel_id=1, replica_groups=mesh['x'=4,'h'=2,'y'=4,'k'=2,'e'=2,'l'=4] {'y'}, dimensions={0}, use_global_device_ids=true | all-gather | bytes 983040 | tf_op jit(solution)/shard_map/all_gather | solution.py:39
  99.5 2.3 convert_reduce_fusion
  101.8 0.6 convolution_convert_fusion.2
  102.4 1.9 collective-permute-start.3
  104.3 2.0 collective-permute-done.3
  106.3 1.4 multiply_convert_fusion.2
  107.7 4.8 %all-to-all-start.3 = ((bf16[4,192,384]{2,1,0:T(8,128)(2,1)}), bf16[4,192,384]{2,1,0:T(8,128)(2,1)S(1)}, u32[]{:S(2)}, u32[]{:S(2)}) async-start(bf16[4,192,384]{2,1,0:T(8,128)(2,1)} %bitcast.24), calls=%async_computation.3 | async-start | bytes 1179648 | tf_op jit(solution)/shard_map/all_to_all | solution.py:33
  112.5 1.3 fusion.10
  113.8 13.3 %all_gather.25.hidden = bf16[512,768]{1,0:T(8,128)(2,1)S(1)} all-gather(bf16[128,768]{1,0:T(8,128)(2,1)S(1)} %fusion.10), channel_id=1, replica_groups=mesh['x'=4,'h'=2,'y'=4,'k'=2,'e'=2,'l'=4] {'y'}, dimensions={0}, use_global_device_ids=true | all-gather | bytes 983040 | tf_op jit(solution)/shard_map/all_gather | solution.py:39
  127.1 0.5 convolution_convert_fusion.1
  127.6 1.9 collective-permute-start.4
  129.5 2.0 collective-permute-done.4
  131.5 1.3 multiply_convert_fusion.1
  132.9 5.6 %all-to-all-start.2 = ((bf16[4,96,768]{2,1,0:T(8,128)(2,1)}), bf16[4,96,768]{2,1,0:T(8,128)(2,1)S(1)}, u32[]{:S(2)}, u32[]{:S(2)}) async-start(bf16[4,96,768]{2,1,0:T(8,128)(2,1)} %bitcast.23), calls=%async_computation.2 | async-start | bytes 1179648 | tf_op jit(solution)/shard_map/all_to_all | solution.py:204
  138.4 3.8 %shard_map.75 = bf16[512,768]{1,0:T(8,128)(2,1)} custom-call(bf16[512,768]{1,0:T(8,128)(2,1)} %copy-done.1, bf16[512,768]{1,0:T(8,128)(2,1)} %copy-done.2, bf16[768,384]{1,0:T(8,128)(2,1)} %collective-permute-done.2.down, bf16[384,768]{1,0:T(8,128)(2,1)} %copy-done.8), custom_call_target="tpu_custom_call" | custom-call | flops 603979776 | bytes 3932160 | tf_op jit(solution)/shard_map/pallas_call | solution.py:74
  142.3 1.9 collective-permute-start.5
  144.2 2.5 %collective-permute-done.5.rest_0_ = bf16[512,768]{1,0:T(8,128)(2,1)S(1)} collective-permute-done((bf16[512,768]{1,0:T(8,128)(2,1)}, bf16[512,768]{1,0:T(8,128)(2,1)S(1)}, u32[]{:S(2)}, u32[]{:S(2)}) %collective-permute-start.5) | collective-permute-done | bytes 786464 | tf_op jit(solution)/shard_map/ppermute | solution.py:43
  146.7 0.9 copy-done.5
  147.5 4.3 %shard_map.76 = bf16[4,256,768]{2,1,0:T(8,128)(2,1)} custom-call(bf16[512,768]{1,0:T(8,128)(2,1)} %copy-done.1, bf16[512,768]{1,0:T(8,128)(2,1)} %copy-done.2, bf16[768,384]{1,0:T(8,128)(2,1)} %copy-done.3, bf16[384,768]{1,0:T(8,128)(2,1)} %copy-done.4, bf16[512,768]{1,0:T(8,128)(2,1)} %copy-done.5), custom_call_target="tpu_custom_call" | custom-call | flops 603979776 | bytes 3932160 | tf_op jit(solution)/shard_map/pallas_call | solution.py:74
  151.9 0.1 reduce_sum.69
  152.0 2.7 %all-to-all-done.2 = bf16[4,96,768]{2,1,0:T(8,128)(2,1)S(1)} async-done(((bf16[4,96,768]{2,1,0:T(8,128)(2,1)}), bf16[4,96,768]{2,1,0:T(8,128)(2,1)S(1)}, u32[]{:S(2)}, u32[]{:S(2)}) %all-to-all-start.2) | async-done | bytes 589856 | tf_op jit(solution)/shard_map/all_to_all | solution.py:204
  154.6 0.1 reduce_sum.68
  154.8 0.6 fusion.3
  156.3 4.5 %all-to-all-start.4 = ((bf16[4,256,768]{2,1,0:T(8,128)(2,1)}), bf16[4,256,768]{2,1,0:T(8,128)(2,1)S(1)}, u32[]{:S(2)}, u32[]{:S(2)}) async-start(bf16[4,256,768]{2,1,0:T(8,128)(2,1)} %shard_map.76), calls=%async_computation.4 | async-start | bytes 3145728 | tf_op jit(solution)/shard_map/all_to_all | solution.py:33
  160.8 48.8 %all-gather.2 = f16[3200,384]{1,0:T(8,128)(2,1)} all-gather(f16[400,384]{1,0:T(8,128)(2,1)S(1)} %concatenate.22), channel_id=2, replica_groups={{0,2,4,6,7,5,3,1},{8,10,12,14,15,13,11,9},{16,18,20,22,23,21,19,17},{24..., dimensions={0}, use_global_device_ids=true | all-gather | bytes 2764800 | tf_op jit(solution)/shard_map/all_gather | solution.py:208
  209.6 0.4 reduce_sum.70
  210.1 0.8 copy.9
  210.8 6.7 %all-to-all-start.5 = ((bf16[4,64,768]{2,1,0:T(8,128)(2,1)}), bf16[4,64,768]{2,1,0:T(8,128)(2,1)S(1)}, u32[]{:S(2)}, u32[]{:S(2)}) async-start(bf16[4,64,768]{2,1,0:T(8,128)(2,1)} %bitcast.11), calls=%async_computation.5 | async-start | bytes 786432 | tf_op jit(solution)/shard_map/all_to_all | solution.py:33
  217.5 0.9 exponential_reduce_fusion
  218.4 4.2 %multiply_convert_fusion.pieces = bf16[8,384,384]{2,1,0:T(8,128)(2,1)} fusion(f32[8]{0:T(128)S(1)} %exponential_reduce_fusion, f16[8,400,384]{2,1,0:T(8,128)(2,1)} %bitcast.21), kind=kLoop, calls=%fused_computation | loop fusion | flops 3538944 | bytes 4718624 | tf_op jit(solution)/shard_map/convert_element_type | solution.py:96
  222.6 3.3 %shard_map.77 = (bf16[384,1536]{1,0:T(8,128)(2,1)}, bf16[1536,384]{1,0:T(8,128)(2,1)}) custom-call(bf16[8,384,384]{2,1,0:T(8,128)(2,1)} %multiply_convert_fusion.pieces), custom_call_target="tpu_custom_call" | custom-call | tf_op jit(solution)/shard_map/pallas_call | solution.py:129
  225.9 17.2 %all-to-all-done.5 = bf16[4,64,768]{2,1,0:T(8,128)(2,1)S(1)} async-done(((bf16[4,64,768]{2,1,0:T(8,128)(2,1)}), bf16[4,64,768]{2,1,0:T(8,128)(2,1)S(1)}, u32[]{:S(2)}, u32[]{:S(2)}) %all-to-all-start.5) | async-done | bytes 393248 | tf_op jit(solution)/shard_map/all_to_all | solution.py:33
  243.2 0.6 fusion.27
  (38 shorter events, 0.6 us)
Async XLA Ops:
  0.6 2.9 %copy-start = (bf16[1536,384]{1,0:T(8,128)(2,1)S(1)}, bf16[1536,384]{1,0:T(8,128)(2,1)}, u32[]{:S(2)}) copy-start(bf16[1536,384]{1,0:T(8,128)(2,1)} %param.6) | copy-start | bytes 3538948
  0.6 3.0 %copy-start.9 = (bf16[384,1536]{1,0:T(8,128)(2,1)S(1)}, bf16[384,1536]{1,0:T(8,128)(2,1)}, u32[]{:S(2)}) copy-start(bf16[384,1536]{1,0:T(8,128)(2,1)} %param.5) | copy-start | bytes 3538948
  1.6 3.1 %collective-permute-start = (bf16[32,768]{1,0:T(8,128)(2,1)S(1)}, bf16[32,768]{1,0:T(8,128)(2,1)S(1)}, u32[]{:S(2)}, u32[]{:S(2)}) collective-permute-start(bf16[32,768]{1,0:T(8,128)(2,1)S(1)} %pad_maximum_fusion.2), channel_id=1, source_target_pairs={{0,8},{8,0},{1,9},{9,1},{2,10},{10,2},{3,11},{11,3},{4,12},{12,4},... | collective-permute-start | bytes 147464 | tf_op jit(solution)/shard_map/ppermute | solution.py:43
  3.7 71.4 %copy-start.3 = (bf16[768,384]{1,0:T(8,128)(2,1)}, bf16[768,384]{1,0:T(8,128)(2,1)S(1)}, u32[]{:S(2)}) copy-start(bf16[768,384]{1,0:T(8,128)(2,1)S(1)} %constant_dynamic-slice_fusion.down) | copy-start | bytes 1769476
  3.7 48.2 %copy-start.4 = (bf16[384,768]{1,0:T(8,128)(2,1)}, bf16[384,768]{1,0:T(8,128)(2,1)S(1)}, u32[]{:S(2)}) copy-start(bf16[384,768]{1,0:T(8,128)(2,1)S(1)} %constant_dynamic-slice_fusion.1.up) | copy-start | bytes 1769476
  4.8 45.5 %collective-permute-start.1 = (bf16[384,768]{1,0:T(8,128)(2,1)S(1)}, bf16[384,768]{1,0:T(8,128)(2,1)S(1)}, u32[]{:S(2)}, u32[]{:S(2)}) collective-permute-start(bf16[384,768]{1,0:T(8,128)(2,1)S(1)} %constant_dynamic-slice_fusion.1.up), channel_id=1, source_target_pairs={{0,8},{8,0},{1,9},{9,1},{2,10},{10,2},{3,11},{11,3},{4,12},{12,4},... | collective-permute-start | bytes 1769480 | tf_op jit(solution)/shard_map/ppermute | solution.py:43
  50.3 1.7 copy-start.6
  50.3 1.7 copy-start.8
  51.9 21.4 %all-to-all-start = ((bf16[4,128,768]{2,1,0:T(8,128)(2,1)}), bf16[4,128,768]{2,1,0:T(8,128)(2,1)S(1)}, u32[]{:S(2)}, u32[]{:S(2)}) async-start(bf16[4,128,768]{2,1,0:T(8,128)(2,1)} %bitcast), calls=%async_computation | async-start | bytes 1572864 | tf_op jit(solution)/shard_map/all_to_all | solution.py:33
  56.9 16.6 %collective-permute-start.2 = (bf16[768,384]{1,0:T(8,128)(2,1)S(1)}, bf16[768,384]{1,0:T(8,128)(2,1)}, u32[]{:S(2)}, u32[]{:S(2)}) collective-permute-start(bf16[768,384]{1,0:T(8,128)(2,1)S(1)} %constant_dynamic-slice_fusion.down), channel_id=1, source_target_pairs={{0,8},{8,0},{1,9},{9,1},{2,10},{10,2},{3,11},{11,3},{4,12},{12,4},... | collective-permute-start | bytes 1769480 | tf_op jit(solution)/shard_map/ppermute | solution.py:43
  76.6 22.9 %all-to-all-start.1 = ((bf16[4,128,768]{2,1,0:T(8,128)(2,1)}), bf16[4,128,768]{2,1,0:T(8,128)(2,1)}, u32[]{:S(2)}, u32[]{:S(2)}) async-start(bf16[4,128,768]{2,1,0:T(8,128)(2,1)} %bitcast.1), calls=%async_computation.1 | async-start | bytes 1572864 | tf_op jit(solution)/shard_map/all_to_all | solution.py:33
  99.5 6.8 %copy-start.1 = (bf16[512,768]{1,0:T(8,128)(2,1)}, bf16[512,768]{1,0:T(8,128)(2,1)S(1)}, u32[]{:S(2)}) copy-start(bf16[512,768]{1,0:T(8,128)(2,1)S(1)} %all_gather.23.act) | copy-start | bytes 2359300
  102.4 3.9 %collective-permute-start.3 = (bf16[768,384]{1,0:T(8,128)(2,1)S(1)}, bf16[768,384]{1,0:T(8,128)(2,1)S(1)}, u32[]{:S(2)}, u32[]{:S(2)}) collective-permute-start(bf16[768,384]{1,0:T(8,128)(2,1)S(1)} %convolution_convert_fusion.2), channel_id=1, source_target_pairs={{0,8},{8,0},{1,9},{9,1},{2,10},{10,2},{3,11},{11,3},{4,12},{12,4},... | collective-permute-start | bytes 1769480 | tf_op jit(solution)/shard_map/ppermute | solution.py:43
  107.7 19.4 %copy-start.7 = (bf16[512,768]{1,0:T(8,128)(2,1)S(1)}, bf16[512,768]{1,0:T(8,128)(2,1)}, u32[]{:S(2)}) copy-start(bf16[512,768]{1,0:T(8,128)(2,1)} %copy-done.6) | copy-start | bytes 2359300
  107.7 25.2 %all-to-all-start.3 = ((bf16[4,192,384]{2,1,0:T(8,128)(2,1)}), bf16[4,192,384]{2,1,0:T(8,128)(2,1)S(1)}, u32[]{:S(2)}, u32[]{:S(2)}) async-start(bf16[4,192,384]{2,1,0:T(8,128)(2,1)} %bitcast.24), calls=%async_computation.3 | async-start | bytes 1179648 | tf_op jit(solution)/shard_map/all_to_all | solution.py:33
  127.1 5.8 %copy-start.2 = (bf16[512,768]{1,0:T(8,128)(2,1)}, bf16[512,768]{1,0:T(8,128)(2,1)S(1)}, u32[]{:S(2)}) copy-start(bf16[512,768]{1,0:T(8,128)(2,1)S(1)} %all_gather.25.hidden) | copy-start | bytes 2359300
  127.6 3.9 %collective-permute-start.4 = (bf16[384,768]{1,0:T(8,128)(2,1)S(1)}, bf16[384,768]{1,0:T(8,128)(2,1)S(1)}, u32[]{:S(2)}, u32[]{:S(2)}) collective-permute-start(bf16[384,768]{1,0:T(8,128)(2,1)S(1)} %convolution_convert_fusion.1), channel_id=1, source_target_pairs={{0,8},{8,0},{1,9},{9,1},{2,10},{10,2},{3,11},{11,3},{4,12},{12,4},... | collective-permute-start | bytes 1769480 | tf_op jit(solution)/shard_map/ppermute | solution.py:43
  132.9 21.8 %all-to-all-start.2 = ((bf16[4,96,768]{2,1,0:T(8,128)(2,1)}), bf16[4,96,768]{2,1,0:T(8,128)(2,1)S(1)}, u32[]{:S(2)}, u32[]{:S(2)}) async-start(bf16[4,96,768]{2,1,0:T(8,128)(2,1)} %bitcast.23), calls=%async_computation.2 | async-start | bytes 1179648 | tf_op jit(solution)/shard_map/all_to_all | solution.py:204
  142.3 4.4 %collective-permute-start.5 = (bf16[512,768]{1,0:T(8,128)(2,1)}, bf16[512,768]{1,0:T(8,128)(2,1)S(1)}, u32[]{:S(2)}, u32[]{:S(2)}) collective-permute-start(bf16[512,768]{1,0:T(8,128)(2,1)} %shard_map.75), channel_id=1, source_target_pairs={{0,8},{8,0},{1,9},{9,1},{2,10},{10,2},{3,11},{11,3},{4,12},{12,4},... | collective-permute-start | bytes 2359304 | tf_op jit(solution)/shard_map/ppermute | solution.py:43
  146.7 0.9 copy-start.5
  156.3 53.3 %all-to-all-start.4 = ((bf16[4,256,768]{2,1,0:T(8,128)(2,1)}), bf16[4,256,768]{2,1,0:T(8,128)(2,1)S(1)}, u32[]{:S(2)}, u32[]{:S(2)}) async-start(bf16[4,256,768]{2,1,0:T(8,128)(2,1)} %shard_map.76), calls=%async_computation.4 | async-start | bytes 3145728 | tf_op jit(solution)/shard_map/all_to_all | solution.py:33
  210.8 32.2 %all-to-all-start.5 = ((bf16[4,64,768]{2,1,0:T(8,128)(2,1)}), bf16[4,64,768]{2,1,0:T(8,128)(2,1)S(1)}, u32[]{:S(2)}, u32[]{:S(2)}) async-start(bf16[4,64,768]{2,1,0:T(8,128)(2,1)} %bitcast.11), calls=%async_computation.5 | async-start | bytes 786432 | tf_op jit(solution)/shard_map/all_to_all | solution.py:33

commit v6 on v5

--- a/solution.py
+++ b/solution.py
@@ -47,39 +47,40 @@
     return lax.optimization_barrier((values, earlier))[0]
 
 
-def feature_kernel(act, hidden, down, up, *rest):
+def feature_kernel(act, hidden, weights, *rest):
     out = rest[-1]
-    features = down.shape[1]
+    features = weights.shape[1] // 2
     rows = act.shape[0] // 4
-    for block in range(4):
-        here = pl.ds(block * rows, rows)
-        values = (
-            contract(act[here], down[...], ((1,), (0,))).astype(BF16),
-            contract(hidden[here], up[...], ((1,), (1,))).astype(BF16),
-        )
-        for side, value in enumerate(values):
-            columns = pl.ds(side * features, features)
-            if len(rest) == 1:
-                out[here, columns] = value
-            else:
-                out[block, pl.ds(0, rows), columns] = value
-        if len(rest) == 2:
-            out[block, pl.ds(rows, rows)] = rest[0][here]
-
-
-def feature_values(act, hidden, down, up, *more):
+    low, high = pl.ds(0, features), pl.ds(features, features)
+    for columns in (low, high):
+        if columns is low:
+            values = contract(act[...], weights[:, low], ((1,), (0,)))
+        else:
+            values = contract(hidden[:, low], weights[low, high], ((1,), (1,)))
+            values += contract(hidden[:, high], weights[high, high], ((1,), (1,)))
+        values = values.astype(BF16)
+        if len(rest) == 1:
+            out[:, columns] = values
+        else:
+            for block in range(4):
+                out[block, pl.ds(0, rows), columns] = values[block * rows : (block + 1) * rows]
+    if len(rest) == 2:
+        for block in range(4):
+            out[block, pl.ds(rows, rows)] = rest[0][pl.ds(block * rows, rows)]
+
+
+def feature_values(act, hidden, weights, *more):
     rows, depth = act.shape
-    features = down.shape[1]
-    shape = (4, rows // 2, 2 * features) if more else (rows, 2 * features)
+    shape = (4, rows // 2, depth) if more else (rows, depth)
     return pl.pallas_call(
         feature_kernel,
         out_shape=jax.ShapeDtypeStruct(shape, BF16),
         cost_estimate=pl.CostEstimate(
-            flops=4 * rows * depth * features,
-            bytes_accessed=4 * rows * depth + 8 * depth * features,
+            flops=2 * rows * depth * depth,
+            bytes_accessed=6 * rows * depth + 2 * depth * depth,
             transcendentals=0,
         ),
-    )(act, hidden, down, up, *more)
+    )(act, hidden, weights, *more)
 
 
 def pack(piece):
@@ -158,9 +159,12 @@
 
     kept, received = half_rows(side), other_core(half_rows(1 - side))
     up_half, down_half = after((up_half, down_half), received)
-    up_far = other_core(up_half)
+    both = jnp.concatenate([up_half[:, :features], up_half[:, features:]], axis=0)
+    my_both = jnp.concatenate([down_half, both], axis=1)
+    far_both = other_core(my_both)
+    down_far = far_both[:, :features]
+    up_far = jnp.concatenate([far_both[:features, features:], far_both[features:, features:]], axis=1)
     up_both = jnp.concatenate([up_half, up_far], axis=0)
-    down_far = other_core(down_half)
     rows = jnp.concatenate(
         [
             kept[:, :features],
@@ -198,8 +202,8 @@
     up_term = (loss_scale * up_term).astype(BF16)
 
     act, hidden = after((act, hidden), up_term)
-    far = other_core(feature_values(act, hidden, down_far, up_far))
-    total = feature_values(act, hidden, down_half, up_half, far)
+    far = other_core(feature_values(act, hidden, far_both))
+    total = feature_values(act, hidden, my_both, far)
     total = total.reshape(16 * own, 2 * features)
     up_parts = after(lax.all_to_all(up_term, "l", 0, 0, tiled=True), total)
     up_piece = jnp.sum(up_parts.reshape(4, -1, half).astype(F32), axis=0).astype(BF16)

time: 245 us -> 236 us (0.963)
  the two profiles are of different devices: /device:TPU:10 before, /device:TPU:6 now
where the time goes in v6:
time: 236 us; the launch traced here: 234 us
  blocking collectives  137 us (58%)
  starting transfers between devices  40.1 us (17%)
  waiting for transfers between devices  22.5 us (10%)
  Pallas kernels  11.1 us (5%)
  other arithmetic  9.93 us (4%)
  matrix products  7.65 us (3%)
  local copies, waits for them, and re-layouts  3.7 us (2%)
    all_gather x5, blocking collectives, gather(): return lax.all_gather(values, axis, axis=0, tiled=True)  88.7 us
    all_gather x1, blocking collectives, on_device(): pieces = lax.all_gather(packed, ('e', 'l'), axis_index_groups=[FOLDED])  48.6 us
    all_to_all x5, starting transfers between devices, scatter_sum(): parts = lax.all_to_all(values, axis, 0, 0, tiled=True)  24.9 us
    all_to_all x5, waiting for transfers between devices, scatter_sum(): parts = lax.all_to_all(values, axis, 0, 0, tiled=True)  12.1 us
    ppermute x5, starting transfers between devices, other_core(): return lax.ppermute(values, 'k', [(0, 1), (1, 0)])  9.74 us
    pallas_call x2, Pallas kernels, feature_values(): pl.pallas_call(feature_kernel, out_shape=jax.ShapeDtypeStruct(shape, BF16...  7.84 us
    dot_general x7, matrix products, contract(): lax.dot_general(left, right, (dims, ((), ())), preferred_element_type=F32)  7.65 us
    ppermute x5, waiting for transfers between devices, other_core(): return lax.ppermute(values, 'k', [(0, 1), (1, 0)])  7.44 us
  transfers between devices with their start and end apart: 11, of which 6 were waited for; matrix products, arithmetic and copies ran while one was open for 3% of the time, Pallas kernels for 5%

profile of v6, /device:TPU:6, one launch (start us, length us, event | category | flops | bytes accessed | tf_op | source)
XLA Modules:
  0.0 234.1 jit_solution(17634182007199412032)
XLA Ops:
  0.7 1.0 constant_dynamic-slice_fusion.2
  1.6 1.9 collective-permute-start
  3.7 1.0 collective-permute-done
  4.8 0.1 maximum_maximum_fusion.weights
  4.9 2.1 collective-permute-start.1
  7.1 29.0 %all_gather.21 = bf16[128,1536]{1,0:T(8,128)(2,1)S(1)} all-gather(bf16[32,1536]{1,0:T(8,128)(2,1)S(1)} %pad_maximum_fusion.1), channel_id=1, replica_groups=mesh['x'=4,'h'=2,'y'=4,'k'=2,'e'=2,'l'=4] {'h','e'}, dimensions={0}, use_global_device_ids=true | all-gather | bytes 491520 | tf_op jit(solution)/shard_map/all_gather | solution.py:39
  36.1 14.3 %all_gather.22 = bf16[512,768]{1,0:T(8,128)(2,1)S(1)} all-gather(bf16[128,768]{1,0:T(8,128)(2,1)S(1)} %get-tuple-element.45), channel_id=1, replica_groups=mesh['x'=4,'h'=2,'y'=4,'k'=2,'e'=2,'l'=4] {'x'}, dimensions={0}, use_global_device_ids=true | all-gather | bytes 983040 | tf_op jit(solution)/shard_map/all_gather | solution.py:39
  50.5 1.7 convolution_convert_fusion
  52.2 4.5 %all-to-all-start = ((bf16[4,128,768]{2,1,0:T(8,128)(2,1)}), bf16[4,128,768]{2,1,0:T(8,128)(2,1)}, u32[]{:S(2)}, u32[]{:S(2)}) async-start(bf16[4,128,768]{2,1,0:T(8,128)(2,1)} %bitcast.22), calls=%async_computation | async-start | bytes 1572864 | tf_op jit(solution)/shard_map/all_to_all | solution.py:33
  56.6 14.9 %all_gather.24 = bf16[512,768]{1,0:T(8,128)(2,1)} all-gather(bf16[128,768]{1,0:T(8,128)(2,1)S(1)} %get-tuple-element.25), channel_id=1, replica_groups=mesh['x'=4,'h'=2,'y'=4,'k'=2,'e'=2,'l'=4] {'x'}, dimensions={0}, use_global_device_ids=true | all-gather | bytes 983040 | tf_op jit(solution)/shard_map/all_gather | solution.py:39
  71.5 1.3 convert_reduce_fusion.1
  72.9 0.6 fusion.7
  73.5 1.5 add_convert_fusion
  75.0 4.9 %all-to-all-start.1 = ((bf16[4,128,768]{2,1,0:T(8,128)(2,1)}), bf16[4,128,768]{2,1,0:T(8,128)(2,1)S(1)}, u32[]{:S(2)}, u32[]{:S(2)}) async-start(bf16[4,128,768]{2,1,0:T(8,128)(2,1)} %bitcast.1), calls=%async_computation.1 | async-start | bytes 1572864 | tf_op jit(solution)/shard_map/all_to_all | solution.py:33
  79.9 0.8 convert_element_type.113
  80.7 17.0 %all_gather.23.act = bf16[512,768]{1,0:T(8,128)(2,1)S(1)} all-gather(bf16[128,768]{1,0:T(8,128)(2,1)S(1)} %multiply_convert_fusion.3), channel_id=1, replica_groups=mesh['x'=4,'h'=2,'y'=4,'k'=2,'e'=2,'l'=4] {'y'}, dimensions={0}, use_global_device_ids=true | all-gather | bytes 983040 | tf_op jit(solution)/shard_map/all_gather | solution.py:39
  97.7 1.0 convert_reduce_fusion
  98.7 0.6 convolution_convert_fusion.2
  99.3 1.9 collective-permute-start.2
  101.3 2.0 collective-permute-done.2
  103.2 1.4 multiply_convert_fusion.2
  104.7 4.0 %all-to-all-start.3 = ((bf16[4,192,384]{2,1,0:T(8,128)(2,1)}), bf16[4,192,384]{2,1,0:T(8,128)(2,1)S(1)}, u32[]{:S(2)}, u32[]{:S(2)}) async-start(bf16[4,192,384]{2,1,0:T(8,128)(2,1)} %bitcast.6), calls=%async_computation.3 | async-start | bytes 1179648 | tf_op jit(solution)/shard_map/all_to_all | solution.py:33
  108.7 0.2 fusion.14
  108.8 13.5 %all_gather.25.hidden = bf16[512,768]{1,0:T(8,128)(2,1)S(1)} all-gather(bf16[128,768]{1,0:T(8,128)(2,1)S(1)} %fusion.14), channel_id=1, replica_groups=mesh['x'=4,'h'=2,'y'=4,'k'=2,'e'=2,'l'=4] {'y'}, dimensions={0}, use_global_device_ids=true | all-gather | bytes 983040 | tf_op jit(solution)/shard_map/all_gather | solution.py:39
  122.4 0.5 convolution_convert_fusion.1
  122.9 1.9 collective-permute-start.3
  124.8 2.0 collective-permute-done.3
  126.8 1.3 multiply_convert_fusion.1
  128.1 5.4 %all-to-all-start.2 = ((bf16[4,96,768]{2,1,0:T(8,128)(2,1)}), bf16[4,96,768]{2,1,0:T(8,128)(2,1)S(1)}, u32[]{:S(2)}, u32[]{:S(2)}) async-start(bf16[4,96,768]{2,1,0:T(8,128)(2,1)} %bitcast.3), calls=%async_computation.2 | async-start | bytes 1179648 | tf_op jit(solution)/shard_map/all_to_all | solution.py:208
  133.5 3.7 %shard_map.75 = bf16[512,768]{1,0:T(8,128)(2,1)} custom-call(bf16[512,768]{1,0:T(8,128)(2,1)} %copy-done.1, bf16[512,768]{1,0:T(8,128)(2,1)} %copy-done.2, bf16[768,768]{1,0:T(8,128)(2,1)} %copy-done.3), custom_call_target="tpu_custom_call" | custom-call | flops 603979776 | bytes 3538944 | tf_op jit(solution)/shard_map/pallas_call | solution.py:75
  137.2 1.9 collective-permute-start.4
  139.1 2.5 %collective-permute-done.4.rest_0_ = bf16[512,768]{1,0:T(8,128)(2,1)S(1)} collective-permute-done((bf16[512,768]{1,0:T(8,128)(2,1)}, bf16[512,768]{1,0:T(8,128)(2,1)S(1)}, u32[]{:S(2)}, u32[]{:S(2)}) %collective-permute-start.4) | collective-permute-done | bytes 786464 | tf_op jit(solution)/shard_map/ppermute | solution.py:43
  141.6 0.9 copy-done.9
  142.5 4.2 %shard_map.76 = bf16[4,256,768]{2,1,0:T(8,128)(2,1)} custom-call(bf16[512,768]{1,0:T(8,128)(2,1)} %copy-done.1, bf16[512,768]{1,0:T(8,128)(2,1)} %copy-done.2, bf16[768,768]{1,0:T(8,128)(2,1)} %copy-done.4, bf16[512,768]{1,0:T(8,128)(2,1)} %copy-done.9), custom_call_target="tpu_custom_call" | custom-call | flops 603979776 | bytes 3538944 | tf_op jit(solution)/shard_map/pallas_call | solution.py:75
  146.6 0.1 reduce_sum.69
  146.7 3.0 %all-to-all-done.2 = bf16[4,96,768]{2,1,0:T(8,128)(2,1)S(1)} async-done(((bf16[4,96,768]{2,1,0:T(8,128)(2,1)}), bf16[4,96,768]{2,1,0:T(8,128)(2,1)S(1)}, u32[]{:S(2)}, u32[]{:S(2)}) %all-to-all-start.2) | async-done | bytes 589856 | tf_op jit(solution)/shard_map/all_to_all | solution.py:208
  149.7 0.1 reduce_sum.68
  149.8 0.6 fusion.5
  151.4 4.6 %all-to-all-start.4 = ((bf16[4,256,768]{2,1,0:T(8,128)(2,1)}), bf16[4,256,768]{2,1,0:T(8,128)(2,1)S(1)}, u32[]{:S(2)}, u32[]{:S(2)}) async-start(bf16[4,256,768]{2,1,0:T(8,128)(2,1)} %shard_map.76), calls=%async_computation.4 | async-start | bytes 3145728 | tf_op jit(solution)/shard_map/all_to_all | solution.py:33
  156.0 48.6 %all-gather.2 = f16[3200,384]{1,0:T(8,128)(2,1)} all-gather(f16[400,384]{1,0:T(8,128)(2,1)S(1)} %concatenate.34), channel_id=2, replica_groups={{0,2,4,6,7,5,3,1},{8,10,12,14,15,13,11,9},{16,18,20,22,23,21,19,17},{24..., dimensions={0}, use_global_device_ids=true | all-gather | bytes 2764800 | tf_op jit(solution)/shard_map/all_gather | solution.py:212
  204.6 0.4 reduce_sum.70
  205.1 0.8 copy.9
  205.8 7.0 %all-to-all-start.5 = ((bf16[4,64,768]{2,1,0:T(8,128)(2,1)}), bf16[4,64,768]{2,1,0:T(8,128)(2,1)S(1)}, u32[]{:S(2)}, u32[]{:S(2)}) async-start(bf16[4,64,768]{2,1,0:T(8,128)(2,1)} %bitcast.11), calls=%async_computation.5 | async-start | bytes 786432 | tf_op jit(solution)/shard_map/all_to_all | solution.py:33
  212.9 0.9 exponential_reduce_fusion
  213.7 4.2 %multiply_convert_fusion.pieces = bf16[8,384,384]{2,1,0:T(8,128)(2,1)} fusion(f32[8]{0:T(128)S(1)} %exponential_reduce_fusion, f16[8,400,384]{2,1,0:T(8,128)(2,1)} %bitcast.20), kind=kLoop, calls=%fused_computation | loop fusion | flops 3538944 | bytes 4718624 | tf_op jit(solution)/shard_map/convert_element_type | solution.py:97
  217.9 3.3 %shard_map.77 = (bf16[384,1536]{1,0:T(8,128)(2,1)}, bf16[1536,384]{1,0:T(8,128)(2,1)}) custom-call(bf16[8,384,384]{2,1,0:T(8,128)(2,1)} %multiply_convert_fusion.pieces), custom_call_target="tpu_custom_call" | custom-call | tf_op jit(solution)/shard_map/pallas_call | solution.py:130
  221.2 12.0 %all-to-all-done.5 = bf16[4,64,768]{2,1,0:T(8,128)(2,1)S(1)} async-done(((bf16[4,64,768]{2,1,0:T(8,128)(2,1)}), bf16[4,64,768]{2,1,0:T(8,128)(2,1)S(1)}, u32[]{:S(2)}, u32[]{:S(2)}) %all-to-all-start.5) | async-done | bytes 393248 | tf_op jit(solution)/shard_map/all_to_all | solution.py:33
  233.4 0.6 fusion.32
  (45 shorter events, 0.7 us)
Async XLA Ops:
  0.6 2.9 %copy-start = (bf16[1536,384]{1,0:T(8,128)(2,1)S(1)}, bf16[1536,384]{1,0:T(8,128)(2,1)}, u32[]{:S(2)}) copy-start(bf16[1536,384]{1,0:T(8,128)(2,1)} %param.6) | copy-start | bytes 3538948
  0.6 3.0 %copy-start.12 = (bf16[384,1536]{1,0:T(8,128)(2,1)S(1)}, bf16[384,1536]{1,0:T(8,128)(2,1)}, u32[]{:S(2)}) copy-start(bf16[384,1536]{1,0:T(8,128)(2,1)} %param.5) | copy-start | bytes 3538948
  1.6 3.1 %collective-permute-start = (bf16[32,768]{1,0:T(8,128)(2,1)S(1)}, bf16[32,768]{1,0:T(8,128)(2,1)S(1)}, u32[]{:S(2)}, u32[]{:S(2)}) collective-permute-start(bf16[32,768]{1,0:T(8,128)(2,1)S(1)} %pad_maximum_fusion.2), channel_id=1, source_target_pairs={{0,8},{8,0},{1,9},{9,1},{2,10},{10,2},{3,11},{11,3},{4,12},{12,4},... | collective-permute-start | bytes 147464 | tf_op jit(solution)/shard_map/ppermute | solution.py:43
  4.9 45.5 %copy-start.4 = (bf16[768,768]{1,0:T(8,128)(2,1)}, bf16[768,768]{1,0:T(8,128)(2,1)S(1)}, u32[]{:S(2)}) copy-start(bf16[768,768]{1,0:T(8,128)(2,1)S(1)} %maximum_maximum_fusion.weights) | copy-start | bytes 3538948
  4.9 45.5 %collective-permute-start.1 = (bf16[768,768]{1,0:T(8,128)(2,1)S(1)}, bf16[768,768]{1,0:T(8,128)(2,1)S(1)}, u32[]{:S(2)}, u32[]{:S(2)}) collective-permute-start(bf16[768,768]{1,0:T(8,128)(2,1)S(1)} %maximum_maximum_fusion.weights), channel_id=1, source_target_pairs={{0,8},{8,0},{1,9},{9,1},{2,10},{10,2},{3,11},{11,3},{4,12},{12,4},... | collective-permute-start | bytes 3538952 | tf_op jit(solution)/shard_map/ppermute | solution.py:43
  50.4 1.8 copy-start.10
  50.4 22.4 %copy-start.3 = (bf16[768,768]{1,0:T(8,128)(2,1)}, bf16[768,768]{1,0:T(8,128)(2,1)S(1)}, u32[]{:S(2)}) copy-start(bf16[768,768]{1,0:T(8,128)(2,1)S(1)} %collective-permute-done.1.weights) | copy-start | bytes 3538948
  52.2 19.4 %all-to-all-start = ((bf16[4,128,768]{2,1,0:T(8,128)(2,1)}), bf16[4,128,768]{2,1,0:T(8,128)(2,1)}, u32[]{:S(2)}, u32[]{:S(2)}) async-start(bf16[4,128,768]{2,1,0:T(8,128)(2,1)} %bitcast.22), calls=%async_computation | async-start | bytes 1572864 | tf_op jit(solution)/shard_map/all_to_all | solution.py:33
  71.5 1.4 copy-start.5
  75.0 22.7 %all-to-all-start.1 = ((bf16[4,128,768]{2,1,0:T(8,128)(2,1)}), bf16[4,128,768]{2,1,0:T(8,128)(2,1)S(1)}, u32[]{:S(2)}, u32[]{:S(2)}) async-start(bf16[4,128,768]{2,1,0:T(8,128)(2,1)} %bitcast.1), calls=%async_computation.1 | async-start | bytes 1572864 | tf_op jit(solution)/shard_map/all_to_all | solution.py:33
  80.6 18.1 %copy-start.6 = (bf16[512,768]{1,0:T(8,128)(2,1)S(1)}, bf16[512,768]{1,0:T(8,128)(2,1)}, u32[]{:S(2)}) copy-start(bf16[512,768]{1,0:T(8,128)(2,1)} %all_gather.24) | copy-start | bytes 2359300
  97.7 5.5 %copy-start.1 = (bf16[512,768]{1,0:T(8,128)(2,1)}, bf16[512,768]{1,0:T(8,128)(2,1)S(1)}, u32[]{:S(2)}) copy-start(bf16[512,768]{1,0:T(8,128)(2,1)S(1)} %all_gather.23.act) | copy-start | bytes 2359300
  99.3 3.9 %collective-permute-start.2 = (bf16[768,384]{1,0:T(8,128)(2,1)S(1)}, bf16[768,384]{1,0:T(8,128)(2,1)S(1)}, u32[]{:S(2)}, u32[]{:S(2)}) collective-permute-start(bf16[768,384]{1,0:T(8,128)(2,1)S(1)} %convolution_convert_fusion.2), channel_id=1, source_target_pairs={{0,8},{8,0},{1,9},{9,1},{2,10},{10,2},{3,11},{11,3},{4,12},{12,4},... | collective-permute-start | bytes 1769480 | tf_op jit(solution)/shard_map/ppermute | solution.py:43
  104.7 4.0 %copy-start.7 = (f32[128,768]{1,0:T(8,128)S(1)}, f32[128,768]{1,0:T(8,128)}, u32[]{:S(2)}) copy-start(f32[128,768]{1,0:T(8,128)} %convert_element_type.113) | copy-start | bytes 1179652
  104.7 4.0 %copy-start.8 = (f32[128,768]{1,0:T(8,128)S(1)}, f32[128,768]{1,0:T(8,128)}, u32[]{:S(2)}) copy-start(f32[128,768]{1,0:T(8,128)} %convert_reduce_fusion) | copy-start | bytes 1179652
  104.7 23.4 %all-to-all-start.3 = ((bf16[4,192,384]{2,1,0:T(8,128)(2,1)}), bf16[4,192,384]{2,1,0:T(8,128)(2,1)S(1)}, u32[]{:S(2)}, u32[]{:S(2)}) async-start(bf16[4,192,384]{2,1,0:T(8,128)(2,1)} %bitcast.6), calls=%async_computation.3 | async-start | bytes 1179648 | tf_op jit(solution)/shard_map/all_to_all | solution.py:33
  108.7 13.7 %copy-start.11 = (bf16[512,768]{1,0:T(8,128)(2,1)S(1)}, bf16[512,768]{1,0:T(8,128)(2,1)}, u32[]{:S(2)}) copy-start(bf16[512,768]{1,0:T(8,128)(2,1)} %copy-done.10) | copy-start | bytes 2359300
  122.4 5.7 %copy-start.2 = (bf16[512,768]{1,0:T(8,128)(2,1)}, bf16[512,768]{1,0:T(8,128)(2,1)S(1)}, u32[]{:S(2)}) copy-start(bf16[512,768]{1,0:T(8,128)(2,1)S(1)} %all_gather.25.hidden) | copy-start | bytes 2359300
  122.9 3.9 %collective-permute-start.3 = (bf16[384,768]{1,0:T(8,128)(2,1)S(1)}, bf16[384,768]{1,0:T(8,128)(2,1)S(1)}, u32[]{:S(2)}, u32[]{:S(2)}) collective-permute-start(bf16[384,768]{1,0:T(8,128)(2,1)S(1)} %convolution_convert_fusion.1), channel_id=1, source_target_pairs={{0,8},{8,0},{1,9},{9,1},{2,10},{10,2},{3,11},{11,3},{4,12},{12,4},... | collective-permute-start | bytes 1769480 | tf_op jit(solution)/shard_map/ppermute | solution.py:43
  128.1 21.6 %all-to-all-start.2 = ((bf16[4,96,768]{2,1,0:T(8,128)(2,1)}), bf16[4,96,768]{2,1,0:T(8,128)(2,1)S(1)}, u32[]{:S(2)}, u32[]{:S(2)}) async-start(bf16[4,96,768]{2,1,0:T(8,128)(2,1)} %bitcast.3), calls=%async_computation.2 | async-start | bytes 1179648 | tf_op jit(solution)/shard_map/all_to_all | solution.py:208
  137.2 4.4 %collective-permute-start.4 = (bf16[512,768]{1,0:T(8,128)(2,1)}, bf16[512,768]{1,0:T(8,128)(2,1)S(1)}, u32[]{:S(2)}, u32[]{:S(2)}) collective-permute-start(bf16[512,768]{1,0:T(8,128)(2,1)} %shard_map.75), channel_id=1, source_target_pairs={{0,8},{8,0},{1,9},{9,1},{2,10},{10,2},{3,11},{11,3},{4,12},{12,4},... | collective-permute-start | bytes 2359304 | tf_op jit(solution)/shard_map/ppermute | solution.py:43
  141.6 0.9 copy-start.9
  151.4 53.3 %all-to-all-start.4 = ((bf16[4,256,768]{2,1,0:T(8,128)(2,1)}), bf16[4,256,768]{2,1,0:T(8,128)(2,1)S(1)}, u32[]{:S(2)}, u32[]{:S(2)}) async-start(bf16[4,256,768]{2,1,0:T(8,128)(2,1)} %shard_map.76), calls=%async_computation.4 | async-start | bytes 3145728 | tf_op jit(solution)/shard_map/all_to_all | solution.py:33
  205.8 27.5 %all-to-all-start.5 = ((bf16[4,64,768]{2,1,0:T(8,128)(2,1)}), bf16[4,64,768]{2,1,0:T(8,128)(2,1)S(1)}, u32[]{:S(2)}, u32[]{:S(2)}) async-start(bf16[4,64,768]{2,1,0:T(8,128)(2,1)} %bitcast.11), calls=%async_computation.5 | async-start | bytes 786432 | tf_op jit(solution)/shard_map/all_to_all | solution.py:33

commit v7 on v6

--- a/solution.py
+++ b/solution.py
@@ -50,7 +50,7 @@
 def feature_kernel(act, hidden, weights, *rest):
     out = rest[-1]
     features = weights.shape[1] // 2
-    rows = act.shape[0] // 4
+    rows = act.shape[0] // 16
     low, high = pl.ds(0, features), pl.ds(features, features)
     for columns in (low, high):
         if columns is low:
@@ -62,16 +62,16 @@
         if len(rest) == 1:
             out[:, columns] = values
         else:
-            for block in range(4):
+            for block in range(16):
                 out[block, pl.ds(0, rows), columns] = values[block * rows : (block + 1) * rows]
     if len(rest) == 2:
-        for block in range(4):
+        for block in range(16):
             out[block, pl.ds(rows, rows)] = rest[0][pl.ds(block * rows, rows)]
 
 
 def feature_values(act, hidden, weights, *more):
     rows, depth = act.shape
-    shape = (4, rows // 2, depth) if more else (rows, depth)
+    shape = (16, rows // 8, depth) if more else (rows, depth)
     return pl.pallas_call(
         feature_kernel,
         out_shape=jax.ShapeDtypeStruct(shape, BF16),
@@ -88,11 +88,11 @@
     top = jnp.maximum(jnp.max(jnp.abs(wide)), 1e-37)
     power = jnp.clip(14.0 - jnp.ceil(jnp.log2(top)), -20.0, 120.0)
     scaled = (wide * jnp.exp2(power)).astype(F16)
-    return jnp.concatenate([scaled, jnp.full((16, piece.shape[1]), power).astype(F16)], axis=0)
+    return jnp.concatenate([scaled, jnp.full((8, piece.shape[1]), power).astype(F16)], axis=0)
 
 
 def unpack(packed):
-    rows = packed.shape[1] - 16
+    rows = packed.shape[1] - 8
     power = packed[:, rows:, :1].astype(F32)[:, :1]
     return (packed[:, :rows].astype(F32) * jnp.exp2(-power)).astype(BF16)
 
@@ -191,11 +191,12 @@
         (gather(gelu_value(preact).astype(BF16), "y"), act_grad, preact)
     )
     far = contract(act, far_grad, ((0,), (0,))).astype(BF16)
+    hidden_grad = (act_grad * gelu_slope(preact)).astype(BF16)
+    my_grad = after(my_grad, hidden_grad)
     down_term = contract(act, my_grad, ((0,), (0,))) + other_core(far).astype(F32)
     down_term = (loss_scale * down_term).astype(BF16)
     down_piece = scatter_sum(down_term, "l").astype(BF16)
 
-    hidden_grad = (act_grad * gelu_slope(preact)).astype(BF16)
     hidden = gather(after(hidden_grad, down_term), "y")
     far = contract(every_input[:, features:], hidden, ((0,), (0,))).astype(BF16)
     up_term = contract(every_input[:, :features], hidden, ((0,), (0,))) + other_core(far).astype(F32)
@@ -214,8 +215,7 @@
         (scatter_sum(after(total, packed), "x").astype(BF16), pieces)
     )
     up_grad, down_grad = place(unpack(pieces))
-    total = total.reshape(2, 4, own // 2, 2 * features).transpose(1, 0, 2, 3)
-    total = scatter_sum(total.reshape(4 * own, 2 * features), ("h", "e")).astype(BF16)
+    total = scatter_sum(total, ("h", "e")).astype(BF16)
     total = after(total, (up_grad, down_grad))
     swapped = jnp.concatenate([total[own // 2 :], total[: own // 2]], axis=0)
     total = jnp.where(side == 0, total, swapped)

time: 236 us -> 238 us (level)
  no operation moved by 1% of the time
where the time goes in v7:
time: 238 us; the launch traced here: 234 us
  blocking collectives  137 us (58%)
  starting transfers between devices  40.1 us (17%)
  waiting for transfers between devices  21.6 us (9%)
  Pallas kernels  11.1 us (5%)
  other arithmetic  9.85 us (4%)
  matrix products  8.67 us (4%)
  local copies, waits for them, and re-layouts  3.96 us (2%)
    all_gather x5, blocking collectives, gather(): return lax.all_gather(values, axis, axis=0, tiled=True)  89.4 us
    all_gather x1, blocking collectives, on_device(): pieces = lax.all_gather(packed, ('e', 'l'), axis_index_groups=[FOLDED])  47.7 us
    all_to_all x5, starting transfers between devices, scatter_sum(): parts = lax.all_to_all(values, axis, 0, 0, tiled=True)  25.1 us
    all_to_all x5, waiting for transfers between devices, scatter_sum(): parts = lax.all_to_all(values, axis, 0, 0, tiled=True)  12.1 us
    ppermute x5, starting transfers between devices, other_core(): return lax.ppermute(values, 'k', [(0, 1), (1, 0)])  9.74 us
    dot_general x7, matrix products, contract(): lax.dot_general(left, right, (dims, ((), ())), preferred_element_type=F32)  8.67 us
    pallas_call x2, Pallas kernels, feature_values(): pl.pallas_call(feature_kernel, out_shape=jax.ShapeDtypeStruct(shape, BF16...  7.82 us
    ppermute x5, waiting for transfers between devices, other_core(): return lax.ppermute(values, 'k', [(0, 1), (1, 0)])  6.56 us
  transfers between devices with their start and end apart: 11, of which 6 were waited for; matrix products, arithmetic and copies ran while one was open for 3% of the time, Pallas kernels for 5%

profile of v7, /device:TPU:6, one launch (start us, length us, event | category | flops | bytes accessed | tf_op | source)
XLA Modules:
  0.0 234.1 jit_solution(2465216772961096882)
XLA Ops:
  0.7 1.0 constant_dynamic-slice_fusion.2
  1.6 1.9 collective-permute-start
  3.7 1.0 collective-permute-done
  4.8 0.1 maximum_maximum_fusion.weights
  4.9 2.1 collective-permute-start.1
  7.1 29.0 %all_gather.21 = bf16[128,1536]{1,0:T(8,128)(2,1)S(1)} all-gather(bf16[32,1536]{1,0:T(8,128)(2,1)S(1)} %pad_maximum_fusion.1), channel_id=1, replica_groups=mesh['x'=4,'h'=2,'y'=4,'k'=2,'e'=2,'l'=4] {'h','e'}, dimensions={0}, use_global_device_ids=true | all-gather | bytes 491520 | tf_op jit(solution)/shard_map/all_gather | solution.py:39
  36.1 14.3 %all_gather.22 = bf16[512,768]{1,0:T(8,128)(2,1)S(1)} all-gather(bf16[128,768]{1,0:T(8,128)(2,1)S(1)} %get-tuple-element.47), channel_id=1, replica_groups=mesh['x'=4,'h'=2,'y'=4,'k'=2,'e'=2,'l'=4] {'x'}, dimensions={0}, use_global_device_ids=true | all-gather | bytes 983040 | tf_op jit(solution)/shard_map/all_gather | solution.py:39
  50.4 1.1 copy-done.3
  51.5 1.7 convolution_convert_fusion
  53.2 4.5 %all-to-all-start = ((bf16[4,128,768]{2,1,0:T(8,128)(2,1)}), bf16[4,128,768]{2,1,0:T(8,128)(2,1)S(1)}, u32[]{:S(2)}, u32[]{:S(2)}) async-start(bf16[4,128,768]{2,1,0:T(8,128)(2,1)} %bitcast), calls=%async_computation | async-start | bytes 1572864 | tf_op jit(solution)/shard_map/all_to_all | solution.py:33
  57.7 13.9 %all_gather.24 = bf16[512,768]{1,0:T(8,128)(2,1)S(1)} all-gather(bf16[128,768]{1,0:T(8,128)(2,1)S(1)} %get-tuple-element.26), channel_id=1, replica_groups=mesh['x'=4,'h'=2,'y'=4,'k'=2,'e'=2,'l'=4] {'x'}, dimensions={0}, use_global_device_ids=true | all-gather | bytes 983040 | tf_op jit(solution)/shard_map/all_gather | solution.py:39
  71.6 0.1 convert_reduce_fusion.1
  71.7 1.7 fusion.7
  73.3 1.5 add_convert_fusion
  74.8 4.5 %all-to-all-start.1 = ((bf16[4,128,768]{2,1,0:T(8,128)(2,1)}), bf16[4,128,768]{2,1,0:T(8,128)(2,1)}, u32[]{:S(2)}, u32[]{:S(2)}) async-start(bf16[4,128,768]{2,1,0:T(8,128)(2,1)} %bitcast.1), calls=%async_computation.1 | async-start | bytes 1572864 | tf_op jit(solution)/shard_map/all_to_all | solution.py:33
  79.4 0.1 multiply_convert_fusion.3
  79.5 18.0 %all_gather.23.act = bf16[512,768]{1,0:T(8,128)(2,1)S(1)} all-gather(bf16[128,768]{1,0:T(8,128)(2,1)S(1)} %multiply_convert_fusion.3), channel_id=1, replica_groups=mesh['x'=4,'h'=2,'y'=4,'k'=2,'e'=2,'l'=4] {'y'}, dimensions={0}, use_global_device_ids=true | all-gather | bytes 983040 | tf_op jit(solution)/shard_map/all_gather | solution.py:39
  97.5 1.6 convert_reduce_fusion
  99.0 0.6 convolution_convert_fusion.2
  99.6 1.9 collective-permute-start.2
  101.6 0.8 fusion.14
  102.5 1.1 collective-permute-done.2
  103.5 1.4 multiply_convert_fusion.2
  105.0 4.4 %all-to-all-start.3 = ((bf16[4,192,384]{2,1,0:T(8,128)(2,1)}), bf16[4,192,384]{2,1,0:T(8,128)(2,1)S(1)}, u32[]{:S(2)}, u32[]{:S(2)}) async-start(bf16[4,192,384]{2,1,0:T(8,128)(2,1)} %bitcast.6), calls=%async_computation.3 | async-start | bytes 1179648 | tf_op jit(solution)/shard_map/all_to_all | solution.py:33
  109.4 14.2 %all_gather.25.hidden = bf16[512,768]{1,0:T(8,128)(2,1)S(1)} all-gather(bf16[128,768]{1,0:T(8,128)(2,1)} %fusion.14), channel_id=1, replica_groups=mesh['x'=4,'h'=2,'y'=4,'k'=2,'e'=2,'l'=4] {'y'}, dimensions={0}, use_global_device_ids=true | all-gather | bytes 983040 | tf_op jit(solution)/shard_map/all_gather | solution.py:39
  123.6 0.5 convolution_convert_fusion.1
  124.1 1.9 collective-permute-start.3
  126.0 2.0 collective-permute-done.3
  128.0 1.3 multiply_convert_fusion.1
  129.3 5.3 %all-to-all-start.2 = ((bf16[4,96,768]{2,1,0:T(8,128)(2,1)}), bf16[4,96,768]{2,1,0:T(8,128)(2,1)S(1)}, u32[]{:S(2)}, u32[]{:S(2)}) async-start(bf16[4,96,768]{2,1,0:T(8,128)(2,1)} %bitcast.20), calls=%async_computation.2 | async-start | bytes 1179648 | tf_op jit(solution)/shard_map/all_to_all | solution.py:209
  134.6 3.7 %shard_map.75 = bf16[512,768]{1,0:T(8,128)(2,1)} custom-call(bf16[512,768]{1,0:T(8,128)(2,1)} %copy-done.1, bf16[512,768]{1,0:T(8,128)(2,1)} %copy-done.2, bf16[768,768]{1,0:T(8,128)(2,1)} %copy-done.3), custom_call_target="tpu_custom_call" | custom-call | flops 603979776 | bytes 3538944 | tf_op jit(solution)/shard_map/pallas_call | solution.py:75
  138.3 1.9 collective-permute-start.4
  140.2 2.5 %collective-permute-done.4.rest_0_ = bf16[512,768]{1,0:T(8,128)(2,1)S(1)} collective-permute-done((bf16[512,768]{1,0:T(8,128)(2,1)}, bf16[512,768]{1,0:T(8,128)(2,1)S(1)}, u32[]{:S(2)}, u32[]{:S(2)}) %collective-permute-start.4) | collective-permute-done | bytes 786464 | tf_op jit(solution)/shard_map/ppermute | solution.py:43
  142.7 0.9 copy-done.5
  143.6 4.2 %shard_map.76 = bf16[16,64,768]{2,1,0:T(8,128)(2,1)} custom-call(bf16[512,768]{1,0:T(8,128)(2,1)} %copy-done.1, bf16[512,768]{1,0:T(8,128)(2,1)} %copy-done.2, bf16[768,768]{1,0:T(8,128)(2,1)} %copy-done.4, bf16[512,768]{1,0:T(8,128)(2,1)} %copy-done.5), custom_call_target="tpu_custom_call" | custom-call | flops 603979776 | bytes 3538944 | tf_op jit(solution)/shard_map/pallas_call | solution.py:75
  147.7 0.1 reduce_sum.69
  147.8 3.0 %all-to-all-done.2 = bf16[4,96,768]{2,1,0:T(8,128)(2,1)S(1)} async-done(((bf16[4,96,768]{2,1,0:T(8,128)(2,1)}), bf16[4,96,768]{2,1,0:T(8,128)(2,1)S(1)}, u32[]{:S(2)}, u32[]{:S(2)}) %all-to-all-start.2) | async-done | bytes 589856 | tf_op jit(solution)/shard_map/all_to_all | solution.py:209
  150.8 0.1 reduce_sum.68
  150.9 0.6 fusion.5
  152.5 4.7 %all-to-all-start.4 = ((bf16[4,256,768]{2,1,0:T(8,128)(2,1)}), bf16[4,256,768]{2,1,0:T(8,128)(2,1)S(1)}, u32[]{:S(2)}, u32[]{:S(2)}) async-start(bf16[4,256,768]{2,1,0:T(8,128)(2,1)} %bitcast.19), calls=%async_computation.4 | async-start | bytes 3145728 | tf_op jit(solution)/shard_map/all_to_all | solution.py:33
  157.2 47.7 %all-gather.2 = f16[3136,384]{1,0:T(8,128)(2,1)} all-gather(f16[392,384]{1,0:T(8,128)(2,1)S(1)} %concatenate.34), channel_id=2, replica_groups={{0,2,4,6,7,5,3,1},{8,10,12,14,15,13,11,9},{16,18,20,22,23,21,19,17},{24..., dimensions={0}, use_global_device_ids=true | all-gather | bytes 2709504 | tf_op jit(solution)/shard_map/all_gather | solution.py:213
  204.9 1.1 reduce_sum.70
  206.0 7.0 %all-to-all-start.5 = ((bf16[4,64,768]{2,1,0:T(8,128)(2,1)}), bf16[4,64,768]{2,1,0:T(8,128)(2,1)S(1)}, u32[]{:S(2)}, u32[]{:S(2)}) async-start(bf16[4,64,768]{2,1,0:T(8,128)(2,1)} %bitcast.9), calls=%async_computation.5 | async-start | bytes 786432 | tf_op jit(solution)/shard_map/all_to_all | solution.py:33
  213.0 0.9 exponential_reduce_fusion
  213.8 4.2 %multiply_convert_fusion.pieces = bf16[8,384,384]{2,1,0:T(8,128)(2,1)} fusion(f32[8]{0:T(128)S(1)} %exponential_reduce_fusion, f16[8,392,384]{2,1,0:T(8,128)(2,1)} %bitcast.18), kind=kLoop, calls=%fused_computation | loop fusion | flops 3538944 | bytes 4718624 | tf_op jit(solution)/shard_map/convert_element_type | solution.py:97
  218.0 3.3 %shard_map.77 = (bf16[384,1536]{1,0:T(8,128)(2,1)}, bf16[1536,384]{1,0:T(8,128)(2,1)}) custom-call(bf16[8,384,384]{2,1,0:T(8,128)(2,1)} %multiply_convert_fusion.pieces), custom_call_target="tpu_custom_call" | custom-call | tf_op jit(solution)/shard_map/pallas_call | solution.py:130
  221.3 12.0 %all-to-all-done.5 = bf16[4,64,768]{2,1,0:T(8,128)(2,1)S(1)} async-done(((bf16[4,64,768]{2,1,0:T(8,128)(2,1)}), bf16[4,64,768]{2,1,0:T(8,128)(2,1)S(1)}, u32[]{:S(2)}, u32[]{:S(2)}) %all-to-all-start.5) | async-done | bytes 393248 | tf_op jit(solution)/shard_map/all_to_all | solution.py:33
  233.5 0.6 fusion.28
  (37 shorter events, 0.7 us)
Async XLA Ops:
  0.6 2.9 %copy-start = (bf16[1536,384]{1,0:T(8,128)(2,1)S(1)}, bf16[1536,384]{1,0:T(8,128)(2,1)}, u32[]{:S(2)}) copy-start(bf16[1536,384]{1,0:T(8,128)(2,1)} %param.6) | copy-start | bytes 3538948
  0.6 3.0 %copy-start.8 = (bf16[384,1536]{1,0:T(8,128)(2,1)S(1)}, bf16[384,1536]{1,0:T(8,128)(2,1)}, u32[]{:S(2)}) copy-start(bf16[384,1536]{1,0:T(8,128)(2,1)} %param.5) | copy-start | bytes 3538948
  1.6 3.1 %collective-permute-start = (bf16[32,768]{1,0:T(8,128)(2,1)S(1)}, bf16[32,768]{1,0:T(8,128)(2,1)S(1)}, u32[]{:S(2)}, u32[]{:S(2)}) collective-permute-start(bf16[32,768]{1,0:T(8,128)(2,1)S(1)} %pad_maximum_fusion.2), channel_id=1, source_target_pairs={{0,8},{8,0},{1,9},{9,1},{2,10},{10,2},{3,11},{11,3},{4,12},{12,4},... | collective-permute-start | bytes 147464 | tf_op jit(solution)/shard_map/ppermute | solution.py:43
  4.9 45.5 %copy-start.4 = (bf16[768,768]{1,0:T(8,128)(2,1)}, bf16[768,768]{1,0:T(8,128)(2,1)S(1)}, u32[]{:S(2)}) copy-start(bf16[768,768]{1,0:T(8,128)(2,1)S(1)} %maximum_maximum_fusion.weights) | copy-start | bytes 3538948
  4.9 45.5 %collective-permute-start.1 = (bf16[768,768]{1,0:T(8,128)(2,1)S(1)}, bf16[768,768]{1,0:T(8,128)(2,1)S(1)}, u32[]{:S(2)}, u32[]{:S(2)}) collective-permute-start(bf16[768,768]{1,0:T(8,128)(2,1)S(1)} %maximum_maximum_fusion.weights), channel_id=1, source_target_pairs={{0,8},{8,0},{1,9},{9,1},{2,10},{10,2},{3,11},{11,3},{4,12},{12,4},... | collective-permute-start | bytes 3538952 | tf_op jit(solution)/shard_map/ppermute | solution.py:43
  50.4 2.8 %copy-start.6 = (bf16[512,768]{1,0:T(8,128)(2,1)}, bf16[512,768]{1,0:T(8,128)(2,1)S(1)}, u32[]{:S(2)}) copy-start(bf16[512,768]{1,0:T(8,128)(2,1)S(1)} %all_gather.22) | copy-start | bytes 2359300
  50.4 1.1 copy-start.3
  53.2 18.3 %all-to-all-start = ((bf16[4,128,768]{2,1,0:T(8,128)(2,1)}), bf16[4,128,768]{2,1,0:T(8,128)(2,1)S(1)}, u32[]{:S(2)}, u32[]{:S(2)}) async-start(bf16[4,128,768]{2,1,0:T(8,128)(2,1)} %bitcast), calls=%async_computation | async-start | bytes 1572864 | tf_op jit(solution)/shard_map/all_to_all | solution.py:33
  74.8 22.7 %all-to-all-start.1 = ((bf16[4,128,768]{2,1,0:T(8,128)(2,1)}), bf16[4,128,768]{2,1,0:T(8,128)(2,1)}, u32[]{:S(2)}, u32[]{:S(2)}) async-start(bf16[4,128,768]{2,1,0:T(8,128)(2,1)} %bitcast.1), calls=%async_computation.1 | async-start | bytes 1572864 | tf_op jit(solution)/shard_map/all_to_all | solution.py:33
  97.5 6.1 %copy-start.1 = (bf16[512,768]{1,0:T(8,128)(2,1)}, bf16[512,768]{1,0:T(8,128)(2,1)S(1)}, u32[]{:S(2)}) copy-start(bf16[512,768]{1,0:T(8,128)(2,1)S(1)} %all_gather.23.act) | copy-start | bytes 2359300
  99.6 3.9 %collective-permute-start.2 = (bf16[768,384]{1,0:T(8,128)(2,1)S(1)}, bf16[768,384]{1,0:T(8,128)(2,1)S(1)}, u32[]{:S(2)}, u32[]{:S(2)}) collective-permute-start(bf16[768,384]{1,0:T(8,128)(2,1)S(1)} %convolution_convert_fusion.2), channel_id=1, source_target_pairs={{0,8},{8,0},{1,9},{9,1},{2,10},{10,2},{3,11},{11,3},{4,12},{12,4},... | collective-permute-start | bytes 1769480 | tf_op jit(solution)/shard_map/ppermute | solution.py:43
  105.0 18.6 %copy-start.7 = (bf16[512,768]{1,0:T(8,128)(2,1)S(1)}, bf16[512,768]{1,0:T(8,128)(2,1)}, u32[]{:S(2)}) copy-start(bf16[512,768]{1,0:T(8,128)(2,1)} %copy-done.6) | copy-start | bytes 2359300
  105.0 24.3 %all-to-all-start.3 = ((bf16[4,192,384]{2,1,0:T(8,128)(2,1)}), bf16[4,192,384]{2,1,0:T(8,128)(2,1)S(1)}, u32[]{:S(2)}, u32[]{:S(2)}) async-start(bf16[4,192,384]{2,1,0:T(8,128)(2,1)} %bitcast.6), calls=%async_computation.3 | async-start | bytes 1179648 | tf_op jit(solution)/shard_map/all_to_all | solution.py:33
  123.6 5.7 %copy-start.2 = (bf16[512,768]{1,0:T(8,128)(2,1)}, bf16[512,768]{1,0:T(8,128)(2,1)S(1)}, u32[]{:S(2)}) copy-start(bf16[512,768]{1,0:T(8,128)(2,1)S(1)} %all_gather.25.hidden) | copy-start | bytes 2359300
  124.1 3.9 %collective-permute-start.3 = (bf16[384,768]{1,0:T(8,128)(2,1)S(1)}, bf16[384,768]{1,0:T(8,128)(2,1)S(1)}, u32[]{:S(2)}, u32[]{:S(2)}) collective-permute-start(bf16[384,768]{1,0:T(8,128)(2,1)S(1)} %convolution_convert_fusion.1), channel_id=1, source_target_pairs={{0,8},{8,0},{1,9},{9,1},{2,10},{10,2},{3,11},{11,3},{4,12},{12,4},... | collective-permute-start | bytes 1769480 | tf_op jit(solution)/shard_map/ppermute | solution.py:43
  129.3 21.5 %all-to-all-start.2 = ((bf16[4,96,768]{2,1,0:T(8,128)(2,1)}), bf16[4,96,768]{2,1,0:T(8,128)(2,1)S(1)}, u32[]{:S(2)}, u32[]{:S(2)}) async-start(bf16[4,96,768]{2,1,0:T(8,128)(2,1)} %bitcast.20), calls=%async_computation.2 | async-start | bytes 1179648 | tf_op jit(solution)/shard_map/all_to_all | solution.py:209
  138.3 4.4 %collective-permute-start.4 = (bf16[512,768]{1,0:T(8,128)(2,1)}, bf16[512,768]{1,0:T(8,128)(2,1)S(1)}, u32[]{:S(2)}, u32[]{:S(2)}) collective-permute-start(bf16[512,768]{1,0:T(8,128)(2,1)} %shard_map.75), channel_id=1, source_target_pairs={{0,8},{8,0},{1,9},{9,1},{2,10},{10,2},{3,11},{11,3},{4,12},{12,4},... | collective-permute-start | bytes 2359304 | tf_op jit(solution)/shard_map/ppermute | solution.py:43
  142.7 0.9 copy-start.5
  152.5 52.4 %all-to-all-start.4 = ((bf16[4,256,768]{2,1,0:T(8,128)(2,1)}), bf16[4,256,768]{2,1,0:T(8,128)(2,1)S(1)}, u32[]{:S(2)}, u32[]{:S(2)}) async-start(bf16[4,256,768]{2,1,0:T(8,128)(2,1)} %bitcast.19), calls=%async_computation.4 | async-start | bytes 3145728 | tf_op jit(solution)/shard_map/all_to_all | solution.py:33
  206.0 27.4 %all-to-all-start.5 = ((bf16[4,64,768]{2,1,0:T(8,128)(2,1)}), bf16[4,64,768]{2,1,0:T(8,128)(2,1)S(1)}, u32[]{:S(2)}, u32[]{:S(2)}) async-start(bf16[4,64,768]{2,1,0:T(8,128)(2,1)} %bitcast.9), calls=%async_computation.5 | async-start | bytes 786432 | tf_op jit(solution)/shard_map/all_to_all | solution.py:33

commit v8 on v6

--- a/solution.py
+++ b/solution.py
@@ -88,11 +88,11 @@
     top = jnp.maximum(jnp.max(jnp.abs(wide)), 1e-37)
     power = jnp.clip(14.0 - jnp.ceil(jnp.log2(top)), -20.0, 120.0)
     scaled = (wide * jnp.exp2(power)).astype(F16)
-    return jnp.concatenate([scaled, jnp.full((16, piece.shape[1]), power).astype(F16)], axis=0)
+    return jnp.concatenate([scaled, jnp.full((8, piece.shape[1]), power).astype(F16)], axis=0)
 
 
 def unpack(packed):
-    rows = packed.shape[1] - 16
+    rows = packed.shape[1] - 8
     power = packed[:, rows:, :1].astype(F32)[:, :1]
     return (packed[:, :rows].astype(F32) * jnp.exp2(-power)).astype(BF16)
 

time: 236 us -> 238 us (level)
  waiting for transfers between devices: 22.5 us -> 26.7 us
    all_to_all x5, waiting for transfers between devices: 12.1 us -> 16.3 us  [scatter_sum(): parts = lax.all_to_all(values, axis, 0, 0, tiled=True)]
where the time goes in v8:
time: 238 us; the launch traced here: 237 us
  blocking collectives  136 us (57%)
  starting transfers between devices  40.2 us (17%)
  waiting for transfers between devices  26.7 us (11%)
  Pallas kernels  11.2 us (5%)
  other arithmetic  9.91 us (4%)
  matrix products  7.65 us (3%)
  local copies, waits for them, and re-layouts  3.71 us (2%)
    all_gather x5, blocking collectives, gather(): return lax.all_gather(values, axis, axis=0, tiled=True)  88.7 us
    all_gather x1, blocking collectives, on_device(): pieces = lax.all_gather(packed, ('e', 'l'), axis_index_groups=[FOLDED])  47.7 us
    all_to_all x5, starting transfers between devices, scatter_sum(): parts = lax.all_to_all(values, axis, 0, 0, tiled=True)  25 us
    all_to_all x5, waiting for transfers between devices, scatter_sum(): parts = lax.all_to_all(values, axis, 0, 0, tiled=True)  16.3 us
    ppermute x5, starting transfers between devices, other_core(): return lax.ppermute(values, 'k', [(0, 1), (1, 0)])  9.74 us
    pallas_call x2, Pallas kernels, feature_values(): pl.pallas_call(feature_kernel, out_shape=jax.ShapeDtypeStruct(shape, BF16...  7.86 us
    dot_general x7, matrix products, contract(): lax.dot_general(left, right, (dims, ((), ())), preferred_element_type=F32)  7.65 us
    ppermute x5, waiting for transfers between devices, other_core(): return lax.ppermute(values, 'k', [(0, 1), (1, 0)])  7.44 us
  transfers between devices with their start and end apart: 11, of which 6 were waited for; matrix products, arithmetic and copies ran while one was open for 3% of the time, Pallas kernels for 5%

profile of v8, /device:TPU:6, one launch (start us, length us, event | category | flops | bytes accessed | tf_op | source)
XLA Modules:
  0.0 237.5 jit_solution(17523783462580849301)
XLA Ops:
  0.7 1.0 constant_dynamic-slice_fusion.2
  1.6 1.9 collective-permute-start
  3.7 1.0 collective-permute-done
  4.8 0.1 maximum_maximum_fusion.weights
  4.9 2.1 collective-permute-start.1
  7.1 29.0 %all_gather.21 = bf16[128,1536]{1,0:T(8,128)(2,1)S(1)} all-gather(bf16[32,1536]{1,0:T(8,128)(2,1)S(1)} %pad_maximum_fusion.1), channel_id=1, replica_groups=mesh['x'=4,'h'=2,'y'=4,'k'=2,'e'=2,'l'=4] {'h','e'}, dimensions={0}, use_global_device_ids=true | all-gather | bytes 491520 | tf_op jit(solution)/shard_map/all_gather | solution.py:39
  36.1 14.3 %all_gather.22 = bf16[512,768]{1,0:T(8,128)(2,1)S(1)} all-gather(bf16[128,768]{1,0:T(8,128)(2,1)S(1)} %get-tuple-element.45), channel_id=1, replica_groups=mesh['x'=4,'h'=2,'y'=4,'k'=2,'e'=2,'l'=4] {'x'}, dimensions={0}, use_global_device_ids=true | all-gather | bytes 983040 | tf_op jit(solution)/shard_map/all_gather | solution.py:39
  50.5 1.7 convolution_convert_fusion
  52.2 4.5 %all-to-all-start = ((bf16[4,128,768]{2,1,0:T(8,128)(2,1)}), bf16[4,128,768]{2,1,0:T(8,128)(2,1)}, u32[]{:S(2)}, u32[]{:S(2)}) async-start(bf16[4,128,768]{2,1,0:T(8,128)(2,1)} %bitcast.22), calls=%async_computation | async-start | bytes 1572864 | tf_op jit(solution)/shard_map/all_to_all | solution.py:33
  56.6 14.9 %all_gather.24 = bf16[512,768]{1,0:T(8,128)(2,1)} all-gather(bf16[128,768]{1,0:T(8,128)(2,1)S(1)} %get-tuple-element.25), channel_id=1, replica_groups=mesh['x'=4,'h'=2,'y'=4,'k'=2,'e'=2,'l'=4] {'x'}, dimensions={0}, use_global_device_ids=true | all-gather | bytes 983040 | tf_op jit(solution)/shard_map/all_gather | solution.py:39
  71.5 1.3 convert_reduce_fusion.1
  72.9 0.6 fusion.7
  73.5 1.5 add_convert_fusion
  75.0 4.9 %all-to-all-start.1 = ((bf16[4,128,768]{2,1,0:T(8,128)(2,1)}), bf16[4,128,768]{2,1,0:T(8,128)(2,1)S(1)}, u32[]{:S(2)}, u32[]{:S(2)}) async-start(bf16[4,128,768]{2,1,0:T(8,128)(2,1)} %bitcast.1), calls=%async_computation.1 | async-start | bytes 1572864 | tf_op jit(solution)/shard_map/all_to_all | solution.py:33
  79.9 0.8 convert_element_type.113
  80.7 17.0 %all_gather.23.act = bf16[512,768]{1,0:T(8,128)(2,1)S(1)} all-gather(bf16[128,768]{1,0:T(8,128)(2,1)S(1)} %multiply_convert_fusion.3), channel_id=1, replica_groups=mesh['x'=4,'h'=2,'y'=4,'k'=2,'e'=2,'l'=4] {'y'}, dimensions={0}, use_global_device_ids=true | all-gather | bytes 983040 | tf_op jit(solution)/shard_map/all_gather | solution.py:39
  97.7 1.0 convert_reduce_fusion
  98.7 0.6 convolution_convert_fusion.2
  99.3 1.9 collective-permute-start.2
  101.3 2.0 collective-permute-done.2
  103.2 1.4 multiply_convert_fusion.2
  104.7 4.0 %all-to-all-start.3 = ((bf16[4,192,384]{2,1,0:T(8,128)(2,1)}), bf16[4,192,384]{2,1,0:T(8,128)(2,1)S(1)}, u32[]{:S(2)}, u32[]{:S(2)}) async-start(bf16[4,192,384]{2,1,0:T(8,128)(2,1)} %bitcast.6), calls=%async_computation.3 | async-start | bytes 1179648 | tf_op jit(solution)/shard_map/all_to_all | solution.py:33
  108.7 0.2 fusion.14
  108.8 13.5 %all_gather.25.hidden = bf16[512,768]{1,0:T(8,128)(2,1)S(1)} all-gather(bf16[128,768]{1,0:T(8,128)(2,1)S(1)} %fusion.14), channel_id=1, replica_groups=mesh['x'=4,'h'=2,'y'=4,'k'=2,'e'=2,'l'=4] {'y'}, dimensions={0}, use_global_device_ids=true | all-gather | bytes 983040 | tf_op jit(solution)/shard_map/all_gather | solution.py:39
  122.4 0.5 convolution_convert_fusion.1
  122.9 1.9 collective-permute-start.3
  124.8 2.0 collective-permute-done.3
  126.8 1.3 multiply_convert_fusion.1
  128.1 5.4 %all-to-all-start.2 = ((bf16[4,96,768]{2,1,0:T(8,128)(2,1)}), bf16[4,96,768]{2,1,0:T(8,128)(2,1)S(1)}, u32[]{:S(2)}, u32[]{:S(2)}) async-start(bf16[4,96,768]{2,1,0:T(8,128)(2,1)} %bitcast.3), calls=%async_computation.2 | async-start | bytes 1179648 | tf_op jit(solution)/shard_map/all_to_all | solution.py:208
  133.5 3.7 %shard_map.75 = bf16[512,768]{1,0:T(8,128)(2,1)} custom-call(bf16[512,768]{1,0:T(8,128)(2,1)} %copy-done.1, bf16[512,768]{1,0:T(8,128)(2,1)} %copy-done.2, bf16[768,768]{1,0:T(8,128)(2,1)} %copy-done.3), custom_call_target="tpu_custom_call" | custom-call | flops 603979776 | bytes 3538944 | tf_op jit(solution)/shard_map/pallas_call | solution.py:75
  137.2 1.9 collective-permute-start.4
  139.1 2.5 %collective-permute-done.4.rest_0_ = bf16[512,768]{1,0:T(8,128)(2,1)S(1)} collective-permute-done((bf16[512,768]{1,0:T(8,128)(2,1)}, bf16[512,768]{1,0:T(8,128)(2,1)S(1)}, u32[]{:S(2)}, u32[]{:S(2)}) %collective-permute-start.4) | collective-permute-done | bytes 786464 | tf_op jit(solution)/shard_map/ppermute | solution.py:43
  141.6 0.9 copy-done.9
  142.5 4.2 %shard_map.76 = bf16[4,256,768]{2,1,0:T(8,128)(2,1)} custom-call(bf16[512,768]{1,0:T(8,128)(2,1)} %copy-done.1, bf16[512,768]{1,0:T(8,128)(2,1)} %copy-done.2, bf16[768,768]{1,0:T(8,128)(2,1)} %copy-done.4, bf16[512,768]{1,0:T(8,128)(2,1)} %copy-done.9), custom_call_target="tpu_custom_call" | custom-call | flops 603979776 | bytes 3538944 | tf_op jit(solution)/shard_map/pallas_call | solution.py:75
  146.7 0.1 reduce_sum.69
  146.7 3.0 %all-to-all-done.2 = bf16[4,96,768]{2,1,0:T(8,128)(2,1)S(1)} async-done(((bf16[4,96,768]{2,1,0:T(8,128)(2,1)}), bf16[4,96,768]{2,1,0:T(8,128)(2,1)S(1)}, u32[]{:S(2)}, u32[]{:S(2)}) %all-to-all-start.2) | async-done | bytes 589856 | tf_op jit(solution)/shard_map/all_to_all | solution.py:208
  149.7 0.1 reduce_sum.68
  149.8 0.6 fusion.5
  151.4 4.6 %all-to-all-start.4 = ((bf16[4,256,768]{2,1,0:T(8,128)(2,1)}), bf16[4,256,768]{2,1,0:T(8,128)(2,1)S(1)}, u32[]{:S(2)}, u32[]{:S(2)}) async-start(bf16[4,256,768]{2,1,0:T(8,128)(2,1)} %shard_map.76), calls=%async_computation.4 | async-start | bytes 3145728 | tf_op jit(solution)/shard_map/all_to_all | solution.py:33
  156.0 47.7 %all-gather.2 = f16[3136,384]{1,0:T(8,128)(2,1)} all-gather(f16[392,384]{1,0:T(8,128)(2,1)S(1)} %concatenate.34), channel_id=2, replica_groups={{0,2,4,6,7,5,3,1},{8,10,12,14,15,13,11,9},{16,18,20,22,23,21,19,17},{24..., dimensions={0}, use_global_device_ids=true | all-gather | bytes 2709504 | tf_op jit(solution)/shard_map/all_gather | solution.py:212
  203.7 0.4 reduce_sum.70
  204.2 0.8 copy.9
  204.9 7.1 %all-to-all-start.5 = ((bf16[4,64,768]{2,1,0:T(8,128)(2,1)}), bf16[4,64,768]{2,1,0:T(8,128)(2,1)S(1)}, u32[]{:S(2)}, u32[]{:S(2)}) async-start(bf16[4,64,768]{2,1,0:T(8,128)(2,1)} %bitcast.11), calls=%async_computation.5 | async-start | bytes 786432 | tf_op jit(solution)/shard_map/all_to_all | solution.py:33
  212.0 0.9 exponential_reduce_fusion
  212.9 4.2 %multiply_convert_fusion.pieces = bf16[8,384,384]{2,1,0:T(8,128)(2,1)} fusion(f32[8]{0:T(128)S(1)} %exponential_reduce_fusion, f16[8,392,384]{2,1,0:T(8,128)(2,1)} %bitcast.20), kind=kLoop, calls=%fused_computation | loop fusion | flops 3538944 | bytes 4718624 | tf_op jit(solution)/shard_map/convert_element_type | solution.py:97
  217.1 3.3 %shard_map.77 = (bf16[384,1536]{1,0:T(8,128)(2,1)}, bf16[1536,384]{1,0:T(8,128)(2,1)}) custom-call(bf16[8,384,384]{2,1,0:T(8,128)(2,1)} %multiply_convert_fusion.pieces), custom_call_target="tpu_custom_call" | custom-call | tf_op jit(solution)/shard_map/pallas_call | solution.py:130
  220.4 16.3 %all-to-all-done.5 = bf16[4,64,768]{2,1,0:T(8,128)(2,1)S(1)} async-done(((bf16[4,64,768]{2,1,0:T(8,128)(2,1)}), bf16[4,64,768]{2,1,0:T(8,128)(2,1)S(1)}, u32[]{:S(2)}, u32[]{:S(2)}) %all-to-all-start.5) | async-done | bytes 393248 | tf_op jit(solution)/shard_map/all_to_all | solution.py:33
  236.8 0.6 fusion.32
  (45 shorter events, 0.7 us)
Async XLA Ops:
  0.6 2.9 %copy-start = (bf16[1536,384]{1,0:T(8,128)(2,1)S(1)}, bf16[1536,384]{1,0:T(8,128)(2,1)}, u32[]{:S(2)}) copy-start(bf16[1536,384]{1,0:T(8,128)(2,1)} %param.6) | copy-start | bytes 3538948
  0.6 3.0 %copy-start.12 = (bf16[384,1536]{1,0:T(8,128)(2,1)S(1)}, bf16[384,1536]{1,0:T(8,128)(2,1)}, u32[]{:S(2)}) copy-start(bf16[384,1536]{1,0:T(8,128)(2,1)} %param.5) | copy-start | bytes 3538948
  1.6 3.1 %collective-permute-start = (bf16[32,768]{1,0:T(8,128)(2,1)S(1)}, bf16[32,768]{1,0:T(8,128)(2,1)S(1)}, u32[]{:S(2)}, u32[]{:S(2)}) collective-permute-start(bf16[32,768]{1,0:T(8,128)(2,1)S(1)} %pad_maximum_fusion.2), channel_id=1, source_target_pairs={{0,8},{8,0},{1,9},{9,1},{2,10},{10,2},{3,11},{11,3},{4,12},{12,4},... | collective-permute-start | bytes 147464 | tf_op jit(solution)/shard_map/ppermute | solution.py:43
  4.9 45.5 %copy-start.4 = (bf16[768,768]{1,0:T(8,128)(2,1)}, bf16[768,768]{1,0:T(8,128)(2,1)S(1)}, u32[]{:S(2)}) copy-start(bf16[768,768]{1,0:T(8,128)(2,1)S(1)} %maximum_maximum_fusion.weights) | copy-start | bytes 3538948
  4.9 45.5 %collective-permute-start.1 = (bf16[768,768]{1,0:T(8,128)(2,1)S(1)}, bf16[768,768]{1,0:T(8,128)(2,1)S(1)}, u32[]{:S(2)}, u32[]{:S(2)}) collective-permute-start(bf16[768,768]{1,0:T(8,128)(2,1)S(1)} %maximum_maximum_fusion.weights), channel_id=1, source_target_pairs={{0,8},{8,0},{1,9},{9,1},{2,10},{10,2},{3,11},{11,3},{4,12},{12,4},... | collective-permute-start | bytes 3538952 | tf_op jit(solution)/shard_map/ppermute | solution.py:43
  50.4 1.8 copy-start.10
  50.4 22.4 %copy-start.3 = (bf16[768,768]{1,0:T(8,128)(2,1)}, bf16[768,768]{1,0:T(8,128)(2,1)S(1)}, u32[]{:S(2)}) copy-start(bf16[768,768]{1,0:T(8,128)(2,1)S(1)} %collective-permute-done.1.weights) | copy-start | bytes 3538948
  52.2 19.4 %all-to-all-start = ((bf16[4,128,768]{2,1,0:T(8,128)(2,1)}), bf16[4,128,768]{2,1,0:T(8,128)(2,1)}, u32[]{:S(2)}, u32[]{:S(2)}) async-start(bf16[4,128,768]{2,1,0:T(8,128)(2,1)} %bitcast.22), calls=%async_computation | async-start | bytes 1572864 | tf_op jit(solution)/shard_map/all_to_all | solution.py:33
  71.5 1.4 copy-start.5
  75.0 22.7 %all-to-all-start.1 = ((bf16[4,128,768]{2,1,0:T(8,128)(2,1)}), bf16[4,128,768]{2,1,0:T(8,128)(2,1)S(1)}, u32[]{:S(2)}, u32[]{:S(2)}) async-start(bf16[4,128,768]{2,1,0:T(8,128)(2,1)} %bitcast.1), calls=%async_computation.1 | async-start | bytes 1572864 | tf_op jit(solution)/shard_map/all_to_all | solution.py:33
  80.6 18.1 %copy-start.6 = (bf16[512,768]{1,0:T(8,128)(2,1)S(1)}, bf16[512,768]{1,0:T(8,128)(2,1)}, u32[]{:S(2)}) copy-start(bf16[512,768]{1,0:T(8,128)(2,1)} %all_gather.24) | copy-start | bytes 2359300
  97.7 5.5 %copy-start.1 = (bf16[512,768]{1,0:T(8,128)(2,1)}, bf16[512,768]{1,0:T(8,128)(2,1)S(1)}, u32[]{:S(2)}) copy-start(bf16[512,768]{1,0:T(8,128)(2,1)S(1)} %all_gather.23.act) | copy-start | bytes 2359300
  99.3 3.9 %collective-permute-start.2 = (bf16[768,384]{1,0:T(8,128)(2,1)S(1)}, bf16[768,384]{1,0:T(8,128)(2,1)S(1)}, u32[]{:S(2)}, u32[]{:S(2)}) collective-permute-start(bf16[768,384]{1,0:T(8,128)(2,1)S(1)} %convolution_convert_fusion.2), channel_id=1, source_target_pairs={{0,8},{8,0},{1,9},{9,1},{2,10},{10,2},{3,11},{11,3},{4,12},{12,4},... | collective-permute-start | bytes 1769480 | tf_op jit(solution)/shard_map/ppermute | solution.py:43
  104.7 4.0 %copy-start.7 = (f32[128,768]{1,0:T(8,128)S(1)}, f32[128,768]{1,0:T(8,128)}, u32[]{:S(2)}) copy-start(f32[128,768]{1,0:T(8,128)} %convert_element_type.113) | copy-start | bytes 1179652
  104.7 4.0 %copy-start.8 = (f32[128,768]{1,0:T(8,128)S(1)}, f32[128,768]{1,0:T(8,128)}, u32[]{:S(2)}) copy-start(f32[128,768]{1,0:T(8,128)} %convert_reduce_fusion) | copy-start | bytes 1179652
  104.7 23.4 %all-to-all-start.3 = ((bf16[4,192,384]{2,1,0:T(8,128)(2,1)}), bf16[4,192,384]{2,1,0:T(8,128)(2,1)S(1)}, u32[]{:S(2)}, u32[]{:S(2)}) async-start(bf16[4,192,384]{2,1,0:T(8,128)(2,1)} %bitcast.6), calls=%async_computation.3 | async-start | bytes 1179648 | tf_op jit(solution)/shard_map/all_to_all | solution.py:33
  108.7 13.7 %copy-start.11 = (bf16[512,768]{1,0:T(8,128)(2,1)S(1)}, bf16[512,768]{1,0:T(8,128)(2,1)}, u32[]{:S(2)}) copy-start(bf16[512,768]{1,0:T(8,128)(2,1)} %copy-done.10) | copy-start | bytes 2359300
  122.4 5.7 %copy-start.2 = (bf16[512,768]{1,0:T(8,128)(2,1)}, bf16[512,768]{1,0:T(8,128)(2,1)S(1)}, u32[]{:S(2)}) copy-start(bf16[512,768]{1,0:T(8,128)(2,1)S(1)} %all_gather.25.hidden) | copy-start | bytes 2359300
  122.9 3.9 %collective-permute-start.3 = (bf16[384,768]{1,0:T(8,128)(2,1)S(1)}, bf16[384,768]{1,0:T(8,128)(2,1)S(1)}, u32[]{:S(2)}, u32[]{:S(2)}) collective-permute-start(bf16[384,768]{1,0:T(8,128)(2,1)S(1)} %convolution_convert_fusion.1), channel_id=1, source_target_pairs={{0,8},{8,0},{1,9},{9,1},{2,10},{10,2},{3,11},{11,3},{4,12},{12,4},... | collective-permute-start | bytes 1769480 | tf_op jit(solution)/shard_map/ppermute | solution.py:43
  128.1 21.6 %all-to-all-start.2 = ((bf16[4,96,768]{2,1,0:T(8,128)(2,1)}), bf16[4,96,768]{2,1,0:T(8,128)(2,1)S(1)}, u32[]{:S(2)}, u32[]{:S(2)}) async-start(bf16[4,96,768]{2,1,0:T(8,128)(2,1)} %bitcast.3), calls=%async_computation.2 | async-start | bytes 1179648 | tf_op jit(solution)/shard_map/all_to_all | solution.py:208
  137.2 4.4 %collective-permute-start.4 = (bf16[512,768]{1,0:T(8,128)(2,1)}, bf16[512,768]{1,0:T(8,128)(2,1)S(1)}, u32[]{:S(2)}, u32[]{:S(2)}) collective-permute-start(bf16[512,768]{1,0:T(8,128)(2,1)} %shard_map.75), channel_id=1, source_target_pairs={{0,8},{8,0},{1,9},{9,1},{2,10},{10,2},{3,11},{11,3},{4,12},{12,4},... | collective-permute-start | bytes 2359304 | tf_op jit(solution)/shard_map/ppermute | solution.py:43
  141.6 0.9 copy-start.9
  151.4 52.4 %all-to-all-start.4 = ((bf16[4,256,768]{2,1,0:T(8,128)(2,1)}), bf16[4,256,768]{2,1,0:T(8,128)(2,1)S(1)}, u32[]{:S(2)}, u32[]{:S(2)}) async-start(bf16[4,256,768]{2,1,0:T(8,128)(2,1)} %shard_map.76), calls=%async_computation.4 | async-start | bytes 3145728 | tf_op jit(solution)/shard_map/all_to_all | solution.py:33
  204.9 31.8 %all-to-all-start.5 = ((bf16[4,64,768]{2,1,0:T(8,128)(2,1)}), bf16[4,64,768]{2,1,0:T(8,128)(2,1)S(1)}, u32[]{:S(2)}, u32[]{:S(2)}) async-start(bf16[4,64,768]{2,1,0:T(8,128)(2,1)} %bitcast.11), calls=%async_computation.5 | async-start | bytes 786432 | tf_op jit(solution)/shard_map/all_to_all | solution.py:33

commit v9 on v6

--- a/solution.py
+++ b/solution.py
@@ -48,9 +48,16 @@
 
 
 def feature_kernel(act, hidden, weights, *rest):
-    out = rest[-1]
+    out = rest[0] if len(rest) == 1 else rest[1]
     features = weights.shape[1] // 2
     rows = act.shape[0] // 4
+    copies = []
+    if len(rest) == 3:
+        for block in range(4):
+            source, target = rest[0].at[pl.ds(block * rows, rows)], out.at[block, pl.ds(rows, rows)]
+            copies.append(pltpu.make_async_copy(source, target, rest[2].at[block]))
+    for copy in copies:
+        copy.start()
     low, high = pl.ds(0, features), pl.ds(features, features)
     for columns in (low, high):
         if columns is low:
@@ -64,17 +71,20 @@
         else:
             for block in range(4):
                 out[block, pl.ds(0, rows), columns] = values[block * rows : (block + 1) * rows]
-    if len(rest) == 2:
-        for block in range(4):
-            out[block, pl.ds(rows, rows)] = rest[0][pl.ds(block * rows, rows)]
+    for copy in copies:
+        copy.wait()
 
 
 def feature_values(act, hidden, weights, *more):
     rows, depth = act.shape
     shape = (4, rows // 2, depth) if more else (rows, depth)
+    vmem = pl.BlockSpec(memory_space=pltpu.VMEM)
     return pl.pallas_call(
         feature_kernel,
         out_shape=jax.ShapeDtypeStruct(shape, BF16),
+        in_specs=[vmem] * 3 + [pl.BlockSpec(memory_space=pl.ANY)] * len(more),
+        out_specs=vmem,
+        scratch_shapes=[pltpu.SemaphoreType.DMA((4,))] * len(more),
         cost_estimate=pl.CostEstimate(
             flops=2 * rows * depth * depth,
             bytes_accessed=6 * rows * depth + 2 * depth * depth,

time: 236 us -> 236 us (level)
  no operation moved by 1% of the time
where the time goes in v9:
time: 236 us; the launch traced here: 235 us
  blocking collectives  137 us (58%)
  starting transfers between devices  40.1 us (17%)
  waiting for transfers between devices  23.2 us (10%)
  Pallas kernels  11.1 us (5%)
  other arithmetic  9.93 us (4%)
  matrix products  7.65 us (3%)
  local copies, waits for them, and re-layouts  3.7 us (2%)
    all_gather x5, blocking collectives, gather(): return lax.all_gather(values, axis, axis=0, tiled=True)  88.7 us
    all_gather x1, blocking collectives, on_device(): pieces = lax.all_gather(packed, ('e', 'l'), axis_index_groups=[FOLDED])  48.7 us
    all_to_all x5, starting transfers between devices, scatter_sum(): parts = lax.all_to_all(values, axis, 0, 0, tiled=True)  24.9 us
    all_to_all x5, waiting for transfers between devices, scatter_sum(): parts = lax.all_to_all(values, axis, 0, 0, tiled=True)  12.7 us
    ppermute x5, starting transfers between devices, other_core(): return lax.ppermute(values, 'k', [(0, 1), (1, 0)])  9.74 us
    pallas_call x2, Pallas kernels, feature_values(): pl.pallas_call(feature_kernel, out_shape=jax.ShapeDtypeStruct(shape, BF16...  7.84 us
    dot_general x7, matrix products, contract(): lax.dot_general(left, right, (dims, ((), ())), preferred_element_type=F32)  7.65 us
    ppermute x5, waiting for transfers between devices, other_core(): return lax.ppermute(values, 'k', [(0, 1), (1, 0)])  7.44 us
  transfers between devices with their start and end apart: 11, of which 6 were waited for; matrix products, arithmetic and copies ran while one was open for 3% of the time, Pallas kernels for 5%

profile of v9, /device:TPU:6, one launch (start us, length us, event | category | flops | bytes accessed | tf_op | source)
XLA Modules:
  0.0 234.7 jit_solution(6582751016899298593)
XLA Ops:
  0.7 1.0 constant_dynamic-slice_fusion.2
  1.6 1.9 collective-permute-start
  3.7 1.0 collective-permute-done
  4.8 0.1 maximum_maximum_fusion.weights
  4.9 2.1 collective-permute-start.1
  7.1 29.0 %all_gather.21 = bf16[128,1536]{1,0:T(8,128)(2,1)S(1)} all-gather(bf16[32,1536]{1,0:T(8,128)(2,1)S(1)} %pad_maximum_fusion.1), channel_id=1, replica_groups=mesh['x'=4,'h'=2,'y'=4,'k'=2,'e'=2,'l'=4] {'h','e'}, dimensions={0}, use_global_device_ids=true | all-gather | bytes 491520 | tf_op jit(solution)/shard_map/all_gather | solution.py:39
  36.1 14.3 %all_gather.22 = bf16[512,768]{1,0:T(8,128)(2,1)S(1)} all-gather(bf16[128,768]{1,0:T(8,128)(2,1)S(1)} %get-tuple-element.45), channel_id=1, replica_groups=mesh['x'=4,'h'=2,'y'=4,'k'=2,'e'=2,'l'=4] {'x'}, dimensions={0}, use_global_device_ids=true | all-gather | bytes 983040 | tf_op jit(solution)/shard_map/all_gather | solution.py:39
  50.5 1.7 convolution_convert_fusion
  52.2 4.5 %all-to-all-start = ((bf16[4,128,768]{2,1,0:T(8,128)(2,1)}), bf16[4,128,768]{2,1,0:T(8,128)(2,1)}, u32[]{:S(2)}, u32[]{:S(2)}) async-start(bf16[4,128,768]{2,1,0:T(8,128)(2,1)} %bitcast.22), calls=%async_computation | async-start | bytes 1572864 | tf_op jit(solution)/shard_map/all_to_all | solution.py:33
  56.6 14.9 %all_gather.24 = bf16[512,768]{1,0:T(8,128)(2,1)} all-gather(bf16[128,768]{1,0:T(8,128)(2,1)S(1)} %get-tuple-element.25), channel_id=1, replica_groups=mesh['x'=4,'h'=2,'y'=4,'k'=2,'e'=2,'l'=4] {'x'}, dimensions={0}, use_global_device_ids=true | all-gather | bytes 983040 | tf_op jit(solution)/shard_map/all_gather | solution.py:39
  71.5 1.3 convert_reduce_fusion.1
  72.9 0.6 fusion.7
  73.5 1.5 add_convert_fusion
  75.0 4.9 %all-to-all-start.1 = ((bf16[4,128,768]{2,1,0:T(8,128)(2,1)}), bf16[4,128,768]{2,1,0:T(8,128)(2,1)S(1)}, u32[]{:S(2)}, u32[]{:S(2)}) async-start(bf16[4,128,768]{2,1,0:T(8,128)(2,1)} %bitcast.1), calls=%async_computation.1 | async-start | bytes 1572864 | tf_op jit(solution)/shard_map/all_to_all | solution.py:33
  79.9 0.8 convert_element_type.113
  80.7 17.0 %all_gather.23.act = bf16[512,768]{1,0:T(8,128)(2,1)S(1)} all-gather(bf16[128,768]{1,0:T(8,128)(2,1)S(1)} %multiply_convert_fusion.3), channel_id=1, replica_groups=mesh['x'=4,'h'=2,'y'=4,'k'=2,'e'=2,'l'=4] {'y'}, dimensions={0}, use_global_device_ids=true | all-gather | bytes 983040 | tf_op jit(solution)/shard_map/all_gather | solution.py:39
  97.7 1.0 convert_reduce_fusion
  98.7 0.6 convolution_convert_fusion.2
  99.3 1.9 collective-permute-start.2
  101.3 2.0 collective-permute-done.2
  103.2 1.4 multiply_convert_fusion.2
  104.7 4.0 %all-to-all-start.3 = ((bf16[4,192,384]{2,1,0:T(8,128)(2,1)}), bf16[4,192,384]{2,1,0:T(8,128)(2,1)S(1)}, u32[]{:S(2)}, u32[]{:S(2)}) async-start(bf16[4,192,384]{2,1,0:T(8,128)(2,1)} %bitcast.6), calls=%async_computation.3 | async-start | bytes 1179648 | tf_op jit(solution)/shard_map/all_to_all | solution.py:33
  108.7 0.2 fusion.14
  108.8 13.5 %all_gather.25.hidden = bf16[512,768]{1,0:T(8,128)(2,1)S(1)} all-gather(bf16[128,768]{1,0:T(8,128)(2,1)S(1)} %fusion.14), channel_id=1, replica_groups=mesh['x'=4,'h'=2,'y'=4,'k'=2,'e'=2,'l'=4] {'y'}, dimensions={0}, use_global_device_ids=true | all-gather | bytes 983040 | tf_op jit(solution)/shard_map/all_gather | solution.py:39
  122.4 0.5 convolution_convert_fusion.1
  122.9 1.9 collective-permute-start.3
  124.8 2.0 collective-permute-done.3
  126.8 1.3 multiply_convert_fusion.1
  128.1 5.4 %all-to-all-start.2 = ((bf16[4,96,768]{2,1,0:T(8,128)(2,1)}), bf16[4,96,768]{2,1,0:T(8,128)(2,1)S(1)}, u32[]{:S(2)}, u32[]{:S(2)}) async-start(bf16[4,96,768]{2,1,0:T(8,128)(2,1)} %bitcast.3), calls=%async_computation.2 | async-start | bytes 1179648 | tf_op jit(solution)/shard_map/all_to_all | solution.py:218
  133.5 3.7 %shard_map.75 = bf16[512,768]{1,0:T(8,128)(2,1)} custom-call(bf16[512,768]{1,0:T(8,128)(2,1)} %copy-done.1, bf16[512,768]{1,0:T(8,128)(2,1)} %copy-done.2, bf16[768,768]{1,0:T(8,128)(2,1)} %copy-done.3), custom_call_target="tpu_custom_call" | custom-call | flops 603979776 | bytes 3538944 | tf_op jit(solution)/shard_map/pallas_call | solution.py:82
  137.2 1.9 collective-permute-start.4
  139.1 2.5 %collective-permute-done.4.rest_0_ = bf16[512,768]{1,0:T(8,128)(2,1)S(1)} collective-permute-done((bf16[512,768]{1,0:T(8,128)(2,1)}, bf16[512,768]{1,0:T(8,128)(2,1)S(1)}, u32[]{:S(2)}, u32[]{:S(2)}) %collective-permute-start.4) | collective-permute-done | bytes 786464 | tf_op jit(solution)/shard_map/ppermute | solution.py:43
  141.6 0.9 copy-done.9
  142.5 4.1 %shard_map.76 = bf16[4,256,768]{2,1,0:T(8,128)(2,1)} custom-call(bf16[512,768]{1,0:T(8,128)(2,1)} %copy-done.1, bf16[512,768]{1,0:T(8,128)(2,1)} %copy-done.2, bf16[768,768]{1,0:T(8,128)(2,1)} %copy-done.4, bf16[512,768]{1,0:T(8,128)(2,1)} %copy-done.9), custom_call_target="tpu_custom_call" | custom-call | flops 603979776 | bytes 3538944 | tf_op jit(solution)/shard_map/pallas_call | solution.py:82
  146.6 0.1 reduce_sum.69
  146.7 3.0 %all-to-all-done.2 = bf16[4,96,768]{2,1,0:T(8,128)(2,1)S(1)} async-done(((bf16[4,96,768]{2,1,0:T(8,128)(2,1)}), bf16[4,96,768]{2,1,0:T(8,128)(2,1)S(1)}, u32[]{:S(2)}, u32[]{:S(2)}) %all-to-all-start.2) | async-done | bytes 589856 | tf_op jit(solution)/shard_map/all_to_all | solution.py:218
  149.7 0.1 reduce_sum.68
  149.8 0.6 fusion.5
  151.4 4.6 %all-to-all-start.4 = ((bf16[4,256,768]{2,1,0:T(8,128)(2,1)}), bf16[4,256,768]{2,1,0:T(8,128)(2,1)S(1)}, u32[]{:S(2)}, u32[]{:S(2)}) async-start(bf16[4,256,768]{2,1,0:T(8,128)(2,1)} %shard_map.76), calls=%async_computation.4 | async-start | bytes 3145728 | tf_op jit(solution)/shard_map/all_to_all | solution.py:33
  156.0 48.7 %all-gather.2 = f16[3200,384]{1,0:T(8,128)(2,1)} all-gather(f16[400,384]{1,0:T(8,128)(2,1)S(1)} %concatenate.34), channel_id=2, replica_groups={{0,2,4,6,7,5,3,1},{8,10,12,14,15,13,11,9},{16,18,20,22,23,21,19,17},{24..., dimensions={0}, use_global_device_ids=true | all-gather | bytes 2764800 | tf_op jit(solution)/shard_map/all_gather | solution.py:222
  204.6 0.4 reduce_sum.70
  205.1 0.8 copy.9
  205.9 7.0 %all-to-all-start.5 = ((bf16[4,64,768]{2,1,0:T(8,128)(2,1)}), bf16[4,64,768]{2,1,0:T(8,128)(2,1)S(1)}, u32[]{:S(2)}, u32[]{:S(2)}) async-start(bf16[4,64,768]{2,1,0:T(8,128)(2,1)} %bitcast.11), calls=%async_computation.5 | async-start | bytes 786432 | tf_op jit(solution)/shard_map/all_to_all | solution.py:33
  212.9 0.9 exponential_reduce_fusion
  213.7 4.2 %multiply_convert_fusion.pieces = bf16[8,384,384]{2,1,0:T(8,128)(2,1)} fusion(f32[8]{0:T(128)S(1)} %exponential_reduce_fusion, f16[8,400,384]{2,1,0:T(8,128)(2,1)} %bitcast.20), kind=kLoop, calls=%fused_computation | loop fusion | flops 3538944 | bytes 4718624 | tf_op jit(solution)/shard_map/convert_element_type | solution.py:107
  217.9 3.3 %shard_map.77 = (bf16[384,1536]{1,0:T(8,128)(2,1)}, bf16[1536,384]{1,0:T(8,128)(2,1)}) custom-call(bf16[8,384,384]{2,1,0:T(8,128)(2,1)} %multiply_convert_fusion.pieces), custom_call_target="tpu_custom_call" | custom-call | tf_op jit(solution)/shard_map/pallas_call | solution.py:140
  221.3 12.7 %all-to-all-done.5 = bf16[4,64,768]{2,1,0:T(8,128)(2,1)S(1)} async-done(((bf16[4,64,768]{2,1,0:T(8,128)(2,1)}), bf16[4,64,768]{2,1,0:T(8,128)(2,1)S(1)}, u32[]{:S(2)}, u32[]{:S(2)}) %all-to-all-start.5) | async-done | bytes 393248 | tf_op jit(solution)/shard_map/all_to_all | solution.py:33
  234.1 0.6 fusion.32
  (45 shorter events, 0.7 us)
Async XLA Ops:
  0.6 2.9 %copy-start = (bf16[1536,384]{1,0:T(8,128)(2,1)S(1)}, bf16[1536,384]{1,0:T(8,128)(2,1)}, u32[]{:S(2)}) copy-start(bf16[1536,384]{1,0:T(8,128)(2,1)} %param.6) | copy-start | bytes 3538948
  0.6 3.0 %copy-start.12 = (bf16[384,1536]{1,0:T(8,128)(2,1)S(1)}, bf16[384,1536]{1,0:T(8,128)(2,1)}, u32[]{:S(2)}) copy-start(bf16[384,1536]{1,0:T(8,128)(2,1)} %param.5) | copy-start | bytes 3538948
  1.6 3.1 %collective-permute-start = (bf16[32,768]{1,0:T(8,128)(2,1)S(1)}, bf16[32,768]{1,0:T(8,128)(2,1)S(1)}, u32[]{:S(2)}, u32[]{:S(2)}) collective-permute-start(bf16[32,768]{1,0:T(8,128)(2,1)S(1)} %pad_maximum_fusion.2), channel_id=1, source_target_pairs={{0,8},{8,0},{1,9},{9,1},{2,10},{10,2},{3,11},{11,3},{4,12},{12,4},... | collective-permute-start | bytes 147464 | tf_op jit(solution)/shard_map/ppermute | solution.py:43
  4.9 45.5 %copy-start.4 = (bf16[768,768]{1,0:T(8,128)(2,1)}, bf16[768,768]{1,0:T(8,128)(2,1)S(1)}, u32[]{:S(2)}) copy-start(bf16[768,768]{1,0:T(8,128)(2,1)S(1)} %maximum_maximum_fusion.weights) | copy-start | bytes 3538948
  4.9 45.5 %collective-permute-start.1 = (bf16[768,768]{1,0:T(8,128)(2,1)S(1)}, bf16[768,768]{1,0:T(8,128)(2,1)S(1)}, u32[]{:S(2)}, u32[]{:S(2)}) collective-permute-start(bf16[768,768]{1,0:T(8,128)(2,1)S(1)} %maximum_maximum_fusion.weights), channel_id=1, source_target_pairs={{0,8},{8,0},{1,9},{9,1},{2,10},{10,2},{3,11},{11,3},{4,12},{12,4},... | collective-permute-start | bytes 3538952 | tf_op jit(solution)/shard_map/ppermute | solution.py:43
  50.4 1.8 copy-start.10
  50.4 22.4 %copy-start.3 = (bf16[768,768]{1,0:T(8,128)(2,1)}, bf16[768,768]{1,0:T(8,128)(2,1)S(1)}, u32[]{:S(2)}) copy-start(bf16[768,768]{1,0:T(8,128)(2,1)S(1)} %collective-permute-done.1.weights) | copy-start | bytes 3538948
  52.2 19.4 %all-to-all-start = ((bf16[4,128,768]{2,1,0:T(8,128)(2,1)}), bf16[4,128,768]{2,1,0:T(8,128)(2,1)}, u32[]{:S(2)}, u32[]{:S(2)}) async-start(bf16[4,128,768]{2,1,0:T(8,128)(2,1)} %bitcast.22), calls=%async_computation | async-start | bytes 1572864 | tf_op jit(solution)/shard_map/all_to_all | solution.py:33
  71.5 1.4 copy-start.5
  75.0 22.7 %all-to-all-start.1 = ((bf16[4,128,768]{2,1,0:T(8,128)(2,1)}), bf16[4,128,768]{2,1,0:T(8,128)(2,1)S(1)}, u32[]{:S(2)}, u32[]{:S(2)}) async-start(bf16[4,128,768]{2,1,0:T(8,128)(2,1)} %bitcast.1), calls=%async_computation.1 | async-start | bytes 1572864 | tf_op jit(solution)/shard_map/all_to_all | solution.py:33
  80.6 18.1 %copy-start.6 = (bf16[512,768]{1,0:T(8,128)(2,1)S(1)}, bf16[512,768]{1,0:T(8,128)(2,1)}, u32[]{:S(2)}) copy-start(bf16[512,768]{1,0:T(8,128)(2,1)} %all_gather.24) | copy-start | bytes 2359300
  97.7 5.5 %copy-start.1 = (bf16[512,768]{1,0:T(8,128)(2,1)}, bf16[512,768]{1,0:T(8,128)(2,1)S(1)}, u32[]{:S(2)}) copy-start(bf16[512,768]{1,0:T(8,128)(2,1)S(1)} %all_gather.23.act) | copy-start | bytes 2359300
  99.3 3.9 %collective-permute-start.2 = (bf16[768,384]{1,0:T(8,128)(2,1)S(1)}, bf16[768,384]{1,0:T(8,128)(2,1)S(1)}, u32[]{:S(2)}, u32[]{:S(2)}) collective-permute-start(bf16[768,384]{1,0:T(8,128)(2,1)S(1)} %convolution_convert_fusion.2), channel_id=1, source_target_pairs={{0,8},{8,0},{1,9},{9,1},{2,10},{10,2},{3,11},{11,3},{4,12},{12,4},... | collective-permute-start | bytes 1769480 | tf_op jit(solution)/shard_map/ppermute | solution.py:43
  104.7 4.0 %copy-start.7 = (f32[128,768]{1,0:T(8,128)S(1)}, f32[128,768]{1,0:T(8,128)}, u32[]{:S(2)}) copy-start(f32[128,768]{1,0:T(8,128)} %convert_element_type.113) | copy-start | bytes 1179652
  104.7 4.0 %copy-start.8 = (f32[128,768]{1,0:T(8,128)S(1)}, f32[128,768]{1,0:T(8,128)}, u32[]{:S(2)}) copy-start(f32[128,768]{1,0:T(8,128)} %convert_reduce_fusion) | copy-start | bytes 1179652
  104.7 23.4 %all-to-all-start.3 = ((bf16[4,192,384]{2,1,0:T(8,128)(2,1)}), bf16[4,192,384]{2,1,0:T(8,128)(2,1)S(1)}, u32[]{:S(2)}, u32[]{:S(2)}) async-start(bf16[4,192,384]{2,1,0:T(8,128)(2,1)} %bitcast.6), calls=%async_computation.3 | async-start | bytes 1179648 | tf_op jit(solution)/shard_map/all_to_all | solution.py:33
  108.7 13.7 %copy-start.11 = (bf16[512,768]{1,0:T(8,128)(2,1)S(1)}, bf16[512,768]{1,0:T(8,128)(2,1)}, u32[]{:S(2)}) copy-start(bf16[512,768]{1,0:T(8,128)(2,1)} %copy-done.10) | copy-start | bytes 2359300
  122.4 5.7 %copy-start.2 = (bf16[512,768]{1,0:T(8,128)(2,1)}, bf16[512,768]{1,0:T(8,128)(2,1)S(1)}, u32[]{:S(2)}) copy-start(bf16[512,768]{1,0:T(8,128)(2,1)S(1)} %all_gather.25.hidden) | copy-start | bytes 2359300
  122.9 3.9 %collective-permute-start.3 = (bf16[384,768]{1,0:T(8,128)(2,1)S(1)}, bf16[384,768]{1,0:T(8,128)(2,1)S(1)}, u32[]{:S(2)}, u32[]{:S(2)}) collective-permute-start(bf16[384,768]{1,0:T(8,128)(2,1)S(1)} %convolution_convert_fusion.1), channel_id=1, source_target_pairs={{0,8},{8,0},{1,9},{9,1},{2,10},{10,2},{3,11},{11,3},{4,12},{12,4},... | collective-permute-start | bytes 1769480 | tf_op jit(solution)/shard_map/ppermute | solution.py:43
  128.1 21.6 %all-to-all-start.2 = ((bf16[4,96,768]{2,1,0:T(8,128)(2,1)}), bf16[4,96,768]{2,1,0:T(8,128)(2,1)S(1)}, u32[]{:S(2)}, u32[]{:S(2)}) async-start(bf16[4,96,768]{2,1,0:T(8,128)(2,1)} %bitcast.3), calls=%async_computation.2 | async-start | bytes 1179648 | tf_op jit(solution)/shard_map/all_to_all | solution.py:218
  137.2 4.4 %collective-permute-start.4 = (bf16[512,768]{1,0:T(8,128)(2,1)}, bf16[512,768]{1,0:T(8,128)(2,1)S(1)}, u32[]{:S(2)}, u32[]{:S(2)}) collective-permute-start(bf16[512,768]{1,0:T(8,128)(2,1)} %shard_map.75), channel_id=1, source_target_pairs={{0,8},{8,0},{1,9},{9,1},{2,10},{10,2},{3,11},{11,3},{4,12},{12,4},... | collective-permute-start | bytes 2359304 | tf_op jit(solution)/shard_map/ppermute | solution.py:43
  141.6 0.9 copy-start.9
  151.4 53.3 %all-to-all-start.4 = ((bf16[4,256,768]{2,1,0:T(8,128)(2,1)}), bf16[4,256,768]{2,1,0:T(8,128)(2,1)S(1)}, u32[]{:S(2)}, u32[]{:S(2)}) async-start(bf16[4,256,768]{2,1,0:T(8,128)(2,1)} %shard_map.76), calls=%async_computation.4 | async-start | bytes 3145728 | tf_op jit(solution)/shard_map/all_to_all | solution.py:33
  205.9 28.1 %all-to-all-start.5 = ((bf16[4,64,768]{2,1,0:T(8,128)(2,1)}), bf16[4,64,768]{2,1,0:T(8,128)(2,1)S(1)}, u32[]{:S(2)}, u32[]{:S(2)}) async-start(bf16[4,64,768]{2,1,0:T(8,128)(2,1)} %bitcast.11), calls=%async_computation.5 | async-start | bytes 786432 | tf_op jit(solution)/shard_map/all_to_all | solution.py:33

commit v10 on v9

--- a/solution.py
+++ b/solution.py
@@ -50,10 +50,10 @@
 def feature_kernel(act, hidden, weights, *rest):
     out = rest[0] if len(rest) == 1 else rest[1]
     features = weights.shape[1] // 2
-    rows = act.shape[0] // 4
+    rows = act.shape[0] // 16
     copies = []
     if len(rest) == 3:
-        for block in range(4):
+        for block in range(16):
             source, target = rest[0].at[pl.ds(block * rows, rows)], out.at[block, pl.ds(rows, rows)]
             copies.append(pltpu.make_async_copy(source, target, rest[2].at[block]))
     for copy in copies:
@@ -69,7 +69,7 @@
         if len(rest) == 1:
             out[:, columns] = values
         else:
-            for block in range(4):
+            for block in range(16):
                 out[block, pl.ds(0, rows), columns] = values[block * rows : (block + 1) * rows]
     for copy in copies:
         copy.wait()
@@ -77,14 +77,14 @@
 
 def feature_values(act, hidden, weights, *more):
     rows, depth = act.shape
-    shape = (4, rows // 2, depth) if more else (rows, depth)
+    shape = (16, rows // 8, depth) if more else (rows, depth)
     vmem = pl.BlockSpec(memory_space=pltpu.VMEM)
     return pl.pallas_call(
         feature_kernel,
         out_shape=jax.ShapeDtypeStruct(shape, BF16),
         in_specs=[vmem] * 3 + [pl.BlockSpec(memory_space=pl.ANY)] * len(more),
         out_specs=vmem,
-        scratch_shapes=[pltpu.SemaphoreType.DMA((4,))] * len(more),
+        scratch_shapes=[pltpu.SemaphoreType.DMA((16,))] * len(more),
         cost_estimate=pl.CostEstimate(
             flops=2 * rows * depth * depth,
             bytes_accessed=6 * rows * depth + 2 * depth * depth,
@@ -224,8 +224,7 @@
         (scatter_sum(after(total, packed), "x").astype(BF16), pieces)
     )
     up_grad, down_grad = place(unpack(pieces))
-    total = total.reshape(2, 4, own // 2, 2 * features).transpose(1, 0, 2, 3)
-    total = scatter_sum(total.reshape(4 * own, 2 * features), ("h", "e")).astype(BF16)
+    total = scatter_sum(total, ("h", "e")).astype(BF16)
     total = after(total, (up_grad, down_grad))
     swapped = jnp.concatenate([total[own // 2 :], total[: own // 2]], axis=0)
     total = jnp.where(side == 0, total, swapped)

time: 236 us -> 239 us (1.013); the launches traced: 235 us -> 235 us
  no operation moved by 1% of the time
where the time goes in v10:
time: 239 us; the launch traced here: 235 us
  blocking collectives  137 us (57%)
  starting transfers between devices  40.1 us (17%)
  waiting for transfers between devices  23.1 us (10%)
  Pallas kernels  11.1 us (5%)
  other arithmetic  10.6 us (4%)
  matrix products  7.65 us (3%)
  local copies, waits for them, and re-layouts  2.93 us (1%)
    all_gather x5, blocking collectives, gather(): return lax.all_gather(values, axis, axis=0, tiled=True)  88.7 us
    all_gather x1, blocking collectives, on_device(): pieces = lax.all_gather(packed, ('e', 'l'), axis_index_groups=[FOLDED])  48.7 us
    all_to_all x5, starting transfers between devices, scatter_sum(): parts = lax.all_to_all(values, axis, 0, 0, tiled=True)  24.9 us
    all_to_all x5, waiting for transfers between devices, scatter_sum(): parts = lax.all_to_all(values, axis, 0, 0, tiled=True)  12.7 us
    ppermute x5, starting transfers between devices, other_core(): return lax.ppermute(values, 'k', [(0, 1), (1, 0)])  9.74 us
    pallas_call x2, Pallas kernels, feature_values(): pl.pallas_call(feature_kernel, out_shape=jax.ShapeDtypeStruct(shape, BF16...  7.84 us
    dot_general x7, matrix products, contract(): lax.dot_general(left, right, (dims, ((), ())), preferred_element_type=F32)  7.65 us
    ppermute x5, waiting for transfers between devices, other_core(): return lax.ppermute(values, 'k', [(0, 1), (1, 0)])  7.44 us
  transfers between devices with their start and end apart: 11, of which 6 were waited for; matrix products, arithmetic and copies ran while one was open for 3% of the time, Pallas kernels for 5%

profile of v10, /device:TPU:6, one launch (start us, length us, event | category | flops | bytes accessed | tf_op | source)
XLA Modules:
  0.0 234.6 jit_solution(14794414749153742424)
XLA Ops:
  0.7 1.0 constant_dynamic-slice_fusion.2
  1.6 1.9 collective-permute-start
  3.7 1.0 collective-permute-done
  4.8 0.1 maximum_maximum_fusion.weights
  4.9 2.1 collective-permute-start.1
  7.1 29.0 %all_gather.21 = bf16[128,1536]{1,0:T(8,128)(2,1)S(1)} all-gather(bf16[32,1536]{1,0:T(8,128)(2,1)S(1)} %pad_maximum_fusion.1), channel_id=1, replica_groups=mesh['x'=4,'h'=2,'y'=4,'k'=2,'e'=2,'l'=4] {'h','e'}, dimensions={0}, use_global_device_ids=true | all-gather | bytes 491520 | tf_op jit(solution)/shard_map/all_gather | solution.py:39
  36.1 14.3 %all_gather.22 = bf16[512,768]{1,0:T(8,128)(2,1)S(1)} all-gather(bf16[128,768]{1,0:T(8,128)(2,1)S(1)} %get-tuple-element.45), channel_id=1, replica_groups=mesh['x'=4,'h'=2,'y'=4,'k'=2,'e'=2,'l'=4] {'x'}, dimensions={0}, use_global_device_ids=true | all-gather | bytes 983040 | tf_op jit(solution)/shard_map/all_gather | solution.py:39
  50.5 1.7 convolution_convert_fusion
  52.2 4.5 %all-to-all-start = ((bf16[4,128,768]{2,1,0:T(8,128)(2,1)}), bf16[4,128,768]{2,1,0:T(8,128)(2,1)}, u32[]{:S(2)}, u32[]{:S(2)}) async-start(bf16[4,128,768]{2,1,0:T(8,128)(2,1)} %bitcast.19), calls=%async_computation | async-start | bytes 1572864 | tf_op jit(solution)/shard_map/all_to_all | solution.py:33
  56.6 14.9 %all_gather.24 = bf16[512,768]{1,0:T(8,128)(2,1)} all-gather(bf16[128,768]{1,0:T(8,128)(2,1)S(1)} %get-tuple-element.25), channel_id=1, replica_groups=mesh['x'=4,'h'=2,'y'=4,'k'=2,'e'=2,'l'=4] {'x'}, dimensions={0}, use_global_device_ids=true | all-gather | bytes 983040 | tf_op jit(solution)/shard_map/all_gather | solution.py:39
  71.5 1.3 convert_reduce_fusion.1
  72.9 0.6 fusion.7
  73.5 1.5 add_convert_fusion
  75.0 4.9 %all-to-all-start.1 = ((bf16[4,128,768]{2,1,0:T(8,128)(2,1)}), bf16[4,128,768]{2,1,0:T(8,128)(2,1)S(1)}, u32[]{:S(2)}, u32[]{:S(2)}) async-start(bf16[4,128,768]{2,1,0:T(8,128)(2,1)} %bitcast.1), calls=%async_computation.1 | async-start | bytes 1572864 | tf_op jit(solution)/shard_map/all_to_all | solution.py:33
  79.9 0.8 convert_element_type.113
  80.6 0.1 multiply_convert_fusion.3
  80.7 17.0 %all_gather.23.act = bf16[512,768]{1,0:T(8,128)(2,1)S(1)} all-gather(bf16[128,768]{1,0:T(8,128)(2,1)S(1)} %multiply_convert_fusion.3), channel_id=1, replica_groups=mesh['x'=4,'h'=2,'y'=4,'k'=2,'e'=2,'l'=4] {'y'}, dimensions={0}, use_global_device_ids=true | all-gather | bytes 983040 | tf_op jit(solution)/shard_map/all_gather | solution.py:39
  97.7 1.0 convert_reduce_fusion
  98.7 0.6 convolution_convert_fusion.2
  99.3 1.9 collective-permute-start.2
  101.3 2.0 collective-permute-done.2
  103.2 1.4 multiply_convert_fusion.2
  104.7 4.0 %all-to-all-start.3 = ((bf16[4,192,384]{2,1,0:T(8,128)(2,1)}), bf16[4,192,384]{2,1,0:T(8,128)(2,1)S(1)}, u32[]{:S(2)}, u32[]{:S(2)}) async-start(bf16[4,192,384]{2,1,0:T(8,128)(2,1)} %bitcast.6), calls=%async_computation.3 | async-start | bytes 1179648 | tf_op jit(solution)/shard_map/all_to_all | solution.py:33
  108.7 0.2 fusion.14
  108.8 13.5 %all_gather.25.hidden = bf16[512,768]{1,0:T(8,128)(2,1)S(1)} all-gather(bf16[128,768]{1,0:T(8,128)(2,1)S(1)} %fusion.14), channel_id=1, replica_groups=mesh['x'=4,'h'=2,'y'=4,'k'=2,'e'=2,'l'=4] {'y'}, dimensions={0}, use_global_device_ids=true | all-gather | bytes 983040 | tf_op jit(solution)/shard_map/all_gather | solution.py:39
  122.4 0.5 convolution_convert_fusion.1
  122.9 1.9 collective-permute-start.3
  124.8 2.0 collective-permute-done.3
  126.8 1.3 multiply_convert_fusion.1
  128.1 5.4 %all-to-all-start.2 = ((bf16[4,96,768]{2,1,0:T(8,128)(2,1)}), bf16[4,96,768]{2,1,0:T(8,128)(2,1)S(1)}, u32[]{:S(2)}, u32[]{:S(2)}) async-start(bf16[4,96,768]{2,1,0:T(8,128)(2,1)} %bitcast.3), calls=%async_computation.2 | async-start | bytes 1179648 | tf_op jit(solution)/shard_map/all_to_all | solution.py:218
  133.5 3.7 %shard_map.75 = bf16[512,768]{1,0:T(8,128)(2,1)} custom-call(bf16[512,768]{1,0:T(8,128)(2,1)} %copy-done.1, bf16[512,768]{1,0:T(8,128)(2,1)} %copy-done.2, bf16[768,768]{1,0:T(8,128)(2,1)} %copy-done.3), custom_call_target="tpu_custom_call" | custom-call | flops 603979776 | bytes 3538944 | tf_op jit(solution)/shard_map/pallas_call | solution.py:82
  137.2 1.9 collective-permute-start.4
  139.1 2.5 %collective-permute-done.4.rest_0_ = bf16[512,768]{1,0:T(8,128)(2,1)S(1)} collective-permute-done((bf16[512,768]{1,0:T(8,128)(2,1)}, bf16[512,768]{1,0:T(8,128)(2,1)S(1)}, u32[]{:S(2)}, u32[]{:S(2)}) %collective-permute-start.4) | collective-permute-done | bytes 786464 | tf_op jit(solution)/shard_map/ppermute | solution.py:43
  141.6 0.9 copy-done.9
  142.5 4.2 %shard_map.76 = bf16[16,64,768]{2,1,0:T(8,128)(2,1)} custom-call(bf16[512,768]{1,0:T(8,128)(2,1)} %copy-done.1, bf16[512,768]{1,0:T(8,128)(2,1)} %copy-done.2, bf16[768,768]{1,0:T(8,128)(2,1)} %copy-done.4, bf16[512,768]{1,0:T(8,128)(2,1)} %copy-done.9), custom_call_target="tpu_custom_call" | custom-call | flops 603979776 | bytes 3538944 | tf_op jit(solution)/shard_map/pallas_call | solution.py:82
  146.7 0.1 reduce_sum.69
  146.7 3.0 %all-to-all-done.2 = bf16[4,96,768]{2,1,0:T(8,128)(2,1)S(1)} async-done(((bf16[4,96,768]{2,1,0:T(8,128)(2,1)}), bf16[4,96,768]{2,1,0:T(8,128)(2,1)S(1)}, u32[]{:S(2)}, u32[]{:S(2)}) %all-to-all-start.2) | async-done | bytes 589856 | tf_op jit(solution)/shard_map/all_to_all | solution.py:218
  149.7 0.1 reduce_sum.68
  149.8 0.6 fusion.5
  151.4 4.6 %all-to-all-start.4 = ((bf16[4,256,768]{2,1,0:T(8,128)(2,1)}), bf16[4,256,768]{2,1,0:T(8,128)(2,1)S(1)}, u32[]{:S(2)}, u32[]{:S(2)}) async-start(bf16[4,256,768]{2,1,0:T(8,128)(2,1)} %bitcast.18), calls=%async_computation.4 | async-start | bytes 3145728 | tf_op jit(solution)/shard_map/all_to_all | solution.py:33
  156.0 48.7 %all-gather.2 = f16[3200,384]{1,0:T(8,128)(2,1)} all-gather(f16[400,384]{1,0:T(8,128)(2,1)S(1)} %concatenate.34), channel_id=2, replica_groups={{0,2,4,6,7,5,3,1},{8,10,12,14,15,13,11,9},{16,18,20,22,23,21,19,17},{24..., dimensions={0}, use_global_device_ids=true | all-gather | bytes 2764800 | tf_op jit(solution)/shard_map/all_gather | solution.py:222
  204.7 1.1 reduce_sum.70
  205.7 7.0 %all-to-all-start.5 = ((bf16[4,64,768]{2,1,0:T(8,128)(2,1)}), bf16[4,64,768]{2,1,0:T(8,128)(2,1)S(1)}, u32[]{:S(2)}, u32[]{:S(2)}) async-start(bf16[4,64,768]{2,1,0:T(8,128)(2,1)} %bitcast.9), calls=%async_computation.5 | async-start | bytes 786432 | tf_op jit(solution)/shard_map/all_to_all | solution.py:33
  212.8 0.9 exponential_reduce_fusion
  213.6 4.2 %multiply_convert_fusion.pieces = bf16[8,384,384]{2,1,0:T(8,128)(2,1)} fusion(f32[8]{0:T(128)S(1)} %exponential_reduce_fusion, f16[8,400,384]{2,1,0:T(8,128)(2,1)} %bitcast.17), kind=kLoop, calls=%fused_computation | loop fusion | flops 3538944 | bytes 4718624 | tf_op jit(solution)/shard_map/convert_element_type | solution.py:107
  217.8 3.3 %shard_map.77 = (bf16[384,1536]{1,0:T(8,128)(2,1)}, bf16[1536,384]{1,0:T(8,128)(2,1)}) custom-call(bf16[8,384,384]{2,1,0:T(8,128)(2,1)} %multiply_convert_fusion.pieces), custom_call_target="tpu_custom_call" | custom-call | tf_op jit(solution)/shard_map/pallas_call | solution.py:140
  221.1 12.7 %all-to-all-done.5 = bf16[4,64,768]{2,1,0:T(8,128)(2,1)S(1)} async-done(((bf16[4,64,768]{2,1,0:T(8,128)(2,1)}), bf16[4,64,768]{2,1,0:T(8,128)(2,1)S(1)}, u32[]{:S(2)}, u32[]{:S(2)}) %all-to-all-start.5) | async-done | bytes 393248 | tf_op jit(solution)/shard_map/all_to_all | solution.py:33
  234.0 0.6 fusion.32
  (44 shorter events, 0.6 us)
Async XLA Ops:
  0.6 2.9 %copy-start = (bf16[1536,384]{1,0:T(8,128)(2,1)S(1)}, bf16[1536,384]{1,0:T(8,128)(2,1)}, u32[]{:S(2)}) copy-start(bf16[1536,384]{1,0:T(8,128)(2,1)} %param.6) | copy-start | bytes 3538948
  0.6 3.0 %copy-start.12 = (bf16[384,1536]{1,0:T(8,128)(2,1)S(1)}, bf16[384,1536]{1,0:T(8,128)(2,1)}, u32[]{:S(2)}) copy-start(bf16[384,1536]{1,0:T(8,128)(2,1)} %param.5) | copy-start | bytes 3538948
  1.6 3.1 %collective-permute-start = (bf16[32,768]{1,0:T(8,128)(2,1)S(1)}, bf16[32,768]{1,0:T(8,128)(2,1)S(1)}, u32[]{:S(2)}, u32[]{:S(2)}) collective-permute-start(bf16[32,768]{1,0:T(8,128)(2,1)S(1)} %pad_maximum_fusion.2), channel_id=1, source_target_pairs={{0,8},{8,0},{1,9},{9,1},{2,10},{10,2},{3,11},{11,3},{4,12},{12,4},... | collective-permute-start | bytes 147464 | tf_op jit(solution)/shard_map/ppermute | solution.py:43
  4.9 45.5 %copy-start.4 = (bf16[768,768]{1,0:T(8,128)(2,1)}, bf16[768,768]{1,0:T(8,128)(2,1)S(1)}, u32[]{:S(2)}) copy-start(bf16[768,768]{1,0:T(8,128)(2,1)S(1)} %maximum_maximum_fusion.weights) | copy-start | bytes 3538948
  4.9 45.5 %collective-permute-start.1 = (bf16[768,768]{1,0:T(8,128)(2,1)S(1)}, bf16[768,768]{1,0:T(8,128)(2,1)S(1)}, u32[]{:S(2)}, u32[]{:S(2)}) collective-permute-start(bf16[768,768]{1,0:T(8,128)(2,1)S(1)} %maximum_maximum_fusion.weights), channel_id=1, source_target_pairs={{0,8},{8,0},{1,9},{9,1},{2,10},{10,2},{3,11},{11,3},{4,12},{12,4},... | collective-permute-start | bytes 3538952 | tf_op jit(solution)/shard_map/ppermute | solution.py:43
  50.4 1.8 copy-start.10
  50.4 22.4 %copy-start.3 = (bf16[768,768]{1,0:T(8,128)(2,1)}, bf16[768,768]{1,0:T(8,128)(2,1)S(1)}, u32[]{:S(2)}) copy-start(bf16[768,768]{1,0:T(8,128)(2,1)S(1)} %collective-permute-done.1.weights) | copy-start | bytes 3538948
  52.2 19.4 %all-to-all-start = ((bf16[4,128,768]{2,1,0:T(8,128)(2,1)}), bf16[4,128,768]{2,1,0:T(8,128)(2,1)}, u32[]{:S(2)}, u32[]{:S(2)}) async-start(bf16[4,128,768]{2,1,0:T(8,128)(2,1)} %bitcast.19), calls=%async_computation | async-start | bytes 1572864 | tf_op jit(solution)/shard_map/all_to_all | solution.py:33
  71.5 1.4 copy-start.5
  75.0 22.7 %all-to-all-start.1 = ((bf16[4,128,768]{2,1,0:T(8,128)(2,1)}), bf16[4,128,768]{2,1,0:T(8,128)(2,1)S(1)}, u32[]{:S(2)}, u32[]{:S(2)}) async-start(bf16[4,128,768]{2,1,0:T(8,128)(2,1)} %bitcast.1), calls=%async_computation.1 | async-start | bytes 1572864 | tf_op jit(solution)/shard_map/all_to_all | solution.py:33
  80.6 18.1 %copy-start.6 = (bf16[512,768]{1,0:T(8,128)(2,1)S(1)}, bf16[512,768]{1,0:T(8,128)(2,1)}, u32[]{:S(2)}) copy-start(bf16[512,768]{1,0:T(8,128)(2,1)} %all_gather.24) | copy-start | bytes 2359300
  97.7 5.5 %copy-start.1 = (bf16[512,768]{1,0:T(8,128)(2,1)}, bf16[512,768]{1,0:T(8,128)(2,1)S(1)}, u32[]{:S(2)}) copy-start(bf16[512,768]{1,0:T(8,128)(2,1)S(1)} %all_gather.23.act) | copy-start | bytes 2359300
  99.3 3.9 %collective-permute-start.2 = (bf16[768,384]{1,0:T(8,128)(2,1)S(1)}, bf16[768,384]{1,0:T(8,128)(2,1)S(1)}, u32[]{:S(2)}, u32[]{:S(2)}) collective-permute-start(bf16[768,384]{1,0:T(8,128)(2,1)S(1)} %convolution_convert_fusion.2), channel_id=1, source_target_pairs={{0,8},{8,0},{1,9},{9,1},{2,10},{10,2},{3,11},{11,3},{4,12},{12,4},... | collective-permute-start | bytes 1769480 | tf_op jit(solution)/shard_map/ppermute | solution.py:43
  104.7 4.0 %copy-start.7 = (f32[128,768]{1,0:T(8,128)S(1)}, f32[128,768]{1,0:T(8,128)}, u32[]{:S(2)}) copy-start(f32[128,768]{1,0:T(8,128)} %convert_element_type.113) | copy-start | bytes 1179652
  104.7 4.0 %copy-start.8 = (f32[128,768]{1,0:T(8,128)S(1)}, f32[128,768]{1,0:T(8,128)}, u32[]{:S(2)}) copy-start(f32[128,768]{1,0:T(8,128)} %convert_reduce_fusion) | copy-start | bytes 1179652
  104.7 23.4 %all-to-all-start.3 = ((bf16[4,192,384]{2,1,0:T(8,128)(2,1)}), bf16[4,192,384]{2,1,0:T(8,128)(2,1)S(1)}, u32[]{:S(2)}, u32[]{:S(2)}) async-start(bf16[4,192,384]{2,1,0:T(8,128)(2,1)} %bitcast.6), calls=%async_computation.3 | async-start | bytes 1179648 | tf_op jit(solution)/shard_map/all_to_all | solution.py:33
  108.7 13.7 %copy-start.11 = (bf16[512,768]{1,0:T(8,128)(2,1)S(1)}, bf16[512,768]{1,0:T(8,128)(2,1)}, u32[]{:S(2)}) copy-start(bf16[512,768]{1,0:T(8,128)(2,1)} %copy-done.10) | copy-start | bytes 2359300
  122.4 5.7 %copy-start.2 = (bf16[512,768]{1,0:T(8,128)(2,1)}, bf16[512,768]{1,0:T(8,128)(2,1)S(1)}, u32[]{:S(2)}) copy-start(bf16[512,768]{1,0:T(8,128)(2,1)S(1)} %all_gather.25.hidden) | copy-start | bytes 2359300
  122.9 3.9 %collective-permute-start.3 = (bf16[384,768]{1,0:T(8,128)(2,1)S(1)}, bf16[384,768]{1,0:T(8,128)(2,1)S(1)}, u32[]{:S(2)}, u32[]{:S(2)}) collective-permute-start(bf16[384,768]{1,0:T(8,128)(2,1)S(1)} %convolution_convert_fusion.1), channel_id=1, source_target_pairs={{0,8},{8,0},{1,9},{9,1},{2,10},{10,2},{3,11},{11,3},{4,12},{12,4},... | collective-permute-start | bytes 1769480 | tf_op jit(solution)/shard_map/ppermute | solution.py:43
  128.1 21.6 %all-to-all-start.2 = ((bf16[4,96,768]{2,1,0:T(8,128)(2,1)}), bf16[4,96,768]{2,1,0:T(8,128)(2,1)S(1)}, u32[]{:S(2)}, u32[]{:S(2)}) async-start(bf16[4,96,768]{2,1,0:T(8,128)(2,1)} %bitcast.3), calls=%async_computation.2 | async-start | bytes 1179648 | tf_op jit(solution)/shard_map/all_to_all | solution.py:218
  137.2 4.4 %collective-permute-start.4 = (bf16[512,768]{1,0:T(8,128)(2,1)}, bf16[512,768]{1,0:T(8,128)(2,1)S(1)}, u32[]{:S(2)}, u32[]{:S(2)}) collective-permute-start(bf16[512,768]{1,0:T(8,128)(2,1)} %shard_map.75), channel_id=1, source_target_pairs={{0,8},{8,0},{1,9},{9,1},{2,10},{10,2},{3,11},{11,3},{4,12},{12,4},... | collective-permute-start | bytes 2359304 | tf_op jit(solution)/shard_map/ppermute | solution.py:43
  141.6 0.9 copy-start.9
  151.4 53.3 %all-to-all-start.4 = ((bf16[4,256,768]{2,1,0:T(8,128)(2,1)}), bf16[4,256,768]{2,1,0:T(8,128)(2,1)S(1)}, u32[]{:S(2)}, u32[]{:S(2)}) async-start(bf16[4,256,768]{2,1,0:T(8,128)(2,1)} %bitcast.18), calls=%async_computation.4 | async-start | bytes 3145728 | tf_op jit(solution)/shard_map/all_to_all | solution.py:33
  205.7 28.1 %all-to-all-start.5 = ((bf16[4,64,768]{2,1,0:T(8,128)(2,1)}), bf16[4,64,768]{2,1,0:T(8,128)(2,1)S(1)}, u32[]{:S(2)}, u32[]{:S(2)}) async-start(bf16[4,64,768]{2,1,0:T(8,128)(2,1)} %bitcast.9), calls=%async_computation.5 | async-start | bytes 786432 | tf_op jit(solution)/shard_map/all_to_all | solution.py:33
